TPU v7x, 32 devices: a whole 2x2x4 slice. The times are simulated.
32 devices in a mesh: ep: 16 (over z, y, core), rep: 2 (over x).
Axes of the slice: x: 2, y: 2, z: 4, core: 2. Of those that a mesh axis runs over, the one named last changes fastest.
Arguments:
- tokens: bfloat16 [256, 3584], P('ep', 'rep'), may hold values from -6 to 6
- expert_ids: int32 [256, 8], P('ep'), may hold values from 0 to 15, all different within a row; in each aligned block of 16 rows (0 to 15, 16 to 31, ...) at most 12 rows name the same one
- gate_weights: float32 [256, 8], P('ep'), may hold values from 0.05 to 0.5
- up_weight: bfloat16 [16, 3584, 1024], P('ep', 'rep'), may hold values from -0.09375 to 0.09375
- down_weight: bfloat16 [16, 1024, 3584], P('ep', None, 'rep'), may hold values from -0.1875 to 0.1875
Outputs:
- mixture: bfloat16 [256, 3584], P('ep', 'rep')
Inputs may be any that keep to these rules, and one draw needn't show every extreme that they name: `expert_ids`: the 8 experts of a token differ. Within the rows of one device (each aligned block of 16 tokens) no expert is named by more than 12 tokens, a bound that some block reaches.
All inputs are finite; a program needn't handle non-finite values.
Results may differ from a plain program's by a relative error of at most 0.017.
Values may be sent and summed in bfloat16 or wider, within the bound.
No kernel may reach another device: no remote copies, remote signals or barrier semaphores. Data moves between devices by JAX's collectives and lax.ppermute only.
A program may use at most 64 MiB of HBM per device.

v0:
```python
import jax
import jax.numpy as jnp
from jax import lax
from jax.sharding import PartitionSpec as P


def local(tokens, expert_ids, gate_weights, up_weight, down_weight):
    n_peers = lax.axis_size("ep")
    tok_rows, top_count = expert_ids.shape
    width_part = tokens.shape[1]
    capacity = min(tok_rows, max(2, 3 * tok_rows * top_count // (2 * n_peers)))
    flat_ids = expert_ids.reshape(-1)
    onehot = (flat_ids[:, None] == jnp.arange(n_peers, dtype=jnp.int32)[None, :]).astype(jnp.int32)
    before = jnp.cumsum(onehot, axis=0) - onehot
    ranking = jnp.sum(before * onehot, axis=1)
    slot_index = flat_ids * capacity + ranking
    token_of_row = jnp.arange(tok_rows * top_count, dtype=jnp.int32) // top_count
    outbound = (
        jnp.zeros((n_peers * capacity, width_part), tokens.dtype)
        .at[slot_index]
        .set(tokens[token_of_row])
    )
    inbound = lax.all_to_all(outbound, "ep", split_axis=0, concat_axis=0, tiled=True)
    up_local = up_weight[0]
    down_local = down_weight[0]
    pre_share = lax.psum_scatter(
        jnp.dot(inbound, up_local, preferred_element_type=jnp.float32).astype(jnp.bfloat16),
        "rep",
        scatter_dimension=0,
        tiled=True,
    ).astype(jnp.float32)
    hidden_share = jax.nn.silu(pre_share).astype(jnp.bfloat16)
    expert_out = jnp.dot(
        lax.all_gather(hidden_share, "rep", axis=0, tiled=True),
        down_local,
        preferred_element_type=jnp.float32,
    ).astype(jnp.bfloat16)
    returned = lax.all_to_all(expert_out, "ep", split_axis=0, concat_axis=0, tiled=True)
    picked = returned[slot_index].astype(jnp.float32).reshape(tok_rows, top_count, width_part)
    mixture = jnp.sum(gate_weights[:, :, None] * picked, axis=1)
    return mixture.astype(jnp.bfloat16)


def solution(mesh):
    placed = (
        P("ep", "rep"),
        P("ep", None),
        P("ep", None),
        P("ep", "rep", None),
        P("ep", None, "rep"),
    )
    return jax.shard_map(
        local, mesh=mesh, in_specs=placed, out_specs=P("ep", "rep"), check_vma=False
    )
```

profile of v0, /device:TPU:0, one launch (start us, length us, event | category | flops | bytes accessed | tf_op | source)
XLA Modules:
  0.0 106.4 jit_solution(7079886100364680434)
XLA Ops:
  6.5 0.0 copy-start
  6.5 0.0 reduce-scatter.2.cloned.1.call-start
  6.5 0.8 copy.11
  7.3 0.7 broadcast_multiply_fusion
  8.0 0.1 eq.15
  8.1 0.1 fusion.18
  8.2 0.2 reduce_window_sum.11
  8.4 0.2 select_reduce_fusion
  8.5 0.1 copy.10
  8.6 0.1 mul.34
  8.7 0.0 copy-done
  8.7 3.0 %scatter_custom_fusion = bf16[192,1792]{1,0:T(8,128)(2,1)S(1)} fusion(s32[128]{0:T(128)S(1)} %fusion.20, bf16[16,1792]{1,0:T(8,128)(2,1)S(1)} %copy-done, s32[1024]{0:T(1024)S(1)} %pad_clamp_fusion.1, bf16[]{:T(256)} %constant.26.clone.1), kind=kCustom, calls=%fused_computation.13 | custom fusion | bytes 688130 | tf_op jit(solution)/shard_map/scatter | solution.py:21
  11.7 0.2 all_to_all.16
  11.9 29.7 %all_to_all.24 = bf16[16,12,1792]{2,1,0:T(8,128)(2,1)S(1)} all-to-all(bf16[16,12,1792]{2,1,0:T(8,128)(2,1)S(1)} %all_to_all.16), channel_id=1, replica_groups=mesh['ep'=16,'rep'=2] {'ep'}, dimensions={0} | all-to-all | bytes 1376256 | tf_op jit(solution)/shard_map/all_to_all | solution.py:23
  41.6 0.2 all_to_all.18
  41.8 3.7 %fusion.7 = bf16[192,1024]{1,0:T(8,128)(2,1)} fusion(bf16[192,1792]{1,0:T(8,128)(2,1)S(1)} %all_to_all.18, bf16[1,1792,1024]{2,1,0:T(8,128)(2,1)} %param.8), kind=kOutput, calls=%fused_computation.8 | convolution fusion | flops 704839680 | bytes 4751360 | tf_op jit(solution)/shard_map/dot_general | solution.py:27
  45.5 0.0 reduce-scatter.2.cloned.1.call-update
  45.5 13.1 %reduce-scatter.2.cloned.1.call-done = bf16[96,1024]{1,0:T(8,128)(2,1)} async-done(((bf16[192,1024]{1,0:T(8,128)(2,1)}), bf16[96,1024]{1,0:T(8,128)(2,1)}) %reduce-scatter.2.cloned.1.call-update) | async-done | bytes 196624 | tf_op jit(solution)/shard_map/reduce_scatter | solution.py:26
  58.5 1.0 fusion.16
  59.6 7.3 %all_gather.3 = bf16[192,1024]{1,0:T(8,128)(2,1)S(1)} all-gather(bf16[96,1024]{1,0:T(8,128)(2,1)S(1)} %fusion.16), channel_id=1, replica_groups=mesh['ep'=16,'rep'=2] {'rep'}, dimensions={0}, use_global_device_ids=true | all-gather | bytes 589824 | tf_op jit(solution)/shard_map/all_gather | solution.py:34
  66.9 0.0 copy-start.1
  66.9 2.9 %fusion.4 = bf16[192,1792]{1,0:T(8,128)(2,1)S(1)} fusion(bf16[192,1024]{1,0:T(8,128)(2,1)S(1)} %all_gather.3, bf16[1,1024,1792]{2,1,0:T(8,128)(2,1)} %param.9), kind=kOutput, calls=%fused_computation.7 | convolution fusion | flops 704987136 | bytes 4751360 | tf_op jit(solution)/shard_map/dot_general | solution.py:33
  69.9 1.1 %all_to_all.19 = bf16[16,12,1792]{2,1,0:T(8,128)(2,1)} reshape(bf16[192,1792]{1,0:T(8,128)(2,1)S(1)} %fusion.4) | data formatting | bytes 1376256 | tf_op jit(solution)/shard_map/all_to_all | solution.py:38
  70.9 5.6 %all-to-all-start.1 = ((bf16[16,12,1792]{2,1,0:T(8,128)(2,1)}), bf16[16,12,1792]{2,1,0:T(8,128)(2,1)S(1)}, u32[]{:S(2)}, u32[]{:S(2)}) async-start(bf16[16,12,1792]{2,1,0:T(8,128)(2,1)} %all_to_all.19), calls=%async_computation.2 | async-start | bytes 1835008 | tf_op jit(solution)/shard_map/all_to_all | solution.py:38
  76.6 0.0 copy-done.1
  76.6 0.1 copy.9
  76.7 20.7 %all-to-all-done.1 = bf16[16,12,1792]{2,1,0:T(8,128)(2,1)S(1)} async-done(((bf16[16,12,1792]{2,1,0:T(8,128)(2,1)}), bf16[16,12,1792]{2,1,0:T(8,128)(2,1)S(1)}, u32[]{:S(2)}, u32[]{:S(2)}) %all-to-all-start.1) | async-done | bytes 688160 | tf_op jit(solution)/shard_map/all_to_all | solution.py:38
  97.4 0.2 all_to_all.21
  97.5 0.9 gather_fusion
  98.5 1.1 fusion.10
  (4 shorter events, 0.0 us)
Async XLA Ops:
  6.5 2.2 %copy-start = (bf16[16,1792]{1,0:T(8,128)(2,1)S(1)}, bf16[16,1792]{1,0:T(8,128)(2,1)}, u32[]{:S(2)}) copy-start(bf16[16,1792]{1,0:T(8,128)(2,1)} %param.5) | copy-start | bytes 172036
  6.5 52.0 %reduce-scatter.2.cloned.1.call-start = ((), (), s32[]{:S(2)}) async-start(), calls=%async_computation.3 | async-start | bytes 589824 | tf_op jit(solution)/shard_map/reduce_scatter | solution.py:26
  66.9 9.7 %copy-start.1 = (f32[16,8]{0,1:T(8,128)S(1)}, f32[16,8]{0,1:T(8,128)}, u32[]{:S(2)}) copy-start(f32[16,8]{0,1:T(8,128)} %param.7) | copy-start | bytes 1540
  70.9 26.4 %all-to-all-start.1 = ((bf16[16,12,1792]{2,1,0:T(8,128)(2,1)}), bf16[16,12,1792]{2,1,0:T(8,128)(2,1)S(1)}, u32[]{:S(2)}, u32[]{:S(2)}) async-start(bf16[16,12,1792]{2,1,0:T(8,128)(2,1)} %all_to_all.19), calls=%async_computation.2 | async-start | bytes 1835008 | tf_op jit(solution)/shard_map/all_to_all | solution.py:38
Sparse Core Ops, SparseCore 0:
  45.6 12.8 reduce-scatter.1
where the time goes:
time: 107 us; the launch traced here: 106 us
  blocking collectives  37.1 us (35%)
  waiting for transfers between devices  33.8 us (32%)
  between operations  13.5 us (13%)
  matrix products  6.64 us (6%)
  local copies, waits for them, and re-layouts  6.53 us (6%)
  starting transfers between devices  5.61 us (5%)
  other arithmetic  3.24 us (3%)
    all_to_all x1, blocking collectives, local(): lax.all_to_all(outbound, 'ep', split_axis=0, concat_axis=0, tiled=True)  29.7 us
    all_to_all x1, waiting for transfers between devices, local(): lax.all_to_all(expert_out, 'ep', split_axis=0, concat_axis=0, tiled=True)  20.7 us
    reduce_scatter x1, waiting for transfers between devices, local(): lax.psum_scatter(jnp.dot(inbound, up_local, preferred_element_type=jnp.fl...  13.1 us
    all_gather x1, blocking collectives, local(): lax.all_gather(hidden_share, 'rep', axis=0, tiled=True)  7.33 us
    all_to_all x1, starting transfers between devices, local(): lax.all_to_all(expert_out, 'ep', split_axis=0, concat_axis=0, tiled=True)  5.61 us
    dot_general x1, matrix products, local(): jnp.dot(inbound, up_local, preferred_element_type=jnp.float32)  3.69 us
    scatter x1, local copies, waits for them, and re-layouts, local(): outbound = jnp.zeros((n_peers * capacity, width_part), tokens.dtype).at[s...  2.95 us
    dot_general x1, matrix products, local(): jnp.dot(lax.all_gather(hidden_share, 'rep', axis=0, tiled=True), down_loc...  2.95 us
  transfers between devices with their start and end apart: 2, of which 2 were waited for; matrix products, arithmetic and copies ran while one was open for 0% of the time, Pallas kernels for 0%

commit v1 on v0

v1 whole, which is shorter than its diff:
```python
import functools

import jax
import jax.numpy as jnp
from jax import lax
from jax.experimental import pallas as pl
from jax.experimental.pallas import tpu as pltpu
from jax.sharding import PartitionSpec as P

LANES = 128
VMEM = pl.BlockSpec(memory_space=pltpu.VMEM)
SMEM = pl.BlockSpec(memory_space=pltpu.SMEM)
F32, BF16 = jnp.float32, jnp.bfloat16


def call(kernel, outs, args, specs=None, scratch=(), limit=None):
    return pl.pallas_call(
        kernel,
        out_shape=outs,
        in_specs=specs or [VMEM] * len(args),
        out_specs=jax.tree.map(lambda _: VMEM, outs),
        scratch_shapes=scratch,
        compiler_params=pltpu.CompilerParams(vmem_limit_bytes=limit),
    )(*args)


def iota(shape, dim):
    return lax.broadcasted_iota(jnp.int32, shape, dim)


def dot(a, b):
    return jnp.dot(a, b, preferred_element_type=F32)


def pack_kernel(tok_ref, ids_ref, gates_ref, out_ref):
    rows, width = tok_ref.shape
    top = ids_ref.shape[0]
    expert = iota((rows, rows), 0)
    gate = jnp.zeros((rows, rows), F32)
    mask = jnp.zeros((rows, rows), F32)
    for k in range(top):
        hit = ids_ref[k : k + 1, :] == expert
        gate = gate + jnp.where(hit, gates_ref[k : k + 1, :], 0.0)
        mask = mask + jnp.where(hit, 1.0, 0.0)
    hi = gate.astype(BF16)
    rest = gate - hi.astype(F32)
    mid = rest.astype(BF16)
    low = (rest - mid.astype(F32)).astype(BF16)
    earlier = (iota((rows, rows), 0) < iota((rows, rows), 1)).astype(BF16)
    rank = (mask * (dot(mask.astype(BF16), earlier) + 1.0)).astype(BF16)
    routing = jnp.zeros((rows, LANES), F32)
    for q, part in enumerate((hi, mid, low, rank)):
        place = (iota((rows, LANES), 0) + q * rows == iota((rows, LANES), 1)).astype(BF16)
        routing = routing + dot(part, place)
    out_ref[:, :width] = tok_ref[...]
    out_ref[:, width:] = routing.astype(BF16)


def spread(routing, q, rows, n):
    total = n * rows
    take = (iota((LANES, total), 0) == q * rows + iota((LANES, total), 1) % rows).astype(BF16)
    every = dot(routing, take)
    return jnp.sum(
        jnp.where(iota((n, total), 1) // rows == iota((n, total), 0), every, 0.0), axis=0, keepdims=True
    )


def selection(routing, rows, cap, n):
    rank = spread(routing, 3, rows, n)
    slot = iota((n * cap, n * rows), 0)
    token = iota((n * cap, n * rows), 1)
    mine = slot // cap == token // rows
    wanted = (slot % cap + 1).astype(F32)
    return jnp.where(mine & (wanted == rank), 1.0, 0.0)


def up_kernel(rows, cap, groups, me_ref, w_ref, *refs):
    pieces = refs[: len(groups)]
    pre_ref, routing_ref, x_ref = refs[len(groups) :]
    width = w_ref.shape[0]
    n = sum(groups)
    here = iota((rows, LANES), 0) == me_ref[0]
    at = 0
    lines = []
    for ref, count in zip(pieces, groups):
        x_ref[at * rows : (at + count) * rows, :] = ref[:, :width]
        for j in range(count):
            block = ref[j * rows : (j + 1) * rows, width:].astype(F32)
            lines.append(jnp.sum(jnp.where(here, block, 0.0), axis=0, keepdims=True))
        at += count
    routing = jnp.concatenate(lines, axis=0).astype(BF16)
    routing_ref[...] = routing
    sel = selection(routing, rows, cap, n).astype(BF16)
    step = 256
    for c in range(0, w_ref.shape[1], step):
        part = dot(x_ref[...], w_ref[:, c : c + step]).astype(BF16)
        pre_ref[:, c : c + step] = dot(sel, part).astype(BF16)


def down_kernel(rows, cap, n, routing_ref, a_ref, b_ref, w_ref, keep_ref, send_ref):
    v = a_ref[...].astype(F32) + b_ref[...].astype(F32)
    hidden = (v / (1.0 + jnp.exp(-v))).astype(BF16)
    routing = routing_ref[...]
    sel = selection(routing, rows, cap, n)
    gate = spread(routing, 0, rows, n) + spread(routing, 1, rows, n) + spread(routing, 2, rows, n)
    gate = jnp.sum(sel * gate, axis=1, keepdims=True)
    sel = sel.astype(BF16)
    half = n * rows // 2
    step = 256
    for c in range(0, w_ref.shape[1], step):
        out = dot(hidden, w_ref[:, c : c + step]).astype(BF16)
        out = (gate * out.astype(F32)).astype(BF16)
        out = lax.dot_general(sel, out, (((0,), (0,)), ((), ())), preferred_element_type=F32).astype(BF16)
        keep_ref[:, c : c + step] = out[:half]
        send_ref[:, c : c + step] = out[half:]


def pairs_kernel(a_ref, b_ref, own_ref, *sends):
    rows = own_ref.shape[0]
    for k, ref in enumerate((own_ref,) + sends):
        at = pl.ds(k * rows, rows)
        ref[...] = (a_ref[at, :].astype(F32) + b_ref[at, :].astype(F32)).astype(ref.dtype)


def half_kernel(rows, own_ref, *refs):
    total = own_ref[...]
    for ref in refs[:-2]:
        total = total + ref[...].astype(F32)
    keep_ref, send_ref = refs[-2:]
    keep_ref[...] = total[:rows]
    send_ref[...] = total[rows:].astype(BF16)


def last_kernel(keep_ref, got_ref, out_ref):
    out_ref[...] = (keep_ref[...] + got_ref[...].astype(F32)).astype(BF16)


def gathered(tokens, expert_ids, gate_weights, up_weight, down_weight, cap):
    n = lax.axis_size("ep")
    rows, width = tokens.shape
    near = n // 4
    shape = jax.ShapeDtypeStruct

    def swap(x, distance):
        return lax.ppermute(x, "ep", [(i, i ^ distance) for i in range(n)])

    packed = call(
        pack_kernel, shape((rows, width + LANES), BF16), (tokens, expert_ids.T, gate_weights.T)
    )
    both = jnp.concatenate([packed, swap(packed, 2 * near)], axis=0)
    blocks = [both] + [swap(both, 2 * k) for k in range(1, near)]
    blocks = blocks + [swap(b, 1) for b in blocks]
    order = [2] * len(blocks)
    me = lax.axis_index("ep").astype(jnp.int32).reshape(1)
    hidden = up_weight.shape[2]
    pre, routing = call(
        functools.partial(up_kernel, rows, cap, order),
        (shape((n * cap, hidden), BF16), shape((n, LANES), BF16)),
        (me, up_weight[0], *blocks),
        specs=[SMEM] + [VMEM] * (1 + len(blocks)),
        scratch=[pltpu.VMEM((n * rows, width), BF16)],
    )
    other = lax.ppermute(pre, "rep", [(0, 1), (1, 0)])
    keep, send = call(
        functools.partial(down_kernel, rows, cap, n),
        (shape((n // 2 * rows, width), BF16),) * 2,
        (routing, pre, other, down_weight[0]),
    )
    got = swap(send, 1)
    own, *sends = call(
        pairs_kernel,
        (shape((2 * rows, width), F32),) + (shape((2 * rows, width), BF16),) * (near - 1),
        (keep, got),
    )
    back = [swap(s, 2 * k) for k, s in enumerate(sends, 1)]
    mine, theirs = call(
        functools.partial(half_kernel, rows),
        (shape((rows, width), F32), shape((rows, width), BF16)),
        (own, *back),
    )
    return call(last_kernel, shape((rows, width), BF16), (mine, swap(theirs, 2 * near)))


def exchanged(tokens, expert_ids, gate_weights, up_weight, down_weight, capacity):
    n_peers = lax.axis_size("ep")
    tok_rows, top_count = expert_ids.shape
    width_part = tokens.shape[1]
    flat_ids = expert_ids.reshape(-1)
    onehot = (flat_ids[:, None] == jnp.arange(n_peers, dtype=jnp.int32)[None, :]).astype(jnp.int32)
    before = jnp.cumsum(onehot, axis=0) - onehot
    ranking = jnp.sum(before * onehot, axis=1)
    slot_index = flat_ids * capacity + ranking
    token_of_row = jnp.arange(tok_rows * top_count, dtype=jnp.int32) // top_count
    outbound = (
        jnp.zeros((n_peers * capacity, width_part), tokens.dtype)
        .at[slot_index]
        .set(tokens[token_of_row])
    )
    inbound = lax.all_to_all(outbound, "ep", split_axis=0, concat_axis=0, tiled=True)
    pre_share = lax.psum_scatter(
        jnp.dot(inbound, up_weight[0], preferred_element_type=F32).astype(BF16),
        "rep",
        scatter_dimension=0,
        tiled=True,
    ).astype(F32)
    hidden_share = jax.nn.silu(pre_share).astype(BF16)
    expert_out = jnp.dot(
        lax.all_gather(hidden_share, "rep", axis=0, tiled=True),
        down_weight[0],
        preferred_element_type=F32,
    ).astype(BF16)
    returned = lax.all_to_all(expert_out, "ep", split_axis=0, concat_axis=0, tiled=True)
    picked = returned[slot_index].astype(F32).reshape(tok_rows, top_count, width_part)
    mixture = jnp.sum(gate_weights[:, :, None] * picked, axis=1)
    return mixture.astype(BF16)


def local(tokens, expert_ids, gate_weights, up_weight, down_weight):
    n = lax.axis_size("ep")
    rows, top = expert_ids.shape
    cap = min(rows, max(2, 3 * rows * top // (2 * n)))
    fits = n <= rows and 4 * rows <= LANES and n >= 8 and n & (n - 1) == 0
    plan = gathered if fits and lax.axis_size("rep") == 2 else exchanged
    return plan(tokens, expert_ids, gate_weights, up_weight, down_weight, cap)


def solution(mesh):
    placed = (
        P("ep", "rep"),
        P("ep", None),
        P("ep", None),
        P("ep", "rep", None),
        P("ep", None, "rep"),
    )
    return jax.shard_map(
        local, mesh=mesh, in_specs=placed, out_specs=P("ep", "rep"), check_vma=False
    )
```

time: 107 us -> 68.2 us (0.64)
  blocking collectives: 37.1 us -> 0 us
  Pallas kernels: 0 us -> 18.6 us
  between operations: 13.5 us -> 0.1 us
  starting transfers between devices: 5.61 us -> 15.8 us
  matrix products: 6.64 us -> 0 us
  waiting for transfers between devices: 33.8 us -> 29.1 us
  local copies, waits for them, and re-layouts: 6.53 us -> 3.39 us
  other arithmetic: 3.24 us -> 0.84 us
    all_to_all x1 -> x0, blocking collectives: 29.7 us -> none  [local(): lax.all_to_all(outbound, 'ep', split_axis=0, concat_axis=0, tiled=True)]
    ppermute x0 -> x14, waiting for transfers between devices: none -> 29.1 us  [the longest x13 19.2 us: swap(): return lax.ppermute(x, 'ep', [(i, i ^ distance) for i in range(n)])]
    all_to_all x1 -> x0, waiting for transfers between devices: 20.7 us -> none  [local(): lax.all_to_all(expert_out, 'ep', split_axis=0, concat_axis=0, tiled=True)]
    pallas_call x0 -> x6, Pallas kernels: none -> 18.6 us  [call(): pl.pallas_call(kernel, out_shape=outs, in_specs=specs or [VMEM] * len(arg...]
    ppermute x0 -> x14, starting transfers between devices: none -> 15.8 us  [the longest x13 14.4 us: swap(): return lax.ppermute(x, 'ep', [(i, i ^ distance) for i in range(n)])]
    reduce_scatter x1 -> x0, waiting for transfers between devices: 13.1 us -> none  [local(): lax.psum_scatter(jnp.dot(inbound, up_local, preferred_element_type=jnp.fl...]
    all_gather x1 -> x0, blocking collectives: 7.33 us -> none  [local(): lax.all_gather(hidden_share, 'rep', axis=0, tiled=True)]
    dot_general x2 -> x0, matrix products: 6.64 us -> none  [the longest x1 3.69 us: local(): jnp.dot(inbound, up_local, preferred_element_type=jnp.float32)]
  transfers between devices with their start and end apart: 2 -> 14, of which waited for: 2 -> 12; matrix products, arithmetic and copies ran while one was open for 0% -> 0% of each run, Pallas kernels for 0% -> 0%
where the time goes in v1:
time: 68.2 us; the launch traced here: 67.9 us
  waiting for transfers between devices  29.1 us (43%)
  Pallas kernels  18.6 us (27%)
  starting transfers between devices  15.8 us (23%)
  local copies, waits for them, and re-layouts  3.39 us (5%)
  other arithmetic  0.84 us (1%)
    ppermute x13, waiting for transfers between devices, swap(): return lax.ppermute(x, 'ep', [(i, i ^ distance) for i in range(n)])  19.2 us
    pallas_call x6, Pallas kernels, call(): pl.pallas_call(kernel, out_shape=outs, in_specs=specs or [VMEM] * len(arg...  18.6 us
    ppermute x13, starting transfers between devices, swap(): return lax.ppermute(x, 'ep', [(i, i ^ distance) for i in range(n)])  14.4 us
    ppermute x1, waiting for transfers between devices, gathered(): other = lax.ppermute(pre, 'rep', [(0, 1), (1, 0)])  9.89 us
    unnamed x28, local copies, waits for them, and re-layouts  3.39 us
    ppermute x1, starting transfers between devices, gathered(): other = lax.ppermute(pre, 'rep', [(0, 1), (1, 0)])  1.49 us
  transfers between devices with their start and end apart: 14, of which 12 were waited for; matrix products, arithmetic and copies ran while one was open for 0% of the time, Pallas kernels for 0%

profile of v1, /device:TPU:0, one launch (start us, length us, event | category | flops | bytes accessed | tf_op | source)
XLA Modules:
  0.0 67.9 jit_solution(8795925100545850577)
XLA Ops:
  0.0 1.7 %shard_map.55 = bf16[16,1920]{1,0:T(8,128)(2,1)} custom-call(bf16[16,1792]{1,0:T(8,128)(2,1)} %tok_ref.1, s32[8,16]{1,0:T(8,128)} %bitcast.7, f32[8,16]{1,0:T(8,128)} %bitcast.8), custom_call_target="tpu_custom_call" | custom-call | tf_op jit(solution)/shard_map/pallas_call | solution.py:17
  1.7 4.0 %collective-permute-start = (bf16[16,1920]{1,0:T(8,128)(2,1)}, bf16[16,1920]{1,0:T(8,128)(2,1)S(1)}, u32[]{:S(2)}, u32[]{:S(2)}) collective-permute-start(bf16[16,1920]{1,0:T(8,128)(2,1)} %shard_map.55), channel_id=1, source_target_pairs={{0,16},{2,18},{4,20},{6,22},{8,24},{10,26},{12,28},{14,30},{16,0},... | collective-permute-start | bytes 184328 | tf_op jit(solution)/shard_map/ppermute | solution.py:145
  5.7 3.1 %collective-permute-done = bf16[16,1920]{1,0:T(8,128)(2,1)S(1)} collective-permute-done((bf16[16,1920]{1,0:T(8,128)(2,1)}, bf16[16,1920]{1,0:T(8,128)(2,1)S(1)}, u32[]{:S(2)}, u32[]{:S(2)}) %collective-permute-start) | collective-permute-done | bytes 61472 | tf_op jit(solution)/shard_map/ppermute | solution.py:145
  8.8 0.8 %pad_maximum_fusion.refs_0_ = bf16[32,1920]{1,0:T(8,128)(2,1)S(1)} fusion(bf16[16,1920]{1,0:T(8,128)(2,1)S(1)} %collective-permute-done, bf16[16,1920]{1,0:T(8,128)(2,1)} %shard_map.55), kind=kLoop, calls=%fused_computation | loop fusion | flops 245760 | bytes 245760 | tf_op jit(solution)/shard_map/concatenate | solution.py:150
  9.6 0.0 copy-start
  9.7 2.3 %collective-permute-start.3 = (bf16[32,1920]{1,0:T(8,128)(2,1)S(1)}, bf16[32,1920]{1,0:T(8,128)(2,1)S(1)}, u32[]{:S(2)}, u32[]{:S(2)}) collective-permute-start(bf16[32,1920]{1,0:T(8,128)(2,1)S(1)} %pad_maximum_fusion.refs_0_), channel_id=1, source_target_pairs={{0,12},{2,14},{4,8},{6,10},{8,4},{10,6},{12,0},{14,2},{16,28},{18,... | collective-permute-start | bytes 368648 | tf_op jit(solution)/shard_map/ppermute | solution.py:145
  12.0 1.6 %collective-permute-start.2 = (bf16[32,1920]{1,0:T(8,128)(2,1)S(1)}, bf16[32,1920]{1,0:T(8,128)(2,1)S(1)}, u32[]{:S(2)}, u32[]{:S(2)}) collective-permute-start(bf16[32,1920]{1,0:T(8,128)(2,1)S(1)} %pad_maximum_fusion.refs_0_), channel_id=1, source_target_pairs={{0,8},{2,10},{4,12},{6,14},{8,0},{10,2},{12,4},{14,6},{16,24},{18,... | collective-permute-start | bytes 368648 | tf_op jit(solution)/shard_map/ppermute | solution.py:145
  13.6 0.0 collective-permute-start.1
  13.6 0.0 collective-permute-start.4
  13.6 2.8 %collective-permute-done.3.refs_3_ = bf16[32,1920]{1,0:T(8,128)(2,1)S(1)} collective-permute-done((bf16[32,1920]{1,0:T(8,128)(2,1)S(1)}, bf16[32,1920]{1,0:T(8,128)(2,1)S(1)}, u32[]{:S(2)}, u32[]{:S(2)}) %collective-permute-start.3) | collective-permute-done | bytes 122912 | tf_op jit(solution)/shard_map/ppermute | solution.py:145
  16.4 0.0 copy-start.3
  16.4 0.0 collective-permute-start.7
  16.4 1.3 %collective-permute-done.2.refs_2_ = bf16[32,1920]{1,0:T(8,128)(2,1)S(1)} collective-permute-done((bf16[32,1920]{1,0:T(8,128)(2,1)S(1)}, bf16[32,1920]{1,0:T(8,128)(2,1)S(1)}, u32[]{:S(2)}, u32[]{:S(2)}) %collective-permute-start.2) | collective-permute-done | bytes 122912 | tf_op jit(solution)/shard_map/ppermute | solution.py:145
  17.7 0.0 copy-start.4
  17.7 0.0 collective-permute-start.6
  17.7 0.7 %collective-permute-done.1.refs_1_ = bf16[32,1920]{1,0:T(8,128)(2,1)S(1)} collective-permute-done((bf16[32,1920]{1,0:T(8,128)(2,1)S(1)}, bf16[32,1920]{1,0:T(8,128)(2,1)S(1)}, u32[]{:S(2)}, u32[]{:S(2)}) %collective-permute-start.1) | collective-permute-done | bytes 122912 | tf_op jit(solution)/shard_map/ppermute | solution.py:145
  18.5 0.0 copy-start.5
  18.5 0.0 collective-permute-start.5
  18.5 0.0 collective-permute-done.4.refs_4_
  18.5 0.0 copy-start.6
  18.5 0.0 collective-permute-done.7.refs_7_
  18.5 0.0 copy-start.7
  18.5 0.6 collective-permute-done.6.refs_6_
  19.1 0.0 copy-start.8
  19.1 0.7 %collective-permute-done.5.refs_5_ = bf16[32,1920]{1,0:T(8,128)(2,1)S(1)} collective-permute-done((bf16[32,1920]{1,0:T(8,128)(2,1)S(1)}, bf16[32,1920]{1,0:T(8,128)(2,1)S(1)}, u32[]{:S(2)}, u32[]{:S(2)}) %collective-permute-start.5) | collective-permute-done | bytes 122912 | tf_op jit(solution)/shard_map/ppermute | solution.py:145
  19.8 0.0 copy-start.9
  19.8 0.0 copy-done
  19.8 0.0 copy-done.3
  19.8 0.0 copy-done.4
  19.8 0.0 copy-done.5
  19.8 0.0 copy-done.6
  19.8 0.0 copy-done.7
  19.8 0.0 copy-done.8
  19.8 0.6 copy-done.9
  20.4 5.8 %shard_map.56 = (bf16[192,1024]{1,0:T(8,128)(2,1)}, bf16[16,128]{1,0:T(8,128)(2,1)}) custom-call(s32[1]{0:T(128)} %bitcast.me_ref, bf16[1792,1024]{1,0:T(8,128)(2,1)} %bitcast.6, bf16[32,1920]{1,0:T(8,128)(2,1)} %copy-done, bf16[32,1920]{1,0:T(8,128)(2,1)} %copy-done.5, bf16[32,1920]{1,0:T(8,128)(2,1)} %copy-done.4, bf16[32,1920]{1,0:T(8,128)(2,1)} %copy-done.3, ...), custom_call_target="tpu_custom_call" | custom-call | tf_op jit(solution)/shard_map/pallas_call | solution.py:17
  26.3 1.5 %collective-permute-start.8 = (bf16[192,1024]{1,0:T(8,128)(2,1)}, bf16[192,1024]{1,0:T(8,128)(2,1)S(1)}, u32[]{:S(2)}, u32[]{:S(2)}) collective-permute-start(bf16[192,1024]{1,0:T(8,128)(2,1)} %get-tuple-element.16.a_ref), channel_id=1, source_target_pairs={{0,1},{1,0},{2,3},{3,2},{4,5},{5,4},{6,7},{7,6},{8,9},{9,8},{10,11... | collective-permute-start | bytes 1179656 | tf_op jit(solution)/shard_map/ppermute | solution.py:163
  27.8 9.9 %collective-permute-done.8.b_ref = bf16[192,1024]{1,0:T(8,128)(2,1)S(1)} collective-permute-done((bf16[192,1024]{1,0:T(8,128)(2,1)}, bf16[192,1024]{1,0:T(8,128)(2,1)S(1)}, u32[]{:S(2)}, u32[]{:S(2)}) %collective-permute-start.8) | collective-permute-done | bytes 393248 | tf_op jit(solution)/shard_map/ppermute | solution.py:163
  37.7 0.0 copy-start.2
  37.7 0.7 %copy-done.2 = bf16[192,1024]{1,0:T(8,128)(2,1)} copy-done((bf16[192,1024]{1,0:T(8,128)(2,1)}, bf16[192,1024]{1,0:T(8,128)(2,1)S(1)}, u32[]{:S(2)}) %copy-start.2) | copy-done | bytes 393240
  38.4 5.7 %shard_map.57 = (bf16[128,1792]{1,0:T(8,128)(2,1)}, bf16[128,1792]{1,0:T(8,128)(2,1)}) custom-call(bf16[16,128]{1,0:T(8,128)(2,1)} %get-tuple-element.15.routing_ref, bf16[192,1024]{1,0:T(8,128)(2,1)} %get-tuple-element.16.a_ref, bf16[192,1024]{1,0:T(8,128)(2,1)} %copy-done.2, bf16[1024,1792]{1,0:T(8,128)(2,1)} %bitcast.5), custom_call_target="tpu_custom_call" | custom-call | tf_op jit(solution)/shard_map/pallas_call | solution.py:17
  44.1 0.0 collective-permute-start.9
  44.1 2.0 %collective-permute-done.9.b_ref = bf16[128,1792]{1,0:T(8,128)(2,1)S(1)} collective-permute-done((bf16[128,1792]{1,0:T(8,128)(2,1)}, bf16[128,1792]{1,0:T(8,128)(2,1)S(1)}, u32[]{:S(2)}, u32[]{:S(2)}) %collective-permute-start.9) | collective-permute-done | bytes 458784 | tf_op jit(solution)/shard_map/ppermute | solution.py:145
  46.2 0.0 copy-start.1
  46.2 0.8 %copy-done.1 = bf16[128,1792]{1,0:T(8,128)(2,1)} copy-done((bf16[128,1792]{1,0:T(8,128)(2,1)}, bf16[128,1792]{1,0:T(8,128)(2,1)S(1)}, u32[]{:S(2)}) %copy-start.1) | copy-done | bytes 458776
  46.9 2.0 %shard_map.58 = (f32[32,1792]{1,0:T(8,128)}, bf16[32,1792]{1,0:T(8,128)(2,1)}, bf16[32,1792]{1,0:T(8,128)(2,1)}, bf16[32,1792]{1,0:T(8,128)(2,1)}) custom-call(bf16[128,1792]{1,0:T(8,128)(2,1)} %get-tuple-element.17.a_ref, bf16[128,1792]{1,0:T(8,128)(2,1)} %copy-done.1), custom_call_target="tpu_custom_call" | custom-call | tf_op jit(solution)/shard_map/pallas_call | solution.py:17
  49.0 0.8 %collective-permute-start.10 = (bf16[32,1792]{1,0:T(8,128)(2,1)}, bf16[32,1792]{1,0:T(8,128)(2,1)S(1)}, u32[]{:S(2)}, u32[]{:S(2)}) collective-permute-start(bf16[32,1792]{1,0:T(8,128)(2,1)} %get-tuple-element.20), channel_id=1, source_target_pairs={{0,4},{2,6},{4,0},{6,2},{8,12},{10,14},{12,8},{14,10},{16,20},{18,... | collective-permute-start | bytes 344072 | tf_op jit(solution)/shard_map/ppermute | solution.py:145
  49.7 1.6 %collective-permute-start.11 = (bf16[32,1792]{1,0:T(8,128)(2,1)}, bf16[32,1792]{1,0:T(8,128)(2,1)S(1)}, u32[]{:S(2)}, u32[]{:S(2)}) collective-permute-start(bf16[32,1792]{1,0:T(8,128)(2,1)} %get-tuple-element.21), channel_id=1, source_target_pairs={{0,8},{2,10},{4,12},{6,14},{8,0},{10,2},{12,4},{14,6},{16,24},{18,... | collective-permute-start | bytes 344072 | tf_op jit(solution)/shard_map/ppermute | solution.py:145
  51.3 1.2 %collective-permute-start.12 = (bf16[32,1792]{1,0:T(8,128)(2,1)}, bf16[32,1792]{1,0:T(8,128)(2,1)S(1)}, u32[]{:S(2)}, u32[]{:S(2)}) collective-permute-start(bf16[32,1792]{1,0:T(8,128)(2,1)} %get-tuple-element.22), channel_id=1, source_target_pairs={{0,12},{2,14},{4,8},{6,10},{8,4},{10,6},{12,0},{14,2},{16,28},{18,... | collective-permute-start | bytes 344072 | tf_op jit(solution)/shard_map/ppermute | solution.py:145
  52.4 1.9 %collective-permute-done.10.refs_0_ = bf16[32,1792]{1,0:T(8,128)(2,1)S(1)} collective-permute-done((bf16[32,1792]{1,0:T(8,128)(2,1)}, bf16[32,1792]{1,0:T(8,128)(2,1)S(1)}, u32[]{:S(2)}, u32[]{:S(2)}) %collective-permute-start.10) | collective-permute-done | bytes 114720 | tf_op jit(solution)/shard_map/ppermute | solution.py:145
  54.4 0.0 copy-start.10
  54.4 1.3 %collective-permute-done.11.refs_1_ = bf16[32,1792]{1,0:T(8,128)(2,1)S(1)} collective-permute-done((bf16[32,1792]{1,0:T(8,128)(2,1)}, bf16[32,1792]{1,0:T(8,128)(2,1)S(1)}, u32[]{:S(2)}, u32[]{:S(2)}) %collective-permute-start.11) | collective-permute-done | bytes 114720 | tf_op jit(solution)/shard_map/ppermute | solution.py:145
  55.7 0.0 copy-start.11
  55.7 2.3 %collective-permute-done.12.refs_2_ = bf16[32,1792]{1,0:T(8,128)(2,1)S(1)} collective-permute-done((bf16[32,1792]{1,0:T(8,128)(2,1)}, bf16[32,1792]{1,0:T(8,128)(2,1)S(1)}, u32[]{:S(2)}, u32[]{:S(2)}) %collective-permute-start.12) | collective-permute-done | bytes 114720 | tf_op jit(solution)/shard_map/ppermute | solution.py:145
  58.0 0.0 copy-start.12
  58.0 0.0 copy-done.10
  58.0 0.0 copy-done.11
  58.0 0.6 copy-done.12
  58.6 1.8 %shard_map.59 = (f32[16,1792]{1,0:T(8,128)}, bf16[16,1792]{1,0:T(8,128)(2,1)}) custom-call(f32[32,1792]{1,0:T(8,128)} %get-tuple-element.19.own_ref, bf16[32,1792]{1,0:T(8,128)(2,1)} %copy-done.10, bf16[32,1792]{1,0:T(8,128)(2,1)} %copy-done.11, bf16[32,1792]{1,0:T(8,128)(2,1)} %copy-done.12), custom_call_target="tpu_custom_call" | custom-call | tf_op jit(solution)/shard_map/pallas_call | solution.py:17
  60.4 2.9 %collective-permute-start.13 = (bf16[16,1792]{1,0:T(8,128)(2,1)}, bf16[16,1792]{1,0:T(8,128)(2,1)S(1)}, u32[]{:S(2)}, u32[]{:S(2)}) collective-permute-start(bf16[16,1792]{1,0:T(8,128)(2,1)} %get-tuple-element.24), channel_id=1, source_target_pairs={{0,16},{2,18},{4,20},{6,22},{8,24},{10,26},{12,28},{14,30},{16,0},... | collective-permute-start | bytes 172040 | tf_op jit(solution)/shard_map/ppermute | solution.py:145
  63.3 2.5 %collective-permute-done.13.got_ref = bf16[16,1792]{1,0:T(8,128)(2,1)S(1)} collective-permute-done((bf16[16,1792]{1,0:T(8,128)(2,1)}, bf16[16,1792]{1,0:T(8,128)(2,1)S(1)}, u32[]{:S(2)}, u32[]{:S(2)}) %collective-permute-start.13) | collective-permute-done | bytes 57376 | tf_op jit(solution)/shard_map/ppermute | solution.py:145
  65.8 0.0 copy-start.13
  65.8 0.6 copy-done.13
  66.4 1.5 %shard_map.60 = bf16[16,1792]{1,0:T(8,128)(2,1)} custom-call(f32[16,1792]{1,0:T(8,128)} %get-tuple-element.23.keep_ref, bf16[16,1792]{1,0:T(8,128)(2,1)} %copy-done.13), custom_call_target="tpu_custom_call" | custom-call | tf_op jit(solution)/shard_map/pallas_call | solution.py:17
Async XLA Ops:
  1.7 7.1 %collective-permute-start = (bf16[16,1920]{1,0:T(8,128)(2,1)}, bf16[16,1920]{1,0:T(8,128)(2,1)S(1)}, u32[]{:S(2)}, u32[]{:S(2)}) collective-permute-start(bf16[16,1920]{1,0:T(8,128)(2,1)} %shard_map.55), channel_id=1, source_target_pairs={{0,16},{2,18},{4,20},{6,22},{8,24},{10,26},{12,28},{14,30},{16,0},... | collective-permute-start | bytes 184328 | tf_op jit(solution)/shard_map/ppermute | solution.py:145
  9.6 10.2 %copy-start = (bf16[32,1920]{1,0:T(8,128)(2,1)}, bf16[32,1920]{1,0:T(8,128)(2,1)S(1)}, u32[]{:S(2)}) copy-start(bf16[32,1920]{1,0:T(8,128)(2,1)S(1)} %pad_maximum_fusion.refs_0_) | copy-start | bytes 368644
  9.7 6.7 %collective-permute-start.3 = (bf16[32,1920]{1,0:T(8,128)(2,1)S(1)}, bf16[32,1920]{1,0:T(8,128)(2,1)S(1)}, u32[]{:S(2)}, u32[]{:S(2)}) collective-permute-start(bf16[32,1920]{1,0:T(8,128)(2,1)S(1)} %pad_maximum_fusion.refs_0_), channel_id=1, source_target_pairs={{0,12},{2,14},{4,8},{6,10},{8,4},{10,6},{12,0},{14,2},{16,28},{18,... | collective-permute-start | bytes 368648 | tf_op jit(solution)/shard_map/ppermute | solution.py:145
  12.0 5.8 %collective-permute-start.2 = (bf16[32,1920]{1,0:T(8,128)(2,1)S(1)}, bf16[32,1920]{1,0:T(8,128)(2,1)S(1)}, u32[]{:S(2)}, u32[]{:S(2)}) collective-permute-start(bf16[32,1920]{1,0:T(8,128)(2,1)S(1)} %pad_maximum_fusion.refs_0_), channel_id=1, source_target_pairs={{0,8},{2,10},{4,12},{6,14},{8,0},{10,2},{12,4},{14,6},{16,24},{18,... | collective-permute-start | bytes 368648 | tf_op jit(solution)/shard_map/ppermute | solution.py:145
  13.6 4.9 %collective-permute-start.1 = (bf16[32,1920]{1,0:T(8,128)(2,1)S(1)}, bf16[32,1920]{1,0:T(8,128)(2,1)S(1)}, u32[]{:S(2)}, u32[]{:S(2)}) collective-permute-start(bf16[32,1920]{1,0:T(8,128)(2,1)S(1)} %pad_maximum_fusion.refs_0_), channel_id=1, source_target_pairs={{0,4},{2,6},{4,0},{6,2},{8,12},{10,14},{12,8},{14,10},{16,20},{18,... | collective-permute-start | bytes 368648 | tf_op jit(solution)/shard_map/ppermute | solution.py:145
  13.6 4.9 %collective-permute-start.4 = (bf16[32,1920]{1,0:T(8,128)(2,1)S(1)}, bf16[32,1920]{1,0:T(8,128)(2,1)S(1)}, u32[]{:S(2)}, u32[]{:S(2)}) collective-permute-start(bf16[32,1920]{1,0:T(8,128)(2,1)S(1)} %pad_maximum_fusion.refs_0_), channel_id=1, source_target_pairs={{0,2},{2,0},{4,6},{6,4},{8,10},{10,8},{12,14},{14,12},{16,18},{18,... | collective-permute-start | bytes 368648 | tf_op jit(solution)/shard_map/ppermute | solution.py:145
  16.4 3.4 %copy-start.3 = (bf16[32,1920]{1,0:T(8,128)(2,1)}, bf16[32,1920]{1,0:T(8,128)(2,1)S(1)}, u32[]{:S(2)}) copy-start(bf16[32,1920]{1,0:T(8,128)(2,1)S(1)} %collective-permute-done.3.refs_3_) | copy-start | bytes 368644
  16.4 2.1 %collective-permute-start.7 = (bf16[32,1920]{1,0:T(8,128)(2,1)S(1)}, bf16[32,1920]{1,0:T(8,128)(2,1)S(1)}, u32[]{:S(2)}, u32[]{:S(2)}) collective-permute-start(bf16[32,1920]{1,0:T(8,128)(2,1)S(1)} %collective-permute-done.3.refs_3_), channel_id=1, source_target_pairs={{0,2},{2,0},{4,6},{6,4},{8,10},{10,8},{12,14},{14,12},{16,18},{18,... | collective-permute-start | bytes 368648 | tf_op jit(solution)/shard_map/ppermute | solution.py:145
  17.7 2.1 %copy-start.4 = (bf16[32,1920]{1,0:T(8,128)(2,1)}, bf16[32,1920]{1,0:T(8,128)(2,1)S(1)}, u32[]{:S(2)}) copy-start(bf16[32,1920]{1,0:T(8,128)(2,1)S(1)} %collective-permute-done.2.refs_2_) | copy-start | bytes 368644
  17.7 1.3 %collective-permute-start.6 = (bf16[32,1920]{1,0:T(8,128)(2,1)S(1)}, bf16[32,1920]{1,0:T(8,128)(2,1)S(1)}, u32[]{:S(2)}, u32[]{:S(2)}) collective-permute-start(bf16[32,1920]{1,0:T(8,128)(2,1)S(1)} %collective-permute-done.2.refs_2_), channel_id=1, source_target_pairs={{0,2},{2,0},{4,6},{6,4},{8,10},{10,8},{12,14},{14,12},{16,18},{18,... | collective-permute-start | bytes 368648 | tf_op jit(solution)/shard_map/ppermute | solution.py:145
  18.5 1.4 %copy-start.5 = (bf16[32,1920]{1,0:T(8,128)(2,1)}, bf16[32,1920]{1,0:T(8,128)(2,1)S(1)}, u32[]{:S(2)}) copy-start(bf16[32,1920]{1,0:T(8,128)(2,1)S(1)} %collective-permute-done.1.refs_1_) | copy-start | bytes 368644
  18.5 1.3 %collective-permute-start.5 = (bf16[32,1920]{1,0:T(8,128)(2,1)S(1)}, bf16[32,1920]{1,0:T(8,128)(2,1)S(1)}, u32[]{:S(2)}, u32[]{:S(2)}) collective-permute-start(bf16[32,1920]{1,0:T(8,128)(2,1)S(1)} %collective-permute-done.1.refs_1_), channel_id=1, source_target_pairs={{0,2},{2,0},{4,6},{6,4},{8,10},{10,8},{12,14},{14,12},{16,18},{18,... | collective-permute-start | bytes 368648 | tf_op jit(solution)/shard_map/ppermute | solution.py:145
  18.5 1.4 %copy-start.6 = (bf16[32,1920]{1,0:T(8,128)(2,1)}, bf16[32,1920]{1,0:T(8,128)(2,1)S(1)}, u32[]{:S(2)}) copy-start(bf16[32,1920]{1,0:T(8,128)(2,1)S(1)} %collective-permute-done.4.refs_4_) | copy-start | bytes 368644
  18.5 1.3 %copy-start.7 = (bf16[32,1920]{1,0:T(8,128)(2,1)}, bf16[32,1920]{1,0:T(8,128)(2,1)S(1)}, u32[]{:S(2)}) copy-start(bf16[32,1920]{1,0:T(8,128)(2,1)S(1)} %collective-permute-done.7.refs_7_) | copy-start | bytes 368644
  19.1 0.8 %copy-start.8 = (bf16[32,1920]{1,0:T(8,128)(2,1)}, bf16[32,1920]{1,0:T(8,128)(2,1)S(1)}, u32[]{:S(2)}) copy-start(bf16[32,1920]{1,0:T(8,128)(2,1)S(1)} %collective-permute-done.6.refs_6_) | copy-start | bytes 368644
  19.8 0.7 copy-start.9
  26.3 11.4 %collective-permute-start.8 = (bf16[192,1024]{1,0:T(8,128)(2,1)}, bf16[192,1024]{1,0:T(8,128)(2,1)S(1)}, u32[]{:S(2)}, u32[]{:S(2)}) collective-permute-start(bf16[192,1024]{1,0:T(8,128)(2,1)} %get-tuple-element.16.a_ref), channel_id=1, source_target_pairs={{0,1},{1,0},{2,3},{3,2},{4,5},{5,4},{6,7},{7,6},{8,9},{9,8},{10,11... | collective-permute-start | bytes 1179656 | tf_op jit(solution)/shard_map/ppermute | solution.py:163
  37.7 0.7 %copy-start.2 = (bf16[192,1024]{1,0:T(8,128)(2,1)}, bf16[192,1024]{1,0:T(8,128)(2,1)S(1)}, u32[]{:S(2)}) copy-start(bf16[192,1024]{1,0:T(8,128)(2,1)S(1)} %collective-permute-done.8.b_ref) | copy-start | bytes 1179652
  44.1 2.0 %collective-permute-start.9 = (bf16[128,1792]{1,0:T(8,128)(2,1)}, bf16[128,1792]{1,0:T(8,128)(2,1)S(1)}, u32[]{:S(2)}, u32[]{:S(2)}) collective-permute-start(bf16[128,1792]{1,0:T(8,128)(2,1)} %get-tuple-element.18), channel_id=1, source_target_pairs={{0,2},{2,0},{4,6},{6,4},{8,10},{10,8},{12,14},{14,12},{16,18},{18,... | collective-permute-start | bytes 1376264 | tf_op jit(solution)/shard_map/ppermute | solution.py:145
  46.2 0.8 %copy-start.1 = (bf16[128,1792]{1,0:T(8,128)(2,1)}, bf16[128,1792]{1,0:T(8,128)(2,1)S(1)}, u32[]{:S(2)}) copy-start(bf16[128,1792]{1,0:T(8,128)(2,1)S(1)} %collective-permute-done.9.b_ref) | copy-start | bytes 1376260
  49.0 5.4 %collective-permute-start.10 = (bf16[32,1792]{1,0:T(8,128)(2,1)}, bf16[32,1792]{1,0:T(8,128)(2,1)S(1)}, u32[]{:S(2)}, u32[]{:S(2)}) collective-permute-start(bf16[32,1792]{1,0:T(8,128)(2,1)} %get-tuple-element.20), channel_id=1, source_target_pairs={{0,4},{2,6},{4,0},{6,2},{8,12},{10,14},{12,8},{14,10},{16,20},{18,... | collective-permute-start | bytes 344072 | tf_op jit(solution)/shard_map/ppermute | solution.py:145
  49.7 6.0 %collective-permute-start.11 = (bf16[32,1792]{1,0:T(8,128)(2,1)}, bf16[32,1792]{1,0:T(8,128)(2,1)S(1)}, u32[]{:S(2)}, u32[]{:S(2)}) collective-permute-start(bf16[32,1792]{1,0:T(8,128)(2,1)} %get-tuple-element.21), channel_id=1, source_target_pairs={{0,8},{2,10},{4,12},{6,14},{8,0},{10,2},{12,4},{14,6},{16,24},{18,... | collective-permute-start | bytes 344072 | tf_op jit(solution)/shard_map/ppermute | solution.py:145
  51.3 6.7 %collective-permute-start.12 = (bf16[32,1792]{1,0:T(8,128)(2,1)}, bf16[32,1792]{1,0:T(8,128)(2,1)S(1)}, u32[]{:S(2)}, u32[]{:S(2)}) collective-permute-start(bf16[32,1792]{1,0:T(8,128)(2,1)} %get-tuple-element.22), channel_id=1, source_target_pairs={{0,12},{2,14},{4,8},{6,10},{8,4},{10,6},{12,0},{14,2},{16,28},{18,... | collective-permute-start | bytes 344072 | tf_op jit(solution)/shard_map/ppermute | solution.py:145
  54.4 3.6 %copy-start.10 = (bf16[32,1792]{1,0:T(8,128)(2,1)}, bf16[32,1792]{1,0:T(8,128)(2,1)S(1)}, u32[]{:S(2)}) copy-start(bf16[32,1792]{1,0:T(8,128)(2,1)S(1)} %collective-permute-done.10.refs_0_) | copy-start | bytes 344068
  55.7 2.3 %copy-start.11 = (bf16[32,1792]{1,0:T(8,128)(2,1)}, bf16[32,1792]{1,0:T(8,128)(2,1)S(1)}, u32[]{:S(2)}) copy-start(bf16[32,1792]{1,0:T(8,128)(2,1)S(1)} %collective-permute-done.11.refs_1_) | copy-start | bytes 344068
  58.0 0.6 copy-start.12
  60.4 5.4 %collective-permute-start.13 = (bf16[16,1792]{1,0:T(8,128)(2,1)}, bf16[16,1792]{1,0:T(8,128)(2,1)S(1)}, u32[]{:S(2)}, u32[]{:S(2)}) collective-permute-start(bf16[16,1792]{1,0:T(8,128)(2,1)} %get-tuple-element.24), channel_id=1, source_target_pairs={{0,16},{2,18},{4,20},{6,22},{8,24},{10,26},{12,28},{14,30},{16,0},... | collective-permute-start | bytes 172040 | tf_op jit(solution)/shard_map/ppermute | solution.py:145
  65.8 0.6 copy-start.13

commit v2 on v1

v2 whole, which is shorter than its diff:
```python
import functools

import jax
import jax.numpy as jnp
from jax import lax
from jax.experimental import pallas as pl
from jax.experimental.pallas import tpu as pltpu
from jax.sharding import PartitionSpec as P

LANES = 128
VMEM = pl.BlockSpec(memory_space=pltpu.VMEM)
HBM = pl.BlockSpec(memory_space=pltpu.HBM)
SMEM = pl.BlockSpec(memory_space=pltpu.SMEM)
F32, BF16 = jnp.float32, jnp.bfloat16


def call(kernel, outs, args, specs=None, scratch=(), limit=8 << 20, after=(), aliases={}):
    specs = specs or [VMEM] * len(args)
    args = [pltpu.with_memory_space_constraint(a, pltpu.HBM) if s is HBM else a for a, s in zip(args, specs)]

    def body(*refs):
        kernel(*refs[: len(args)], *refs[len(args) + len(after) :])

    return pl.pallas_call(
        body,
        out_shape=outs,
        in_specs=specs + [pl.BlockSpec(memory_space=pl.ANY)] * len(after),
        out_specs=jax.tree.map(lambda _: VMEM, outs),
        scratch_shapes=scratch,
        input_output_aliases=aliases,
        cost_estimate=pl.CostEstimate(flops=1, bytes_accessed=1, transcendentals=0),
        compiler_params=pltpu.CompilerParams(vmem_limit_bytes=limit),
    )(*args, *after)


def tie(x, *after):
    return call(lambda x_ref, out_ref: None, jax.ShapeDtypeStruct(x.shape, x.dtype), (x,), after=after, aliases={0: 0})


def iota(shape, dim):
    return lax.broadcasted_iota(jnp.int32, shape, dim)


def dot(a, b):
    return jnp.dot(a, b, preferred_element_type=F32)


def pack_kernel(tok_ref, ids_hbm, gates_hbm, out_ref, ids_ref, gates_ref, sems):
    rows, width = tok_ref.shape
    top = ids_ref.shape[0]
    copies = [
        pltpu.make_async_copy(ids_hbm, ids_ref, sems.at[0]),
        pltpu.make_async_copy(gates_hbm, gates_ref, sems.at[1]),
        pltpu.make_async_copy(tok_ref, out_ref.at[:, :width], sems.at[2]),
    ]
    for copy in copies:
        copy.start()
    copies[0].wait()
    copies[1].wait()
    expert = iota((rows, rows), 0)
    gate = jnp.zeros((rows, rows), F32)
    mask = jnp.zeros((rows, rows), F32)
    for k in range(top):
        hit = ids_ref[k : k + 1, :] == expert
        gate = gate + jnp.where(hit, gates_ref[k : k + 1, :], 0.0)
        mask = mask + jnp.where(hit, 1.0, 0.0)
    hi = gate.astype(BF16)
    rest = gate - hi.astype(F32)
    mid = rest.astype(BF16)
    low = (rest - mid.astype(F32)).astype(BF16)
    earlier = (iota((rows, rows), 0) < iota((rows, rows), 1)).astype(BF16)
    rank = (mask * (dot(mask.astype(BF16), earlier) + 1.0)).astype(BF16)
    routing = jnp.zeros((rows, LANES), F32)
    for q, part in enumerate((hi, mid, low, rank)):
        place = (iota((rows, LANES), 0) + q * rows == iota((rows, LANES), 1)).astype(BF16)
        routing = routing + dot(part, place)
    out_ref[:, width:] = routing.astype(BF16)
    copies[2].wait()


def load_kernel(w_hbm, w_ref, sems):
    parts = sems.shape[0]
    rows = w_ref.shape[0] // parts
    copies = [
        pltpu.make_async_copy(w_hbm.at[pl.ds(i * rows, rows)], w_ref.at[pl.ds(i * rows, rows)], sems.at[i])
        for i in range(parts)
    ]
    for copy in copies:
        copy.start()
    for copy in copies:
        copy.wait()


def join_kernel(a_ref, b_ref, out_ref):
    rows = a_ref.shape[0]
    out_ref[:rows, :] = a_ref[...]
    out_ref[rows:, :] = b_ref[...]


def routed(routing, rows, q):
    n = routing.shape[0]
    first = pltpu.roll(routing, (LANES - q * rows) % LANES, 1) if q else routing
    lined = pltpu.roll(first, 0, 1, stride=rows, stride_axis=0)
    mine = iota((n, LANES), 1) // rows == iota((n, LANES), 0)
    return jnp.sum(jnp.where(mine, lined, 0.0), axis=0, keepdims=True)[:, : n * rows]


def selection(routing, rows, cap):
    n = routing.shape[0]
    rank = routed(routing, rows, 3).astype(jnp.int32)
    at = iota((1, n * rows), 1) // rows * cap + rank - 1
    return iota((n * cap, n * rows), 0) == jnp.where(rank > 0, at, -1)


def up_kernel(rows, cap, w_ref, *refs):
    blocks, (pre_ref, routing_ref, x_ref) = refs[:-3], refs[-3:]
    width = w_ref.shape[0]
    here = iota((rows, LANES), 0) == lax.axis_index("ep")
    lines = []
    for i, ref in enumerate(blocks):
        size = ref.shape[0]
        x_ref[i * size : (i + 1) * size, :] = ref[:, :width]
        for j in range(0, size, rows):
            block = ref[j : j + rows, width:].astype(F32)
            lines.append(jnp.sum(jnp.where(here, block, 0.0), axis=0, keepdims=True))
    routing = jnp.concatenate(lines, axis=0)
    routing_ref[...] = routing
    step = 256
    parts = [dot(x_ref[...], w_ref[:, c : c + step]).astype(BF16) for c in range(0, w_ref.shape[1], step)]
    sel = jnp.where(selection(routing, rows, cap), 1.0, 0.0).astype(BF16)
    for i, part in enumerate(parts):
        pre_ref[:, i * step : (i + 1) * step] = dot(sel, part).astype(BF16)


def plan_kernel(rows, cap, routing_ref, turned_ref, gate_ref):
    routing = routing_ref[...]
    total, slots = turned_ref.shape
    sel = jnp.where(selection(routing, rows, cap), 1.0, 0.0)
    turned_ref[...] = jnp.transpose(sel).astype(BF16)
    gate = routed(routing, rows, 0) + routed(routing, rows, 1) + routed(routing, rows, 2)
    gate_ref[...] = jnp.transpose(jnp.broadcast_to(gate, (LANES, total)))


def down_kernel(turned_ref, gate_ref, a_ref, b_ref, w_ref, keep_ref, send_ref):
    v = a_ref[...].astype(F32) + b_ref[...].astype(F32)
    hidden = (v / (1.0 + jnp.exp(-v))).astype(BF16)
    hidden = dot(turned_ref[...], hidden).astype(BF16)
    half = keep_ref.shape[0]
    step = 256
    for c in range(0, w_ref.shape[1], step):
        out = dot(hidden, w_ref[:, c : c + step]).astype(BF16).astype(F32)
        out = (out * jnp.concatenate([gate_ref[...]] * (step // LANES), axis=1)).astype(BF16)
        keep_ref[:, c : c + step] = out[:half]
        send_ref[:, c : c + step] = out[half:]


def pairs_kernel(a_ref, b_ref, *outs):
    rows = outs[0].shape[0]
    for k, ref in enumerate(outs):
        at = pl.ds(k * rows, rows)
        ref[...] = (a_ref[at, :].astype(F32) + b_ref[at, :].astype(F32)).astype(ref.dtype)


def half_kernel(rows, own_ref, *refs):
    total = own_ref[...]
    for ref in refs[:-2]:
        total = total + ref[...].astype(F32)
    keep_ref, send_ref = refs[-2:]
    keep_ref[...] = total[:rows]
    send_ref[...] = total[rows:].astype(BF16)


def last_kernel(keep_ref, got_ref, out_ref):
    out_ref[...] = (keep_ref[...] + got_ref[...].astype(F32)).astype(BF16)


def gathered(tokens, expert_ids, gate_weights, up_weight, down_weight, cap):
    n = lax.axis_size("ep")
    rows, width = tokens.shape
    near = n // 4
    hidden = up_weight.shape[2]
    shape = jax.ShapeDtypeStruct
    dma = pltpu.SemaphoreType.DMA

    def swap(x, distance):
        return lax.ppermute(x, "ep", [(i, i ^ distance) for i in range(n)])

    def load(weight, *after):
        out = pltpu.VMEM(weight.shape, BF16)
        return call(load_kernel, out, (weight,), specs=[HBM], scratch=[dma((8,))], after=after)

    packed = call(
        pack_kernel,
        shape((rows, width + LANES), BF16),
        (tokens, expert_ids.T, gate_weights.T),
        specs=[HBM] * 3,
        scratch=[pltpu.VMEM(expert_ids.shape[::-1], jnp.int32), pltpu.VMEM(expert_ids.shape[::-1], F32), dma((3,))],
    )
    far = swap(packed, 2 * near)
    up = load(up_weight[0])
    block = call(join_kernel, shape((2 * rows, width + LANES), BF16), (packed, far), after=(up,))
    blocks = [block] + [swap(block, 2 * k) for k in range(1, near)]
    halves = (blocks[: near // 2], blocks[near // 2 :])
    started = []
    for half in halves:
        half = half + [swap(b, 1) for b in half]
        count = 2 * len(half)
        pre, routing = call(
            functools.partial(up_kernel, rows, cap),
            (shape((count * cap, hidden), BF16), shape((count, LANES), F32)),
            (up, *half),
            scratch=[pltpu.VMEM((count * rows, width), BF16)],
        )
        turned, gate = call(
            functools.partial(plan_kernel, rows, cap),
            (shape((count * rows, count * cap), BF16), shape((count * rows, LANES), F32)),
            (routing,),
        )
        started.append((count, turned, gate, pre, lax.ppermute(pre, "rep", [(0, 1), (1, 0)])))
    down = load(down_weight[0], started[-1][3])
    sums = []
    for i, (count, turned, gate, pre, other) in enumerate(started):
        keep, send = call(
            down_kernel,
            (shape((count // 2 * rows, width), BF16),) * 2,
            (turned, gate, pre, other, down),
        )
        sums += call(
            pairs_kernel,
            tuple(
                shape((2 * rows, width), F32 if i == 0 and k == 0 else BF16) for k in range(len(halves[i]))
            ),
            (keep, swap(send, 1)),
        )
    back = [swap(s, 2 * k) for k, s in enumerate(sums) if k > 0]
    mine, theirs = call(
        functools.partial(half_kernel, rows),
        (shape((rows, width), F32), shape((rows, width), BF16)),
        (sums[0], *back),
    )
    return call(last_kernel, shape((rows, width), BF16), (mine, swap(theirs, 2 * near)))


def exchanged(tokens, expert_ids, gate_weights, up_weight, down_weight, capacity):
    n_peers = lax.axis_size("ep")
    tok_rows, top_count = expert_ids.shape
    width_part = tokens.shape[1]
    flat_ids = expert_ids.reshape(-1)
    onehot = (flat_ids[:, None] == jnp.arange(n_peers, dtype=jnp.int32)[None, :]).astype(jnp.int32)
    before = jnp.cumsum(onehot, axis=0) - onehot
    ranking = jnp.sum(before * onehot, axis=1)
    slot_index = flat_ids * capacity + ranking
    token_of_row = jnp.arange(tok_rows * top_count, dtype=jnp.int32) // top_count
    outbound = (
        jnp.zeros((n_peers * capacity, width_part), tokens.dtype)
        .at[slot_index]
        .set(tokens[token_of_row])
    )
    inbound = lax.all_to_all(outbound, "ep", split_axis=0, concat_axis=0, tiled=True)
    pre_share = lax.psum_scatter(
        jnp.dot(inbound, up_weight[0], preferred_element_type=F32).astype(BF16),
        "rep",
        scatter_dimension=0,
        tiled=True,
    ).astype(F32)
    hidden_share = jax.nn.silu(pre_share).astype(BF16)
    expert_out = jnp.dot(
        lax.all_gather(hidden_share, "rep", axis=0, tiled=True),
        down_weight[0],
        preferred_element_type=F32,
    ).astype(BF16)
    returned = lax.all_to_all(expert_out, "ep", split_axis=0, concat_axis=0, tiled=True)
    picked = returned[slot_index].astype(F32).reshape(tok_rows, top_count, width_part)
    mixture = jnp.sum(gate_weights[:, :, None] * picked, axis=1)
    return mixture.astype(BF16)


def local(tokens, expert_ids, gate_weights, up_weight, down_weight):
    n = lax.axis_size("ep")
    rows, top = expert_ids.shape
    cap = min(rows, max(2, 3 * rows * top // (2 * n)))
    fits = n <= rows and 4 * rows <= LANES and n >= 8 and n & (n - 1) == 0
    plan = gathered if fits and lax.axis_size("rep") == 2 else exchanged
    return plan(tokens, expert_ids, gate_weights, up_weight, down_weight, cap)


def solution(mesh):
    placed = (
        P("ep", "rep"),
        P("ep", None),
        P("ep", None),
        P("ep", "rep", None),
        P("ep", None, "rep"),
    )
    return jax.shard_map(
        local, mesh=mesh, in_specs=placed, out_specs=P("ep", "rep"), check_vma=False
    )
```

time: 68.2 us -> 46.5 us (0.68)
  waiting for transfers between devices: 29.1 us -> 18.9 us
  Pallas kernels: 18.6 us -> 9.68 us
  local copies, waits for them, and re-layouts: 3.39 us -> 0 us
  starting transfers between devices: 15.8 us -> 17.6 us
  other arithmetic: 0.84 us -> 0 us
    pallas_call x6 -> x14, Pallas kernels: 18.6 us -> 9.68 us  [call(): pl.pallas_call(body, out_shape=outs, in_specs=specs + [pl.BlockSpec(memor...]
    ppermute x13 -> x14, waiting for transfers between devices: 19.2 us -> 13.8 us  [swap(): return lax.ppermute(x, 'ep', [(i, i ^ distance) for i in range(n)])]
    ppermute x1 -> x2, waiting for transfers between devices: 9.89 us -> 5.12 us  [gathered(): lax.ppermute(pre, 'rep', [(0, 1), (1, 0)])]
    unnamed x28 -> x0, local copies, waits for them, and re-layouts: 3.39 us -> none
    ppermute x13 -> x14, starting transfers between devices: 14.4 us -> 15.5 us  [swap(): return lax.ppermute(x, 'ep', [(i, i ^ distance) for i in range(n)])]
    concatenate x1 -> x0, other arithmetic: 0.84 us -> none  [gathered(): both = jnp.concatenate([packed, swap(packed, 2 * near)], axis=0)]
    ppermute x1 -> x2, starting transfers between devices: 1.49 us -> 2.16 us  [gathered(): lax.ppermute(pre, 'rep', [(0, 1), (1, 0)])]
  transfers between devices with their start and end apart: 14 -> 16, of which waited for: 12 -> 10; matrix products, arithmetic and copies ran while one was open for 0% -> 0% of each run, Pallas kernels for 0% -> 17%
where the time goes in v2:
time: 46.5 us; the launch traced here: 46.4 us
  waiting for transfers between devices  18.9 us (41%)
  starting transfers between devices  17.6 us (38%)
  Pallas kernels  9.68 us (21%)
    ppermute x14, starting transfers between devices, swap(): return lax.ppermute(x, 'ep', [(i, i ^ distance) for i in range(n)])  15.5 us
    ppermute x14, waiting for transfers between devices, swap(): return lax.ppermute(x, 'ep', [(i, i ^ distance) for i in range(n)])  13.8 us
    pallas_call x14, Pallas kernels, call(): pl.pallas_call(body, out_shape=outs, in_specs=specs + [pl.BlockSpec(memor...  9.68 us
    ppermute x2, waiting for transfers between devices, gathered(): lax.ppermute(pre, 'rep', [(0, 1), (1, 0)])  5.12 us
    ppermute x2, starting transfers between devices, gathered(): lax.ppermute(pre, 'rep', [(0, 1), (1, 0)])  2.16 us
  transfers between devices with their start and end apart: 16, of which 10 were waited for; matrix products, arithmetic and copies ran while one was open for 0% of the time, Pallas kernels for 17%

profile of v2, /device:TPU:0, one launch (start us, length us, event | category | flops | bytes accessed | tf_op | source)
XLA Modules:
  0.0 46.4 jit_solution(12593662218517048226)
XLA Ops:
  0.0 1.0 %shard_map.56.refs_0_ = bf16[16,1920]{1,0:T(8,128)(2,1)S(1)} custom-call(bf16[16,1792]{1,0:T(8,128)(2,1)} %refs_0_.1, s32[8,16]{1,0:T(8,128)} %bitcast.6, f32[8,16]{1,0:T(8,128)} %bitcast.7), custom_call_target="tpu_custom_call" | custom-call | flops 1 | bytes 1 | tf_op jit(solution)/shard_map/pallas_call | solution.py:24
  1.0 4.1 %collective-permute-start = (bf16[16,1920]{1,0:T(8,128)(2,1)S(1)}, bf16[16,1920]{1,0:T(8,128)(2,1)S(1)}, u32[]{:S(2)}, u32[]{:S(2)}) collective-permute-start(bf16[16,1920]{1,0:T(8,128)(2,1)S(1)} %shard_map.56.refs_0_), channel_id=1, source_target_pairs={{0,16},{2,18},{4,20},{6,22},{8,24},{10,26},{12,28},{14,30},{16,0},... | collective-permute-start | bytes 184328 | tf_op jit(solution)/shard_map/ppermute | solution.py:186
  5.1 2.1 %shard_map.55.refs_2_.refs_0_ = bf16[1792,1024]{1,0:T(8,128)(2,1)S(1)} custom-call(bf16[1792,1024]{1,0:T(8,128)(2,1)} %bitcast.5), custom_call_target="tpu_custom_call" | custom-call | flops 1 | bytes 1 | tf_op jit(solution)/shard_map/pallas_call | solution.py:24
  7.1 0.8 %collective-permute-done.refs_1_ = bf16[16,1920]{1,0:T(8,128)(2,1)S(1)} collective-permute-done((bf16[16,1920]{1,0:T(8,128)(2,1)S(1)}, bf16[16,1920]{1,0:T(8,128)(2,1)S(1)}, u32[]{:S(2)}, u32[]{:S(2)}) %collective-permute-start) | collective-permute-done | bytes 61472 | tf_op jit(solution)/shard_map/ppermute | solution.py:186
  8.0 2.5 %collective-permute-start.1 = (bf16[32,1920]{1,0:T(8,128)(2,1)S(1)}, bf16[32,1920]{1,0:T(8,128)(2,1)S(1)}, u32[]{:S(2)}, u32[]{:S(2)}) collective-permute-start(bf16[32,1920]{1,0:T(8,128)(2,1)S(1)} %shard_map.57.refs_1_), channel_id=1, source_target_pairs={{0,4},{2,6},{4,0},{6,2},{8,12},{10,14},{12,8},{14,10},{16,20},{18,... | collective-permute-start | bytes 368648 | tf_op jit(solution)/shard_map/ppermute | solution.py:186
  10.4 0.4 collective-permute-start.5
  10.8 1.2 %collective-permute-start.6 = (bf16[32,1920]{1,0:T(8,128)(2,1)S(1)}, bf16[32,1920]{1,0:T(8,128)(2,1)S(1)}, u32[]{:S(2)}, u32[]{:S(2)}) collective-permute-start(bf16[32,1920]{1,0:T(8,128)(2,1)S(1)} %shard_map.57.refs_1_), channel_id=1, source_target_pairs={{0,12},{2,14},{4,8},{6,10},{8,4},{10,6},{12,0},{14,2},{16,28},{18,... | collective-permute-start | bytes 368648 | tf_op jit(solution)/shard_map/ppermute | solution.py:186
  12.0 0.0 collective-permute-start.2
  12.0 2.4 %collective-permute-done.1.refs_2_ = bf16[32,1920]{1,0:T(8,128)(2,1)S(1)} collective-permute-done((bf16[32,1920]{1,0:T(8,128)(2,1)S(1)}, bf16[32,1920]{1,0:T(8,128)(2,1)S(1)}, u32[]{:S(2)}, u32[]{:S(2)}) %collective-permute-start.1) | collective-permute-done | bytes 122912 | tf_op jit(solution)/shard_map/ppermute | solution.py:186
  14.3 0.0 collective-permute-start.3
  14.3 1.0 %collective-permute-done.5.refs_1_ = bf16[32,1920]{1,0:T(8,128)(2,1)S(1)} collective-permute-done((bf16[32,1920]{1,0:T(8,128)(2,1)S(1)}, bf16[32,1920]{1,0:T(8,128)(2,1)S(1)}, u32[]{:S(2)}, u32[]{:S(2)}) %collective-permute-start.5) | collective-permute-done | bytes 122912 | tf_op jit(solution)/shard_map/ppermute | solution.py:186
  15.3 0.0 collective-permute-start.7
  15.3 1.5 %collective-permute-done.6.refs_2_ = bf16[32,1920]{1,0:T(8,128)(2,1)S(1)} collective-permute-done((bf16[32,1920]{1,0:T(8,128)(2,1)S(1)}, bf16[32,1920]{1,0:T(8,128)(2,1)S(1)}, u32[]{:S(2)}, u32[]{:S(2)}) %collective-permute-start.6) | collective-permute-done | bytes 122912 | tf_op jit(solution)/shard_map/ppermute | solution.py:186
  16.8 0.0 collective-permute-start.8
  16.8 0.0 collective-permute-done.2.refs_3_
  16.8 0.0 collective-permute-done.3.refs_4_
  16.8 0.8 %shard_map.58 = (bf16[96,1024]{1,0:T(8,128)(2,1)S(1)}, f32[8,128]{1,0:T(8,128)S(1)}) custom-call(bf16[1792,1024]{1,0:T(8,128)(2,1)S(1)} %shard_map.55.refs_2_.refs_0_, bf16[32,1920]{1,0:T(8,128)(2,1)S(1)} %shard_map.57.refs_1_, bf16[32,1920]{1,0:T(8,128)(2,1)S(1)} %collective-permute-done.1.refs_2_, bf16[32,1920]{1,0:T(8,128)(2,1)S(1)} %collective-permute-done.2.refs_3_, ...), custom_call_target="tpu_custom_call" | custom-call | flops 1 | bytes 1 | tf_op jit(solution)/shard_map/pallas_call | solution.py:24
  17.6 1.6 %collective-permute-start.4 = (bf16[96,1024]{1,0:T(8,128)(2,1)S(1)}, bf16[96,1024]{1,0:T(8,128)(2,1)S(1)}, u32[]{:S(2)}, u32[]{:S(2)}) collective-permute-start(bf16[96,1024]{1,0:T(8,128)(2,1)S(1)} %get-tuple-element.26.refs_2_), channel_id=1, source_target_pairs={{0,1},{1,0},{2,3},{3,2},{4,5},{5,4},{6,7},{7,6},{8,9},{9,8},{10,11... | collective-permute-start | bytes 589832 | tf_op jit(solution)/shard_map/ppermute | solution.py:219
  19.2 0.0 collective-permute-done.7.refs_3_
  19.2 0.0 collective-permute-done.8.refs_4_
  19.2 0.8 %shard_map.60 = (bf16[96,1024]{1,0:T(8,128)(2,1)S(1)}, f32[8,128]{1,0:T(8,128)S(1)}) custom-call(bf16[1792,1024]{1,0:T(8,128)(2,1)S(1)} %shard_map.55.refs_2_.refs_0_, bf16[32,1920]{1,0:T(8,128)(2,1)S(1)} %collective-permute-done.5.refs_1_, bf16[32,1920]{1,0:T(8,128)(2,1)S(1)} %collective-permute-done.6.refs_2_, ...), custom_call_target="tpu_custom_call" | custom-call | flops 1 | bytes 1 | tf_op jit(solution)/shard_map/pallas_call | solution.py:24
  20.0 0.6 %collective-permute-start.11 = (bf16[96,1024]{1,0:T(8,128)(2,1)S(1)}, bf16[96,1024]{1,0:T(8,128)(2,1)S(1)}, u32[]{:S(2)}, u32[]{:S(2)}) collective-permute-start(bf16[96,1024]{1,0:T(8,128)(2,1)S(1)} %get-tuple-element.27.refs_1_.refs_2_), channel_id=1, source_target_pairs={{0,1},{1,0},{2,3},{3,2},{4,5},{5,4},{6,7},{7,6},{8,9},{9,8},{10,11... | collective-permute-start | bytes 589832 | tf_op jit(solution)/shard_map/ppermute | solution.py:219
  20.6 0.2 shard_map.59
  20.8 2.1 %shard_map.61.refs_4_ = bf16[1024,1792]{1,0:T(8,128)(2,1)S(1)} custom-call(bf16[1024,1792]{1,0:T(8,128)(2,1)} %bitcast.4, bf16[96,1024]{1,0:T(8,128)(2,1)S(1)} %get-tuple-element.27.refs_1_.refs_2_), custom_call_target="tpu_custom_call" | custom-call | flops 1 | bytes 1 | tf_op jit(solution)/shard_map/pallas_call | solution.py:24
  22.9 0.2 shard_map.64
  23.2 2.2 %collective-permute-done.4.refs_3_ = bf16[96,1024]{1,0:T(8,128)(2,1)S(1)} collective-permute-done((bf16[96,1024]{1,0:T(8,128)(2,1)S(1)}, bf16[96,1024]{1,0:T(8,128)(2,1)S(1)}, u32[]{:S(2)}, u32[]{:S(2)}) %collective-permute-start.4) | collective-permute-done | bytes 196640 | tf_op jit(solution)/shard_map/ppermute | solution.py:219
  25.4 0.8 %shard_map.62 = (bf16[64,1792]{1,0:T(8,128)(2,1)S(1)}, bf16[64,1792]{1,0:T(8,128)(2,1)S(1)}) custom-call(bf16[128,96]{1,0:T(8,128)(2,1)S(1)} %get-tuple-element.24.refs_0_, f32[128,128]{1,0:T(8,128)S(1)} %get-tuple-element.25.refs_1_, bf16[96,1024]{1,0:T(8,128)(2,1)S(1)} %get-tuple-element.26.refs_2_, bf16[96,1024]{1,0:T(8,128)(2,1)S(1)} %collective-permute-done.4.refs_3_, ...), custom_call_target="tpu_custom_call" | custom-call | flops 1 | bytes 1 | tf_op jit(solution)/shard_map/pallas_call | solution.py:24
  26.2 0.1 collective-permute-start.9
  26.3 2.9 %collective-permute-done.11.refs_3_ = bf16[96,1024]{1,0:T(8,128)(2,1)S(1)} collective-permute-done((bf16[96,1024]{1,0:T(8,128)(2,1)S(1)}, bf16[96,1024]{1,0:T(8,128)(2,1)S(1)}, u32[]{:S(2)}, u32[]{:S(2)}) %collective-permute-start.11) | collective-permute-done | bytes 196640 | tf_op jit(solution)/shard_map/ppermute | solution.py:219
  29.2 0.8 %shard_map.65 = (bf16[64,1792]{1,0:T(8,128)(2,1)S(1)}, bf16[64,1792]{1,0:T(8,128)(2,1)S(1)}) custom-call(bf16[128,96]{1,0:T(8,128)(2,1)S(1)} %get-tuple-element.33.refs_0_, f32[128,128]{1,0:T(8,128)S(1)} %get-tuple-element.34.refs_1_, bf16[96,1024]{1,0:T(8,128)(2,1)S(1)} %get-tuple-element.27.refs_1_.refs_2_, ...), custom_call_target="tpu_custom_call" | custom-call | flops 1 | bytes 1 | tf_op jit(solution)/shard_map/pallas_call | solution.py:24
  30.0 0.1 collective-permute-start.12
  30.1 0.0 collective-permute-done.9.refs_1_
  30.1 0.1 shard_map.63
  30.2 1.4 %collective-permute-start.10 = (bf16[32,1792]{1,0:T(8,128)(2,1)S(1)}, bf16[32,1792]{1,0:T(8,128)(2,1)S(1)}, u32[]{:S(2)}, u32[]{:S(2)}) collective-permute-start(bf16[32,1792]{1,0:T(8,128)(2,1)S(1)} %get-tuple-element.31), channel_id=1, source_target_pairs={{0,4},{2,6},{4,0},{6,2},{8,12},{10,14},{12,8},{14,10},{16,20},{18,... | collective-permute-start | bytes 344072 | tf_op jit(solution)/shard_map/ppermute | solution.py:186
  31.5 0.0 collective-permute-done.12.refs_1_
  31.6 0.1 shard_map.66
  31.6 1.5 %collective-permute-start.13 = (bf16[32,1792]{1,0:T(8,128)(2,1)S(1)}, bf16[32,1792]{1,0:T(8,128)(2,1)S(1)}, u32[]{:S(2)}, u32[]{:S(2)}) collective-permute-start(bf16[32,1792]{1,0:T(8,128)(2,1)S(1)} %get-tuple-element.37), channel_id=1, source_target_pairs={{0,8},{2,10},{4,12},{6,14},{8,0},{10,2},{12,4},{14,6},{16,24},{18,... | collective-permute-start | bytes 344072 | tf_op jit(solution)/shard_map/ppermute | solution.py:186
  33.2 1.3 %collective-permute-start.14 = (bf16[32,1792]{1,0:T(8,128)(2,1)S(1)}, bf16[32,1792]{1,0:T(8,128)(2,1)S(1)}, u32[]{:S(2)}, u32[]{:S(2)}) collective-permute-start(bf16[32,1792]{1,0:T(8,128)(2,1)S(1)} %get-tuple-element.38), channel_id=1, source_target_pairs={{0,12},{2,14},{4,8},{6,10},{8,4},{10,6},{12,0},{14,2},{16,28},{18,... | collective-permute-start | bytes 344072 | tf_op jit(solution)/shard_map/ppermute | solution.py:186
  34.5 1.3 %collective-permute-done.10.refs_1_ = bf16[32,1792]{1,0:T(8,128)(2,1)S(1)} collective-permute-done((bf16[32,1792]{1,0:T(8,128)(2,1)S(1)}, bf16[32,1792]{1,0:T(8,128)(2,1)S(1)}, u32[]{:S(2)}, u32[]{:S(2)}) %collective-permute-start.10) | collective-permute-done | bytes 114720 | tf_op jit(solution)/shard_map/ppermute | solution.py:186
  35.8 1.9 %collective-permute-done.13.refs_2_ = bf16[32,1792]{1,0:T(8,128)(2,1)S(1)} collective-permute-done((bf16[32,1792]{1,0:T(8,128)(2,1)S(1)}, bf16[32,1792]{1,0:T(8,128)(2,1)S(1)}, u32[]{:S(2)}, u32[]{:S(2)}) %collective-permute-start.13) | collective-permute-done | bytes 114720 | tf_op jit(solution)/shard_map/ppermute | solution.py:186
  37.7 2.4 %collective-permute-done.14.refs_3_ = bf16[32,1792]{1,0:T(8,128)(2,1)S(1)} collective-permute-done((bf16[32,1792]{1,0:T(8,128)(2,1)S(1)}, bf16[32,1792]{1,0:T(8,128)(2,1)S(1)}, u32[]{:S(2)}, u32[]{:S(2)}) %collective-permute-start.14) | collective-permute-done | bytes 114720 | tf_op jit(solution)/shard_map/ppermute | solution.py:186
  40.1 0.1 shard_map.67
  40.1 3.1 %collective-permute-start.15 = (bf16[16,1792]{1,0:T(8,128)(2,1)S(1)}, bf16[16,1792]{1,0:T(8,128)(2,1)S(1)}, u32[]{:S(2)}, u32[]{:S(2)}) collective-permute-start(bf16[16,1792]{1,0:T(8,128)(2,1)S(1)} %get-tuple-element.40), channel_id=1, source_target_pairs={{0,16},{2,18},{4,20},{6,22},{8,24},{10,26},{12,28},{14,30},{16,0},... | collective-permute-start | bytes 172040 | tf_op jit(solution)/shard_map/ppermute | solution.py:186
  43.2 2.5 %collective-permute-done.15.refs_1_ = bf16[16,1792]{1,0:T(8,128)(2,1)S(1)} collective-permute-done((bf16[16,1792]{1,0:T(8,128)(2,1)S(1)}, bf16[16,1792]{1,0:T(8,128)(2,1)S(1)}, u32[]{:S(2)}, u32[]{:S(2)}) %collective-permute-start.15) | collective-permute-done | bytes 57376 | tf_op jit(solution)/shard_map/ppermute | solution.py:186
  45.7 0.6 %shard_map.68 = bf16[16,1792]{1,0:T(8,128)(2,1)} custom-call(f32[16,1792]{1,0:T(8,128)S(1)} %get-tuple-element.39.refs_0_, bf16[16,1792]{1,0:T(8,128)(2,1)S(1)} %collective-permute-done.15.refs_1_), custom_call_target="tpu_custom_call" | custom-call | flops 1 | bytes 1 | tf_op jit(solution)/shard_map/pallas_call | solution.py:24
  (1 shorter events, 0.0 us)
Async XLA Ops:
  1.0 7.0 %collective-permute-start = (bf16[16,1920]{1,0:T(8,128)(2,1)S(1)}, bf16[16,1920]{1,0:T(8,128)(2,1)S(1)}, u32[]{:S(2)}, u32[]{:S(2)}) collective-permute-start(bf16[16,1920]{1,0:T(8,128)(2,1)S(1)} %shard_map.56.refs_0_), channel_id=1, source_target_pairs={{0,16},{2,18},{4,20},{6,22},{8,24},{10,26},{12,28},{14,30},{16,0},... | collective-permute-start | bytes 184328 | tf_op jit(solution)/shard_map/ppermute | solution.py:186
  8.0 6.4 %collective-permute-start.1 = (bf16[32,1920]{1,0:T(8,128)(2,1)S(1)}, bf16[32,1920]{1,0:T(8,128)(2,1)S(1)}, u32[]{:S(2)}, u32[]{:S(2)}) collective-permute-start(bf16[32,1920]{1,0:T(8,128)(2,1)S(1)} %shard_map.57.refs_1_), channel_id=1, source_target_pairs={{0,4},{2,6},{4,0},{6,2},{8,12},{10,14},{12,8},{14,10},{16,20},{18,... | collective-permute-start | bytes 368648 | tf_op jit(solution)/shard_map/ppermute | solution.py:186
  10.4 4.9 %collective-permute-start.5 = (bf16[32,1920]{1,0:T(8,128)(2,1)S(1)}, bf16[32,1920]{1,0:T(8,128)(2,1)S(1)}, u32[]{:S(2)}, u32[]{:S(2)}) collective-permute-start(bf16[32,1920]{1,0:T(8,128)(2,1)S(1)} %shard_map.57.refs_1_), channel_id=1, source_target_pairs={{0,8},{2,10},{4,12},{6,14},{8,0},{10,2},{12,4},{14,6},{16,24},{18,... | collective-permute-start | bytes 368648 | tf_op jit(solution)/shard_map/ppermute | solution.py:186
  10.8 6.0 %collective-permute-start.6 = (bf16[32,1920]{1,0:T(8,128)(2,1)S(1)}, bf16[32,1920]{1,0:T(8,128)(2,1)S(1)}, u32[]{:S(2)}, u32[]{:S(2)}) collective-permute-start(bf16[32,1920]{1,0:T(8,128)(2,1)S(1)} %shard_map.57.refs_1_), channel_id=1, source_target_pairs={{0,12},{2,14},{4,8},{6,10},{8,4},{10,6},{12,0},{14,2},{16,28},{18,... | collective-permute-start | bytes 368648 | tf_op jit(solution)/shard_map/ppermute | solution.py:186
  12.0 4.8 %collective-permute-start.2 = (bf16[32,1920]{1,0:T(8,128)(2,1)S(1)}, bf16[32,1920]{1,0:T(8,128)(2,1)S(1)}, u32[]{:S(2)}, u32[]{:S(2)}) collective-permute-start(bf16[32,1920]{1,0:T(8,128)(2,1)S(1)} %shard_map.57.refs_1_), channel_id=1, source_target_pairs={{0,2},{2,0},{4,6},{6,4},{8,10},{10,8},{12,14},{14,12},{16,18},{18,... | collective-permute-start | bytes 368648 | tf_op jit(solution)/shard_map/ppermute | solution.py:186
  14.3 2.5 %collective-permute-start.3 = (bf16[32,1920]{1,0:T(8,128)(2,1)S(1)}, bf16[32,1920]{1,0:T(8,128)(2,1)S(1)}, u32[]{:S(2)}, u32[]{:S(2)}) collective-permute-start(bf16[32,1920]{1,0:T(8,128)(2,1)S(1)} %collective-permute-done.1.refs_2_), channel_id=1, source_target_pairs={{0,2},{2,0},{4,6},{6,4},{8,10},{10,8},{12,14},{14,12},{16,18},{18,... | collective-permute-start | bytes 368648 | tf_op jit(solution)/shard_map/ppermute | solution.py:186
  15.3 3.9 %collective-permute-start.7 = (bf16[32,1920]{1,0:T(8,128)(2,1)S(1)}, bf16[32,1920]{1,0:T(8,128)(2,1)S(1)}, u32[]{:S(2)}, u32[]{:S(2)}) collective-permute-start(bf16[32,1920]{1,0:T(8,128)(2,1)S(1)} %collective-permute-done.5.refs_1_), channel_id=1, source_target_pairs={{0,2},{2,0},{4,6},{6,4},{8,10},{10,8},{12,14},{14,12},{16,18},{18,... | collective-permute-start | bytes 368648 | tf_op jit(solution)/shard_map/ppermute | solution.py:186
  16.8 2.4 %collective-permute-start.8 = (bf16[32,1920]{1,0:T(8,128)(2,1)S(1)}, bf16[32,1920]{1,0:T(8,128)(2,1)S(1)}, u32[]{:S(2)}, u32[]{:S(2)}) collective-permute-start(bf16[32,1920]{1,0:T(8,128)(2,1)S(1)} %collective-permute-done.6.refs_2_), channel_id=1, source_target_pairs={{0,2},{2,0},{4,6},{6,4},{8,10},{10,8},{12,14},{14,12},{16,18},{18,... | collective-permute-start | bytes 368648 | tf_op jit(solution)/shard_map/ppermute | solution.py:186
  17.6 7.8 %collective-permute-start.4 = (bf16[96,1024]{1,0:T(8,128)(2,1)S(1)}, bf16[96,1024]{1,0:T(8,128)(2,1)S(1)}, u32[]{:S(2)}, u32[]{:S(2)}) collective-permute-start(bf16[96,1024]{1,0:T(8,128)(2,1)S(1)} %get-tuple-element.26.refs_2_), channel_id=1, source_target_pairs={{0,1},{1,0},{2,3},{3,2},{4,5},{5,4},{6,7},{7,6},{8,9},{9,8},{10,11... | collective-permute-start | bytes 589832 | tf_op jit(solution)/shard_map/ppermute | solution.py:219
  20.0 9.2 %collective-permute-start.11 = (bf16[96,1024]{1,0:T(8,128)(2,1)S(1)}, bf16[96,1024]{1,0:T(8,128)(2,1)S(1)}, u32[]{:S(2)}, u32[]{:S(2)}) collective-permute-start(bf16[96,1024]{1,0:T(8,128)(2,1)S(1)} %get-tuple-element.27.refs_1_.refs_2_), channel_id=1, source_target_pairs={{0,1},{1,0},{2,3},{3,2},{4,5},{5,4},{6,7},{7,6},{8,9},{9,8},{10,11... | collective-permute-start | bytes 589832 | tf_op jit(solution)/shard_map/ppermute | solution.py:219
  26.2 3.9 %collective-permute-start.9 = (bf16[64,1792]{1,0:T(8,128)(2,1)S(1)}, bf16[64,1792]{1,0:T(8,128)(2,1)S(1)}, u32[]{:S(2)}, u32[]{:S(2)}) collective-permute-start(bf16[64,1792]{1,0:T(8,128)(2,1)S(1)} %get-tuple-element.29), channel_id=1, source_target_pairs={{0,2},{2,0},{4,6},{6,4},{8,10},{10,8},{12,14},{14,12},{16,18},{18,... | collective-permute-start | bytes 688136 | tf_op jit(solution)/shard_map/ppermute | solution.py:186
  30.0 1.6 %collective-permute-start.12 = (bf16[64,1792]{1,0:T(8,128)(2,1)S(1)}, bf16[64,1792]{1,0:T(8,128)(2,1)S(1)}, u32[]{:S(2)}, u32[]{:S(2)}) collective-permute-start(bf16[64,1792]{1,0:T(8,128)(2,1)S(1)} %get-tuple-element.36), channel_id=1, source_target_pairs={{0,2},{2,0},{4,6},{6,4},{8,10},{10,8},{12,14},{14,12},{16,18},{18,... | collective-permute-start | bytes 688136 | tf_op jit(solution)/shard_map/ppermute | solution.py:186
  30.2 5.6 %collective-permute-start.10 = (bf16[32,1792]{1,0:T(8,128)(2,1)S(1)}, bf16[32,1792]{1,0:T(8,128)(2,1)S(1)}, u32[]{:S(2)}, u32[]{:S(2)}) collective-permute-start(bf16[32,1792]{1,0:T(8,128)(2,1)S(1)} %get-tuple-element.31), channel_id=1, source_target_pairs={{0,4},{2,6},{4,0},{6,2},{8,12},{10,14},{12,8},{14,10},{16,20},{18,... | collective-permute-start | bytes 344072 | tf_op jit(solution)/shard_map/ppermute | solution.py:186
  31.6 6.1 %collective-permute-start.13 = (bf16[32,1792]{1,0:T(8,128)(2,1)S(1)}, bf16[32,1792]{1,0:T(8,128)(2,1)S(1)}, u32[]{:S(2)}, u32[]{:S(2)}) collective-permute-start(bf16[32,1792]{1,0:T(8,128)(2,1)S(1)} %get-tuple-element.37), channel_id=1, source_target_pairs={{0,8},{2,10},{4,12},{6,14},{8,0},{10,2},{12,4},{14,6},{16,24},{18,... | collective-permute-start | bytes 344072 | tf_op jit(solution)/shard_map/ppermute | solution.py:186
  33.2 6.9 %collective-permute-start.14 = (bf16[32,1792]{1,0:T(8,128)(2,1)S(1)}, bf16[32,1792]{1,0:T(8,128)(2,1)S(1)}, u32[]{:S(2)}, u32[]{:S(2)}) collective-permute-start(bf16[32,1792]{1,0:T(8,128)(2,1)S(1)} %get-tuple-element.38), channel_id=1, source_target_pairs={{0,12},{2,14},{4,8},{6,10},{8,4},{10,6},{12,0},{14,2},{16,28},{18,... | collective-permute-start | bytes 344072 | tf_op jit(solution)/shard_map/ppermute | solution.py:186
  40.1 5.6 %collective-permute-start.15 = (bf16[16,1792]{1,0:T(8,128)(2,1)S(1)}, bf16[16,1792]{1,0:T(8,128)(2,1)S(1)}, u32[]{:S(2)}, u32[]{:S(2)}) collective-permute-start(bf16[16,1792]{1,0:T(8,128)(2,1)S(1)} %get-tuple-element.40), channel_id=1, source_target_pairs={{0,16},{2,18},{4,20},{6,22},{8,24},{10,26},{12,28},{14,30},{16,0},... | collective-permute-start | bytes 172040 | tf_op jit(solution)/shard_map/ppermute | solution.py:186

commit v3 on v2

--- a/solution.py
+++ b/solution.py
@@ -99,66 +99,68 @@
 
 def routed(routing, rows, q):
     n = routing.shape[0]
-    first = pltpu.roll(routing, (LANES - q * rows) % LANES, 1) if q else routing
+    first = pltpu.roll(routing, LANES - q * rows, 1) if q else routing
     lined = pltpu.roll(first, 0, 1, stride=rows, stride_axis=0)
     mine = iota((n, LANES), 1) // rows == iota((n, LANES), 0)
-    return jnp.sum(jnp.where(mine, lined, 0.0), axis=0, keepdims=True)[:, : n * rows]
+    return jnp.sum(jnp.where(mine, lined, 0.0), axis=0, keepdims=True)
 
 
 def selection(routing, rows, cap):
-    n = routing.shape[0]
     rank = routed(routing, rows, 3).astype(jnp.int32)
-    at = iota((1, n * rows), 1) // rows * cap + rank - 1
-    return iota((n * cap, n * rows), 0) == jnp.where(rank > 0, at, -1)
-
-
-def up_kernel(rows, cap, w_ref, *refs):
-    blocks, (pre_ref, routing_ref, x_ref) = refs[:-3], refs[-3:]
-    width = w_ref.shape[0]
-    here = iota((rows, LANES), 0) == lax.axis_index("ep")
-    lines = []
+    at = iota((1, LANES), 1) // rows * cap + rank - 1
+    hit = iota((LANES // rows * cap, LANES), 0) == jnp.where(rank > 0, at, -1)
+    return jnp.where(hit, 1.0, 0.0)
+
+
+def up_kernel(rows, cap, offsets, *refs):
+    weights, blocks, (pre_ref, routing_ref, x_ref) = refs[: len(offsets)], refs[len(offsets) : -3], refs[-3:]
+    width = weights[0].shape[0]
+    pieces = []
     for i, ref in enumerate(blocks):
         size = ref.shape[0]
         x_ref[i * size : (i + 1) * size, :] = ref[:, :width]
-        for j in range(0, size, rows):
-            block = ref[j : j + rows, width:].astype(F32)
-            lines.append(jnp.sum(jnp.where(here, block, 0.0), axis=0, keepdims=True))
-    routing = jnp.concatenate(lines, axis=0)
+        pieces += [ref[j : j + rows, width:].astype(F32) for j in range(0, size, rows)]
+    lines = []
+    for offset in offsets:
+        here = iota((rows, LANES), 0) == lax.axis_index("ep") ^ offset
+        lines += [jnp.sum(jnp.where(here, piece, 0.0), axis=0, keepdims=True) for piece in pieces]
+    routing = jnp.concatenate(lines + [jnp.zeros_like(lines[0])] * (LANES // rows - len(lines)), axis=0)
     routing_ref[...] = routing
     step = 256
-    parts = [dot(x_ref[...], w_ref[:, c : c + step]).astype(BF16) for c in range(0, w_ref.shape[1], step)]
-    sel = jnp.where(selection(routing, rows, cap), 1.0, 0.0).astype(BF16)
+    parts = []
+    for c in range(0, weights[0].shape[1], step):
+        parts.append([dot(x_ref[...], w_ref[:, c : c + step]).astype(BF16) for w_ref in weights])
+    slots, tokens = len(lines) * cap, len(lines) * rows
+    sel = selection(routing, rows, cap)[:slots, :tokens].astype(BF16)
     for i, part in enumerate(parts):
-        pre_ref[:, i * step : (i + 1) * step] = dot(sel, part).astype(BF16)
+        pre_ref[:, i * step : (i + 1) * step] = dot(sel, jnp.concatenate(part, axis=0)).astype(BF16)
 
 
 def plan_kernel(rows, cap, routing_ref, turned_ref, gate_ref):
     routing = routing_ref[...]
-    total, slots = turned_ref.shape
-    sel = jnp.where(selection(routing, rows, cap), 1.0, 0.0)
-    turned_ref[...] = jnp.transpose(sel).astype(BF16)
+    tokens, slots = turned_ref.shape
+    turned_ref[...] = jnp.transpose(selection(routing, rows, cap))[:tokens, :slots].astype(BF16)
     gate = routed(routing, rows, 0) + routed(routing, rows, 1) + routed(routing, rows, 2)
-    gate_ref[...] = jnp.transpose(jnp.broadcast_to(gate, (LANES, total)))
-
-
-def down_kernel(turned_ref, gate_ref, a_ref, b_ref, w_ref, keep_ref, send_ref):
+    gate_ref[...] = jnp.transpose(jnp.broadcast_to(gate, (LANES, LANES)))[:tokens]
+
+
+def down_kernel(experts, terms, turned_ref, gate_ref, a_ref, b_ref, *refs):
+    weights, sums, outs = refs[:experts], refs[experts : experts + terms], refs[experts + terms :]
     v = a_ref[...].astype(F32) + b_ref[...].astype(F32)
     hidden = (v / (1.0 + jnp.exp(-v))).astype(BF16)
     hidden = dot(turned_ref[...], hidden).astype(BF16)
-    half = keep_ref.shape[0]
+    size = hidden.shape[0] // experts
+    rows = outs[0].shape[0]
     step = 256
-    for c in range(0, w_ref.shape[1], step):
-        out = dot(hidden, w_ref[:, c : c + step]).astype(BF16).astype(F32)
-        out = (out * jnp.concatenate([gate_ref[...]] * (step // LANES), axis=1)).astype(BF16)
-        keep_ref[:, c : c + step] = out[:half]
-        send_ref[:, c : c + step] = out[half:]
-
-
-def pairs_kernel(a_ref, b_ref, *outs):
-    rows = outs[0].shape[0]
-    for k, ref in enumerate(outs):
-        at = pl.ds(k * rows, rows)
-        ref[...] = (a_ref[at, :].astype(F32) + b_ref[at, :].astype(F32)).astype(ref.dtype)
+    for c in range(0, weights[0].shape[1], step):
+        total = [ref[:, c : c + step] for ref in sums]
+        for i, w_ref in enumerate(weights):
+            at = slice(i * size, (i + 1) * size)
+            out = dot(hidden[at], w_ref[:, c : c + step]).astype(BF16).astype(F32)
+            total.append(out * jnp.concatenate([gate_ref[at, :]] * (step // LANES), axis=1))
+        total = sum(total[1:], total[0])
+        for k, ref in enumerate(outs):
+            ref[:, c : c + step] = total[k * rows : (k + 1) * rows].astype(ref.dtype)
 
 
 def half_kernel(rows, own_ref, *refs):
@@ -196,47 +198,46 @@
         specs=[HBM] * 3,
         scratch=[pltpu.VMEM(expert_ids.shape[::-1], jnp.int32), pltpu.VMEM(expert_ids.shape[::-1], F32), dma((3,))],
     )
+    up = load(up_weight[0])
     far = swap(packed, 2 * near)
-    up = load(up_weight[0])
     block = call(join_kernel, shape((2 * rows, width + LANES), BF16), (packed, far), after=(up,))
     blocks = [block] + [swap(block, 2 * k) for k in range(1, near)]
-    halves = (blocks[: near // 2], blocks[near // 2 :])
-    started = []
-    for half in halves:
-        half = half + [swap(b, 1) for b in half]
-        count = 2 * len(half)
+    down = down_weight[0]
+    ups, downs = (up, swap(up_weight[0], 1)), (down, swap(down, 1))
+
+    def raised(offsets, blocks, before=None):
+        count, size = len(offsets) * 2 * len(blocks), 2 * len(blocks) * rows
         pre, routing = call(
-            functools.partial(up_kernel, rows, cap),
-            (shape((count * cap, hidden), BF16), shape((count, LANES), F32)),
-            (up, *half),
-            scratch=[pltpu.VMEM((count * rows, width), BF16)],
+            functools.partial(up_kernel, rows, cap, offsets),
+            (shape((count * cap, hidden), BF16), shape((LANES // rows, LANES), F32)),
+            (*(ups[i] for i in offsets), *blocks),
+            scratch=[pltpu.VMEM((size, width), BF16)],
         )
-        turned, gate = call(
+        if before is not None:
+            pre = tie(pre, before)
+        plan = call(
             functools.partial(plan_kernel, rows, cap),
             (shape((count * rows, count * cap), BF16), shape((count * rows, LANES), F32)),
             (routing,),
         )
-        started.append((count, turned, gate, pre, lax.ppermute(pre, "rep", [(0, 1), (1, 0)])))
-    down = load(down_weight[0], started[-1][3])
-    sums = []
-    for i, (count, turned, gate, pre, other) in enumerate(started):
-        keep, send = call(
-            down_kernel,
-            (shape((count // 2 * rows, width), BF16),) * 2,
-            (turned, gate, pre, other, down),
+        return (*plan, pre, lax.ppermute(pre, "rep", [(0, 1), (1, 0)]))
+
+    def lowered(offsets, step, outs, *terms):
+        return call(
+            functools.partial(down_kernel, len(offsets), len(terms)), outs, (*step, *(downs[i] for i in offsets), *terms)
         )
-        sums += call(
-            pairs_kernel,
-            tuple(
-                shape((2 * rows, width), F32 if i == 0 and k == 0 else BF16) for k in range(len(halves[i]))
-            ),
-            (keep, swap(send, 1)),
-        )
-    back = [swap(s, 2 * k) for k, s in enumerate(sums) if k > 0]
+
+    pair = shape((2 * rows, width), F32)
+    here = raised((0, 1), blocks[:1])
+    there = [raised((i,), blocks[1:], here[-1] if i == 0 else None) for i in (0, 1)]
+    own = lowered((0, 1), here, pair)
+    first = lowered((0,), there[0], shape((2 * (near - 1) * rows, width), F32))
+    sends = lowered((1,), there[1], (shape(pair.shape, BF16),) * (near - 1), first)
+    back = [swap(s, 2 * k) for k, s in enumerate(sends, 1)]
     mine, theirs = call(
         functools.partial(half_kernel, rows),
         (shape((rows, width), F32), shape((rows, width), BF16)),
-        (sums[0], *back),
+        (own, *back),
     )
     return call(last_kernel, shape((rows, width), BF16), (mine, swap(theirs, 2 * near)))
 
@@ -279,7 +280,7 @@
     n = lax.axis_size("ep")
     rows, top = expert_ids.shape
     cap = min(rows, max(2, 3 * rows * top // (2 * n)))
-    fits = n <= rows and 4 * rows <= LANES and n >= 8 and n & (n - 1) == 0
+    fits = n <= rows and 4 * rows <= LANES and n // 2 * rows == LANES and n & (n - 1) == 0
     plan = gathered if fits and lax.axis_size("rep") == 2 else exchanged
     return plan(tokens, expert_ids, gate_weights, up_weight, down_weight, cap)
 

time: 46.5 us -> 43.2 us (0.929)
  waiting for transfers between devices: 18.9 us -> 13.2 us
  starting transfers between devices: 17.6 us -> 18.9 us
  Pallas kernels: 9.68 us -> 10.8 us
    ppermute x14 -> x10, waiting for transfers between devices: 13.8 us -> 9.61 us  [swap(): return lax.ppermute(x, 'ep', [(i, i ^ distance) for i in range(n)])]
    ppermute x2 -> x3, starting transfers between devices: 2.16 us -> 4.14 us  [raised(): return (*plan, pre, lax.ppermute(pre, 'rep', [(0, 1), (1, 0)]))]
    ppermute x2 -> x3, waiting for transfers between devices: 5.12 us -> 3.58 us  [raised(): return (*plan, pre, lax.ppermute(pre, 'rep', [(0, 1), (1, 0)]))]
    pallas_call x14 -> x15, Pallas kernels: 9.68 us -> 10.8 us  [call(): pl.pallas_call(body, out_shape=outs, in_specs=specs + [pl.BlockSpec(memor...]
    ppermute x14 -> x10, starting transfers between devices: 15.5 us -> 14.8 us  [swap(): return lax.ppermute(x, 'ep', [(i, i ^ distance) for i in range(n)])]
  transfers between devices with their start and end apart: 16 -> 13, of which waited for: 10 -> 7; matrix products, arithmetic and copies ran while one was open for 0% -> 0% of each run, Pallas kernels for 17% -> 21%
where the time goes in v3:
time: 43.2 us; the launch traced here: 43 us
  starting transfers between devices  18.9 us (44%)
  waiting for transfers between devices  13.2 us (31%)
  Pallas kernels  10.8 us (25%)
    ppermute x10, starting transfers between devices, swap(): return lax.ppermute(x, 'ep', [(i, i ^ distance) for i in range(n)])  14.8 us
    pallas_call x15, Pallas kernels, call(): pl.pallas_call(body, out_shape=outs, in_specs=specs + [pl.BlockSpec(memor...  10.8 us
    ppermute x10, waiting for transfers between devices, swap(): return lax.ppermute(x, 'ep', [(i, i ^ distance) for i in range(n)])  9.61 us
    ppermute x3, starting transfers between devices, raised(): return (*plan, pre, lax.ppermute(pre, 'rep', [(0, 1), (1, 0)]))  4.14 us
    ppermute x3, waiting for transfers between devices, raised(): return (*plan, pre, lax.ppermute(pre, 'rep', [(0, 1), (1, 0)]))  3.58 us
  transfers between devices with their start and end apart: 13, of which 7 were waited for; matrix products, arithmetic and copies ran while one was open for 0% of the time, Pallas kernels for 21%

profile of v3, /device:TPU:0, one launch (start us, length us, event | category | flops | bytes accessed | tf_op | source)
XLA Modules:
  0.0 43.0 jit_solution(15080429735967162090)
XLA Ops:
  0.0 0.5 %collective-permute-start = (bf16[1792,1024]{1,0:T(8,128)(2,1)}, bf16[1792,1024]{1,0:T(8,128)(2,1)S(1)}, u32[]{:S(2)}, u32[]{:S(2)}) collective-permute-start(bf16[1792,1024]{1,0:T(8,128)(2,1)} %bitcast.7), channel_id=1, source_target_pairs={{0,2},{2,0},{4,6},{6,4},{8,10},{10,8},{12,14},{14,12},{16,18},{18,... | collective-permute-start | bytes 11010056 | tf_op jit(solution)/shard_map/ppermute | solution.py:188
  0.5 0.1 collective-permute-start.3
  0.5 1.0 %shard_map.56.refs_0_ = bf16[16,1920]{1,0:T(8,128)(2,1)S(1)} custom-call(bf16[16,1792]{1,0:T(8,128)(2,1)} %refs_0_.1, s32[8,16]{1,0:T(8,128)} %bitcast.9, f32[8,16]{1,0:T(8,128)} %bitcast.10), custom_call_target="tpu_custom_call" | custom-call | flops 1 | bytes 1 | tf_op jit(solution)/shard_map/pallas_call | solution.py:24
  1.5 4.1 %collective-permute-start.1 = (bf16[16,1920]{1,0:T(8,128)(2,1)S(1)}, bf16[16,1920]{1,0:T(8,128)(2,1)S(1)}, u32[]{:S(2)}, u32[]{:S(2)}) collective-permute-start(bf16[16,1920]{1,0:T(8,128)(2,1)S(1)} %shard_map.56.refs_0_), channel_id=1, source_target_pairs={{0,16},{2,18},{4,20},{6,22},{8,24},{10,26},{12,28},{14,30},{16,0},... | collective-permute-start | bytes 184328 | tf_op jit(solution)/shard_map/ppermute | solution.py:188
  5.6 2.1 %shard_map.55.refs_2_.refs_0_ = bf16[1792,1024]{1,0:T(8,128)(2,1)S(1)} custom-call(bf16[1792,1024]{1,0:T(8,128)(2,1)} %bitcast.8), custom_call_target="tpu_custom_call" | custom-call | flops 1 | bytes 1 | tf_op jit(solution)/shard_map/pallas_call | solution.py:24
  7.7 0.8 %collective-permute-done.1.refs_1_ = bf16[16,1920]{1,0:T(8,128)(2,1)S(1)} collective-permute-done((bf16[16,1920]{1,0:T(8,128)(2,1)S(1)}, bf16[16,1920]{1,0:T(8,128)(2,1)S(1)}, u32[]{:S(2)}, u32[]{:S(2)}) %collective-permute-start.1) | collective-permute-done | bytes 61472 | tf_op jit(solution)/shard_map/ppermute | solution.py:188
  8.5 2.6 %collective-permute-start.4 = (bf16[32,1920]{1,0:T(8,128)(2,1)S(1)}, bf16[32,1920]{1,0:T(8,128)(2,1)S(1)}, u32[]{:S(2)}, u32[]{:S(2)}) collective-permute-start(bf16[32,1920]{1,0:T(8,128)(2,1)S(1)} %shard_map.57.refs_2_), channel_id=1, source_target_pairs={{0,4},{2,6},{4,0},{6,2},{8,12},{10,14},{12,8},{14,10},{16,20},{18,... | collective-permute-start | bytes 368648 | tf_op jit(solution)/shard_map/ppermute | solution.py:188
  11.0 0.4 collective-permute-start.5
  11.4 1.2 %collective-permute-start.6 = (bf16[32,1920]{1,0:T(8,128)(2,1)S(1)}, bf16[32,1920]{1,0:T(8,128)(2,1)S(1)}, u32[]{:S(2)}, u32[]{:S(2)}) collective-permute-start(bf16[32,1920]{1,0:T(8,128)(2,1)S(1)} %shard_map.57.refs_2_), channel_id=1, source_target_pairs={{0,12},{2,14},{4,8},{6,10},{8,4},{10,6},{12,0},{14,2},{16,28},{18,... | collective-permute-start | bytes 368648 | tf_op jit(solution)/shard_map/ppermute | solution.py:188
  12.6 0.0 collective-permute-done.refs_1_.refs_0_
  12.6 1.5 %shard_map.58 = (bf16[48,1024]{1,0:T(8,128)(2,1)S(1)}, f32[8,128]{1,0:T(8,128)S(1)}) custom-call(bf16[1792,1024]{1,0:T(8,128)(2,1)S(1)} %shard_map.55.refs_2_.refs_0_, bf16[1792,1024]{1,0:T(8,128)(2,1)S(1)} %collective-permute-done.refs_1_.refs_0_, bf16[32,1920]{1,0:T(8,128)(2,1)S(1)} %shard_map.57.refs_2_), custom_call_target="tpu_custom_call" | custom-call | flops 1 | bytes 1 | tf_op jit(solution)/shard_map/pallas_call | solution.py:24
  14.1 0.0 copy-start
  14.1 2.0 %collective-permute-start.2 = (bf16[48,1024]{1,0:T(8,128)(2,1)S(1)}, bf16[48,1024]{1,0:T(8,128)(2,1)S(1)}, u32[]{:S(2)}, u32[]{:S(2)}) collective-permute-start(bf16[48,1024]{1,0:T(8,128)(2,1)S(1)} %get-tuple-element.25.refs_2_), channel_id=1, source_target_pairs={{0,1},{1,0},{2,3},{3,2},{4,5},{5,4},{6,7},{7,6},{8,9},{9,8},{10,11... | collective-permute-start | bytes 294920 | tf_op jit(solution)/shard_map/ppermute | solution.py:223
  16.1 0.0 collective-permute-done.4.refs_1_
  16.1 0.0 collective-permute-done.5.refs_2_
  16.1 1.8 %collective-permute-done.6.refs_3_ = bf16[32,1920]{1,0:T(8,128)(2,1)S(1)} collective-permute-done((bf16[32,1920]{1,0:T(8,128)(2,1)S(1)}, bf16[32,1920]{1,0:T(8,128)(2,1)S(1)}, u32[]{:S(2)}, u32[]{:S(2)}) %collective-permute-start.6) | collective-permute-done | bytes 122912 | tf_op jit(solution)/shard_map/ppermute | solution.py:188
  18.0 0.9 %shard_map.63 = (bf16[72,1024]{1,0:T(8,128)(2,1)S(1)}, f32[8,128]{1,0:T(8,128)S(1)}) custom-call(bf16[1792,1024]{1,0:T(8,128)(2,1)S(1)} %shard_map.55.refs_2_.refs_0_, bf16[32,1920]{1,0:T(8,128)(2,1)S(1)} %collective-permute-done.4.refs_1_, bf16[32,1920]{1,0:T(8,128)(2,1)S(1)} %collective-permute-done.5.refs_2_, ...), custom_call_target="tpu_custom_call" | custom-call | flops 1 | bytes 1 | tf_op jit(solution)/shard_map/pallas_call | solution.py:24
  18.8 0.0 collective-permute-done.2.refs_3_.refs_1_
  18.9 1.9 %collective-permute-start.8 = (bf16[72,1024]{1,0:T(8,128)(2,1)S(1)}, bf16[72,1024]{1,0:T(8,128)(2,1)S(1)}, u32[]{:S(2)}, u32[]{:S(2)}) collective-permute-start(bf16[72,1024]{1,0:T(8,128)(2,1)S(1)} %shard_map.65.refs_2_), channel_id=1, source_target_pairs={{0,1},{1,0},{2,3},{3,2},{4,5},{5,4},{6,7},{7,6},{8,9},{9,8},{10,11... | collective-permute-start | bytes 442376 | tf_op jit(solution)/shard_map/ppermute | solution.py:223
  20.8 0.9 %shard_map.61 = (bf16[72,1024]{1,0:T(8,128)(2,1)S(1)}, f32[8,128]{1,0:T(8,128)S(1)}) custom-call(bf16[1792,1024]{1,0:T(8,128)(2,1)S(1)} %collective-permute-done.refs_1_.refs_0_, bf16[32,1920]{1,0:T(8,128)(2,1)S(1)} %collective-permute-done.4.refs_1_, bf16[32,1920]{1,0:T(8,128)(2,1)S(1)} %collective-permute-done.5.refs_2_, ...), custom_call_target="tpu_custom_call" | custom-call | flops 1 | bytes 1 | tf_op jit(solution)/shard_map/pallas_call | solution.py:24
  21.6 0.3 collective-permute-start.7
  21.9 0.2 shard_map.64
  22.1 0.2 shard_map.62
  22.4 2.5 %collective-permute-done.8.refs_3_ = bf16[72,1024]{1,0:T(8,128)(2,1)S(1)} collective-permute-done((bf16[72,1024]{1,0:T(8,128)(2,1)S(1)}, bf16[72,1024]{1,0:T(8,128)(2,1)S(1)}, u32[]{:S(2)}, u32[]{:S(2)}) %collective-permute-start.8) | collective-permute-done | bytes 147488 | tf_op jit(solution)/shard_map/ppermute | solution.py:223
  24.9 0.0 copy-done
  24.9 0.9 %shard_map.66.refs_5_ = f32[96,1792]{1,0:T(8,128)S(1)} custom-call(bf16[96,72]{1,0:T(8,128)(2,1)S(1)} %get-tuple-element.31.refs_0_, f32[96,128]{1,0:T(8,128)S(1)} %get-tuple-element.32.refs_1_, bf16[72,1024]{1,0:T(8,128)(2,1)S(1)} %shard_map.65.refs_2_, bf16[72,1024]{1,0:T(8,128)(2,1)S(1)} %collective-permute-done.8.refs_3_, bf16[1024,1792]{1,0:T(8,128)(2,1)S(1)} %bitcast.5), custom_call_target="tpu_custom_call" | custom-call | flops 1 | bytes 1 | tf_op jit(solution)/shard_map/pallas_call | solution.py:24
  25.7 0.0 collective-permute-done.3.refs_5_.refs_4_
  25.7 1.1 %collective-permute-done.7.refs_3_ = bf16[72,1024]{1,0:T(8,128)(2,1)S(1)} collective-permute-done((bf16[72,1024]{1,0:T(8,128)(2,1)S(1)}, bf16[72,1024]{1,0:T(8,128)(2,1)S(1)}, u32[]{:S(2)}, u32[]{:S(2)}) %collective-permute-start.7) | collective-permute-done | bytes 147488 | tf_op jit(solution)/shard_map/ppermute | solution.py:223
  26.8 0.9 %shard_map.67 = (bf16[32,1792]{1,0:T(8,128)(2,1)S(1)}, bf16[32,1792]{1,0:T(8,128)(2,1)S(1)}, bf16[32,1792]{1,0:T(8,128)(2,1)S(1)}) custom-call(bf16[96,72]{1,0:T(8,128)(2,1)S(1)} %get-tuple-element.27.refs_0_, f32[96,128]{1,0:T(8,128)S(1)} %get-tuple-element.28.refs_1_, bf16[72,1024]{1,0:T(8,128)(2,1)S(1)} %get-tuple-element.29.refs_2_, ...), custom_call_target="tpu_custom_call" | custom-call | flops 1 | bytes 1 | tf_op jit(solution)/shard_map/pallas_call | solution.py:24
  27.7 0.6 %collective-permute-start.10 = (bf16[32,1792]{1,0:T(8,128)(2,1)S(1)}, bf16[32,1792]{1,0:T(8,128)(2,1)S(1)}, u32[]{:S(2)}, u32[]{:S(2)}) collective-permute-start(bf16[32,1792]{1,0:T(8,128)(2,1)S(1)} %get-tuple-element.35), channel_id=1, source_target_pairs={{0,8},{2,10},{4,12},{6,14},{8,0},{10,2},{12,4},{14,6},{16,24},{18,... | collective-permute-start | bytes 344072 | tf_op jit(solution)/shard_map/ppermute | solution.py:188
  28.4 3.3 %collective-permute-start.11 = (bf16[32,1792]{1,0:T(8,128)(2,1)S(1)}, bf16[32,1792]{1,0:T(8,128)(2,1)S(1)}, u32[]{:S(2)}, u32[]{:S(2)}) collective-permute-start(bf16[32,1792]{1,0:T(8,128)(2,1)S(1)} %get-tuple-element.36), channel_id=1, source_target_pairs={{0,12},{2,14},{4,8},{6,10},{8,4},{10,6},{12,0},{14,2},{16,28},{18,... | collective-permute-start | bytes 344072 | tf_op jit(solution)/shard_map/ppermute | solution.py:188
  31.6 0.0 collective-permute-start.9
  31.6 0.2 shard_map.59
  31.9 1.3 %shard_map.60.refs_0_ = f32[32,1792]{1,0:T(8,128)S(1)} custom-call(bf16[64,48]{1,0:T(8,128)(2,1)S(1)} %get-tuple-element.23.refs_0_, f32[64,128]{1,0:T(8,128)S(1)} %get-tuple-element.24.refs_1_, bf16[48,1024]{1,0:T(8,128)(2,1)S(1)} %get-tuple-element.25.refs_2_, bf16[48,1024]{1,0:T(8,128)(2,1)S(1)} %collective-permute-done.2.refs_3_.refs_1_, ...), custom_call_target="tpu_custom_call" | custom-call | flops 1 | bytes 1 | tf_op jit(solution)/shard_map/pallas_call | solution.py:24
  33.2 0.0 collective-permute-done.10.refs_2_
  33.2 2.5 %collective-permute-done.11.refs_3_ = bf16[32,1792]{1,0:T(8,128)(2,1)S(1)} collective-permute-done((bf16[32,1792]{1,0:T(8,128)(2,1)S(1)}, bf16[32,1792]{1,0:T(8,128)(2,1)S(1)}, u32[]{:S(2)}, u32[]{:S(2)}) %collective-permute-start.11) | collective-permute-done | bytes 114720 | tf_op jit(solution)/shard_map/ppermute | solution.py:188
  35.7 1.2 %collective-permute-done.9.refs_1_ = bf16[32,1792]{1,0:T(8,128)(2,1)S(1)} collective-permute-done((bf16[32,1792]{1,0:T(8,128)(2,1)S(1)}, bf16[32,1792]{1,0:T(8,128)(2,1)S(1)}, u32[]{:S(2)}, u32[]{:S(2)}) %collective-permute-start.9) | collective-permute-done | bytes 114720 | tf_op jit(solution)/shard_map/ppermute | solution.py:188
  36.9 0.1 shard_map.68
  36.9 2.1 %collective-permute-start.12 = (bf16[16,1792]{1,0:T(8,128)(2,1)S(1)}, bf16[16,1792]{1,0:T(8,128)(2,1)S(1)}, u32[]{:S(2)}, u32[]{:S(2)}) collective-permute-start(bf16[16,1792]{1,0:T(8,128)(2,1)S(1)} %get-tuple-element.38), channel_id=1, source_target_pairs={{0,16},{2,18},{4,20},{6,22},{8,24},{10,26},{12,28},{14,30},{16,0},... | collective-permute-start | bytes 172040 | tf_op jit(solution)/shard_map/ppermute | solution.py:188
  39.1 3.3 %collective-permute-done.12.refs_1_ = bf16[16,1792]{1,0:T(8,128)(2,1)S(1)} collective-permute-done((bf16[16,1792]{1,0:T(8,128)(2,1)S(1)}, bf16[16,1792]{1,0:T(8,128)(2,1)S(1)}, u32[]{:S(2)}, u32[]{:S(2)}) %collective-permute-start.12) | collective-permute-done | bytes 57376 | tf_op jit(solution)/shard_map/ppermute | solution.py:188
  42.4 0.6 %shard_map.69 = bf16[16,1792]{1,0:T(8,128)(2,1)} custom-call(f32[16,1792]{1,0:T(8,128)S(1)} %get-tuple-element.37.refs_0_, bf16[16,1792]{1,0:T(8,128)(2,1)S(1)} %collective-permute-done.12.refs_1_), custom_call_target="tpu_custom_call" | custom-call | flops 1 | bytes 1 | tf_op jit(solution)/shard_map/pallas_call | solution.py:24
  (2 shorter events, 0.0 us)
Async XLA Ops:
  0.0 12.6 %collective-permute-start = (bf16[1792,1024]{1,0:T(8,128)(2,1)}, bf16[1792,1024]{1,0:T(8,128)(2,1)S(1)}, u32[]{:S(2)}, u32[]{:S(2)}) collective-permute-start(bf16[1792,1024]{1,0:T(8,128)(2,1)} %bitcast.7), channel_id=1, source_target_pairs={{0,2},{2,0},{4,6},{6,4},{8,10},{10,8},{12,14},{14,12},{16,18},{18,... | collective-permute-start | bytes 11010056 | tf_op jit(solution)/shard_map/ppermute | solution.py:188
  0.5 25.3 %collective-permute-start.3 = (bf16[1024,1792]{1,0:T(8,128)(2,1)}, bf16[1024,1792]{1,0:T(8,128)(2,1)S(1)}, u32[]{:S(2)}, u32[]{:S(2)}) collective-permute-start(bf16[1024,1792]{1,0:T(8,128)(2,1)} %bitcast.4), channel_id=1, source_target_pairs={{0,2},{2,0},{4,6},{6,4},{8,10},{10,8},{12,14},{14,12},{16,18},{18,... | collective-permute-start | bytes 11010056 | tf_op jit(solution)/shard_map/ppermute | solution.py:188
  1.5 7.0 %collective-permute-start.1 = (bf16[16,1920]{1,0:T(8,128)(2,1)S(1)}, bf16[16,1920]{1,0:T(8,128)(2,1)S(1)}, u32[]{:S(2)}, u32[]{:S(2)}) collective-permute-start(bf16[16,1920]{1,0:T(8,128)(2,1)S(1)} %shard_map.56.refs_0_), channel_id=1, source_target_pairs={{0,16},{2,18},{4,20},{6,22},{8,24},{10,26},{12,28},{14,30},{16,0},... | collective-permute-start | bytes 184328 | tf_op jit(solution)/shard_map/ppermute | solution.py:188
  8.5 7.7 %collective-permute-start.4 = (bf16[32,1920]{1,0:T(8,128)(2,1)S(1)}, bf16[32,1920]{1,0:T(8,128)(2,1)S(1)}, u32[]{:S(2)}, u32[]{:S(2)}) collective-permute-start(bf16[32,1920]{1,0:T(8,128)(2,1)S(1)} %shard_map.57.refs_2_), channel_id=1, source_target_pairs={{0,4},{2,6},{4,0},{6,2},{8,12},{10,14},{12,8},{14,10},{16,20},{18,... | collective-permute-start | bytes 368648 | tf_op jit(solution)/shard_map/ppermute | solution.py:188
  11.0 5.1 %collective-permute-start.5 = (bf16[32,1920]{1,0:T(8,128)(2,1)S(1)}, bf16[32,1920]{1,0:T(8,128)(2,1)S(1)}, u32[]{:S(2)}, u32[]{:S(2)}) collective-permute-start(bf16[32,1920]{1,0:T(8,128)(2,1)S(1)} %shard_map.57.refs_2_), channel_id=1, source_target_pairs={{0,8},{2,10},{4,12},{6,14},{8,0},{10,2},{12,4},{14,6},{16,24},{18,... | collective-permute-start | bytes 368648 | tf_op jit(solution)/shard_map/ppermute | solution.py:188
  11.4 6.5 %collective-permute-start.6 = (bf16[32,1920]{1,0:T(8,128)(2,1)S(1)}, bf16[32,1920]{1,0:T(8,128)(2,1)S(1)}, u32[]{:S(2)}, u32[]{:S(2)}) collective-permute-start(bf16[32,1920]{1,0:T(8,128)(2,1)S(1)} %shard_map.57.refs_2_), channel_id=1, source_target_pairs={{0,12},{2,14},{4,8},{6,10},{8,4},{10,6},{12,0},{14,2},{16,28},{18,... | collective-permute-start | bytes 368648 | tf_op jit(solution)/shard_map/ppermute | solution.py:188
  14.1 10.7 %copy-start = (bf16[1,1024,1792]{2,1,0:T(8,128)(2,1)S(1)}, bf16[1,1024,1792]{2,1,0:T(8,128)(2,1)}, u32[]{:S(2)}) copy-start(bf16[1,1024,1792]{2,1,0:T(8,128)(2,1)} %param.9) | copy-start | bytes 11010052
  14.1 4.7 %collective-permute-start.2 = (bf16[48,1024]{1,0:T(8,128)(2,1)S(1)}, bf16[48,1024]{1,0:T(8,128)(2,1)S(1)}, u32[]{:S(2)}, u32[]{:S(2)}) collective-permute-start(bf16[48,1024]{1,0:T(8,128)(2,1)S(1)} %get-tuple-element.25.refs_2_), channel_id=1, source_target_pairs={{0,1},{1,0},{2,3},{3,2},{4,5},{5,4},{6,7},{7,6},{8,9},{9,8},{10,11... | collective-permute-start | bytes 294920 | tf_op jit(solution)/shard_map/ppermute | solution.py:223
  18.9 6.0 %collective-permute-start.8 = (bf16[72,1024]{1,0:T(8,128)(2,1)S(1)}, bf16[72,1024]{1,0:T(8,128)(2,1)S(1)}, u32[]{:S(2)}, u32[]{:S(2)}) collective-permute-start(bf16[72,1024]{1,0:T(8,128)(2,1)S(1)} %shard_map.65.refs_2_), channel_id=1, source_target_pairs={{0,1},{1,0},{2,3},{3,2},{4,5},{5,4},{6,7},{7,6},{8,9},{9,8},{10,11... | collective-permute-start | bytes 442376 | tf_op jit(solution)/shard_map/ppermute | solution.py:223
  21.6 5.2 %collective-permute-start.7 = (bf16[72,1024]{1,0:T(8,128)(2,1)S(1)}, bf16[72,1024]{1,0:T(8,128)(2,1)S(1)}, u32[]{:S(2)}, u32[]{:S(2)}) collective-permute-start(bf16[72,1024]{1,0:T(8,128)(2,1)S(1)} %get-tuple-element.29.refs_2_), channel_id=1, source_target_pairs={{0,1},{1,0},{2,3},{3,2},{4,5},{5,4},{6,7},{7,6},{8,9},{9,8},{10,11... | collective-permute-start | bytes 442376 | tf_op jit(solution)/shard_map/ppermute | solution.py:223
  27.7 5.5 %collective-permute-start.10 = (bf16[32,1792]{1,0:T(8,128)(2,1)S(1)}, bf16[32,1792]{1,0:T(8,128)(2,1)S(1)}, u32[]{:S(2)}, u32[]{:S(2)}) collective-permute-start(bf16[32,1792]{1,0:T(8,128)(2,1)S(1)} %get-tuple-element.35), channel_id=1, source_target_pairs={{0,8},{2,10},{4,12},{6,14},{8,0},{10,2},{12,4},{14,6},{16,24},{18,... | collective-permute-start | bytes 344072 | tf_op jit(solution)/shard_map/ppermute | solution.py:188
  28.4 7.3 %collective-permute-start.11 = (bf16[32,1792]{1,0:T(8,128)(2,1)S(1)}, bf16[32,1792]{1,0:T(8,128)(2,1)S(1)}, u32[]{:S(2)}, u32[]{:S(2)}) collective-permute-start(bf16[32,1792]{1,0:T(8,128)(2,1)S(1)} %get-tuple-element.36), channel_id=1, source_target_pairs={{0,12},{2,14},{4,8},{6,10},{8,4},{10,6},{12,0},{14,2},{16,28},{18,... | collective-permute-start | bytes 344072 | tf_op jit(solution)/shard_map/ppermute | solution.py:188
  31.6 5.2 %collective-permute-start.9 = (bf16[32,1792]{1,0:T(8,128)(2,1)S(1)}, bf16[32,1792]{1,0:T(8,128)(2,1)S(1)}, u32[]{:S(2)}, u32[]{:S(2)}) collective-permute-start(bf16[32,1792]{1,0:T(8,128)(2,1)S(1)} %get-tuple-element.34), channel_id=1, source_target_pairs={{0,4},{2,6},{4,0},{6,2},{8,12},{10,14},{12,8},{14,10},{16,20},{18,... | collective-permute-start | bytes 344072 | tf_op jit(solution)/shard_map/ppermute | solution.py:188
  36.9 5.5 %collective-permute-start.12 = (bf16[16,1792]{1,0:T(8,128)(2,1)S(1)}, bf16[16,1792]{1,0:T(8,128)(2,1)S(1)}, u32[]{:S(2)}, u32[]{:S(2)}) collective-permute-start(bf16[16,1792]{1,0:T(8,128)(2,1)S(1)} %get-tuple-element.38), channel_id=1, source_target_pairs={{0,16},{2,18},{4,20},{6,22},{8,24},{10,26},{12,28},{14,30},{16,0},... | collective-permute-start | bytes 172040 | tf_op jit(solution)/shard_map/ppermute | solution.py:188

commit v4 on v3

--- a/solution.py
+++ b/solution.py
@@ -205,16 +205,17 @@
     down = down_weight[0]
     ups, downs = (up, swap(up_weight[0], 1)), (down, swap(down, 1))
 
-    def raised(offsets, blocks, before=None):
+    def raised(offsets, blocks, before=(), after=()):
         count, size = len(offsets) * 2 * len(blocks), 2 * len(blocks) * rows
         pre, routing = call(
             functools.partial(up_kernel, rows, cap, offsets),
             (shape((count * cap, hidden), BF16), shape((LANES // rows, LANES), F32)),
             (*(ups[i] for i in offsets), *blocks),
             scratch=[pltpu.VMEM((size, width), BF16)],
+            after=after,
         )
-        if before is not None:
-            pre = tie(pre, before)
+        if before:
+            pre = tie(pre, *before)
         plan = call(
             functools.partial(plan_kernel, rows, cap),
             (shape((count * rows, count * cap), BF16), shape((count * rows, LANES), F32)),
@@ -222,18 +223,23 @@
         )
         return (*plan, pre, lax.ppermute(pre, "rep", [(0, 1), (1, 0)]))
 
-    def lowered(offsets, step, outs, *terms):
+    def lowered(offsets, step, outs, *terms, after=()):
         return call(
-            functools.partial(down_kernel, len(offsets), len(terms)), outs, (*step, *(downs[i] for i in offsets), *terms)
+            functools.partial(down_kernel, len(offsets), len(terms)),
+            outs,
+            (*step, *(downs[i] for i in offsets), *terms),
+            after=after,
         )
 
-    pair = shape((2 * rows, width), F32)
+    both, single = shape((2 * rows, width), F32), shape((2 * rows, width), BF16)
     here = raised((0, 1), blocks[:1])
-    there = [raised((i,), blocks[1:], here[-1] if i == 0 else None) for i in (0, 1)]
-    own = lowered((0, 1), here, pair)
-    first = lowered((0,), there[0], shape((2 * (near - 1) * rows, width), F32))
-    sends = lowered((1,), there[1], (shape(pair.shape, BF16),) * (near - 1), first)
-    back = [swap(s, 2 * k) for k, s in enumerate(sends, 1)]
+    corner = raised((0, 1), blocks[3:])
+    there = [raised((i,), blocks[1:3], here[-1:] * (1 - i), corner[2:3] * (1 - i)) for i in (0, 1)]
+    diagonal = lowered((0, 1), corner, single)
+    first = lowered((0,), there[0], shape((4 * rows, width), F32), after=(diagonal,))
+    sends = lowered((1,), there[1], (single,) * 2, first)
+    own = lowered((0, 1), here, both, after=sends[:1])
+    back = [swap(s, 2 * k) for k, s in enumerate((*sends, diagonal), 1)]
     mine, theirs = call(
         functools.partial(half_kernel, rows),
         (shape((rows, width), F32), shape((rows, width), BF16)),

time: 43.2 us -> 40.7 us (0.942)
  waiting for transfers between devices: 13.2 us -> 7.16 us
  Pallas kernels: 10.8 us -> 13.6 us
  starting transfers between devices: 18.9 us -> 19.7 us
    ppermute x3 -> x4, waiting for transfers between devices: 3.58 us -> 0.35 us  [raised(): return (*plan, pre, lax.ppermute(pre, 'rep', [(0, 1), (1, 0)]))]
    ppermute x10, waiting for transfers between devices: 9.61 us -> 6.81 us  [swap(): return lax.ppermute(x, 'ep', [(i, i ^ distance) for i in range(n)])]
    pallas_call x15 -> x18, Pallas kernels: 10.8 us -> 13.6 us  [call(): pl.pallas_call(body, out_shape=outs, in_specs=specs + [pl.BlockSpec(memor...]
    ppermute x3 -> x4, starting transfers between devices: 4.14 us -> 5.04 us  [raised(): return (*plan, pre, lax.ppermute(pre, 'rep', [(0, 1), (1, 0)]))]
  transfers between devices with their start and end apart: 13 -> 14, of which waited for: 7 -> 5; matrix products, arithmetic and copies ran while one was open for 0% -> 0% of each run, Pallas kernels for 21% -> 32%
where the time goes in v4:
time: 40.7 us; the launch traced here: 40.6 us
  starting transfers between devices  19.7 us (48%)
  Pallas kernels  13.6 us (33%)
  waiting for transfers between devices  7.16 us (18%)
    ppermute x10, starting transfers between devices, swap(): return lax.ppermute(x, 'ep', [(i, i ^ distance) for i in range(n)])  14.6 us
    pallas_call x18, Pallas kernels, call(): pl.pallas_call(body, out_shape=outs, in_specs=specs + [pl.BlockSpec(memor...  13.6 us
    ppermute x10, waiting for transfers between devices, swap(): return lax.ppermute(x, 'ep', [(i, i ^ distance) for i in range(n)])  6.81 us
    ppermute x4, starting transfers between devices, raised(): return (*plan, pre, lax.ppermute(pre, 'rep', [(0, 1), (1, 0)]))  5.04 us
  transfers between devices with their start and end apart: 14, of which 5 were waited for; matrix products, arithmetic and copies ran while one was open for 0% of the time, Pallas kernels for 32%

profile of v4, /device:TPU:0, one launch (start us, length us, event | category | flops | bytes accessed | tf_op | source)
XLA Modules:
  0.0 40.6 jit_solution(13591840996224561393)
XLA Ops:
  0.0 0.5 %collective-permute-start = (bf16[1792,1024]{1,0:T(8,128)(2,1)}, bf16[1792,1024]{1,0:T(8,128)(2,1)S(1)}, u32[]{:S(2)}, u32[]{:S(2)}) collective-permute-start(bf16[1792,1024]{1,0:T(8,128)(2,1)} %bitcast.8), channel_id=1, source_target_pairs={{0,2},{2,0},{4,6},{6,4},{8,10},{10,8},{12,14},{14,12},{16,18},{18,... | collective-permute-start | bytes 11010056 | tf_op jit(solution)/shard_map/ppermute | solution.py:188
  0.5 0.1 collective-permute-start.3
  0.5 1.0 %shard_map.56.refs_0_ = bf16[16,1920]{1,0:T(8,128)(2,1)S(1)} custom-call(bf16[16,1792]{1,0:T(8,128)(2,1)} %refs_0_.1, s32[8,16]{1,0:T(8,128)} %bitcast.10, f32[8,16]{1,0:T(8,128)} %bitcast.11), custom_call_target="tpu_custom_call" | custom-call | flops 1 | bytes 1 | tf_op jit(solution)/shard_map/pallas_call | solution.py:24
  1.5 4.1 %collective-permute-start.1 = (bf16[16,1920]{1,0:T(8,128)(2,1)S(1)}, bf16[16,1920]{1,0:T(8,128)(2,1)S(1)}, u32[]{:S(2)}, u32[]{:S(2)}) collective-permute-start(bf16[16,1920]{1,0:T(8,128)(2,1)S(1)} %shard_map.56.refs_0_), channel_id=1, source_target_pairs={{0,16},{2,18},{4,20},{6,22},{8,24},{10,26},{12,28},{14,30},{16,0},... | collective-permute-start | bytes 184328 | tf_op jit(solution)/shard_map/ppermute | solution.py:188
  5.6 2.1 %shard_map.55.refs_2_.refs_0_ = bf16[1792,1024]{1,0:T(8,128)(2,1)S(1)} custom-call(bf16[1792,1024]{1,0:T(8,128)(2,1)} %bitcast.9), custom_call_target="tpu_custom_call" | custom-call | flops 1 | bytes 1 | tf_op jit(solution)/shard_map/pallas_call | solution.py:24
  7.7 0.8 %collective-permute-done.1.refs_1_ = bf16[16,1920]{1,0:T(8,128)(2,1)S(1)} collective-permute-done((bf16[16,1920]{1,0:T(8,128)(2,1)S(1)}, bf16[16,1920]{1,0:T(8,128)(2,1)S(1)}, u32[]{:S(2)}, u32[]{:S(2)}) %collective-permute-start.1) | collective-permute-done | bytes 61472 | tf_op jit(solution)/shard_map/ppermute | solution.py:188
  8.5 2.4 %collective-permute-start.7 = (bf16[32,1920]{1,0:T(8,128)(2,1)S(1)}, bf16[32,1920]{1,0:T(8,128)(2,1)S(1)}, u32[]{:S(2)}, u32[]{:S(2)}) collective-permute-start(bf16[32,1920]{1,0:T(8,128)(2,1)S(1)} %shard_map.57.refs_2_), channel_id=1, source_target_pairs={{0,12},{2,14},{4,8},{6,10},{8,4},{10,6},{12,0},{14,2},{16,28},{18,... | collective-permute-start | bytes 368648 | tf_op jit(solution)/shard_map/ppermute | solution.py:188
  10.8 1.7 %collective-permute-start.5 = (bf16[32,1920]{1,0:T(8,128)(2,1)S(1)}, bf16[32,1920]{1,0:T(8,128)(2,1)S(1)}, u32[]{:S(2)}, u32[]{:S(2)}) collective-permute-start(bf16[32,1920]{1,0:T(8,128)(2,1)S(1)} %shard_map.57.refs_2_), channel_id=1, source_target_pairs={{0,8},{2,10},{4,12},{6,14},{8,0},{10,2},{12,4},{14,6},{16,24},{18,... | collective-permute-start | bytes 368648 | tf_op jit(solution)/shard_map/ppermute | solution.py:188
  12.5 0.0 collective-permute-start.4
  12.5 0.0 collective-permute-done.refs_1_.refs_0_
  12.5 1.5 %shard_map.58 = (bf16[48,1024]{1,0:T(8,128)(2,1)S(1)}, f32[8,128]{1,0:T(8,128)S(1)}) custom-call(bf16[1792,1024]{1,0:T(8,128)(2,1)S(1)} %shard_map.55.refs_2_.refs_0_, bf16[1792,1024]{1,0:T(8,128)(2,1)S(1)} %collective-permute-done.refs_1_.refs_0_, bf16[32,1920]{1,0:T(8,128)(2,1)S(1)} %shard_map.57.refs_2_), custom_call_target="tpu_custom_call" | custom-call | flops 1 | bytes 1 | tf_op jit(solution)/shard_map/pallas_call | solution.py:24
  14.1 2.1 %collective-permute-start.2 = (bf16[48,1024]{1,0:T(8,128)(2,1)S(1)}, bf16[48,1024]{1,0:T(8,128)(2,1)S(1)}, u32[]{:S(2)}, u32[]{:S(2)}) collective-permute-start(bf16[48,1024]{1,0:T(8,128)(2,1)S(1)} %get-tuple-element.28.refs_2_), channel_id=1, source_target_pairs={{0,1},{1,0},{2,3},{3,2},{4,5},{5,4},{6,7},{7,6},{8,9},{9,8},{10,11... | collective-permute-start | bytes 294920 | tf_op jit(solution)/shard_map/ppermute | solution.py:224
  16.1 0.0 collective-permute-done.7.refs_2_
  16.1 1.5 %shard_map.62 = (bf16[48,1024]{1,0:T(8,128)(2,1)S(1)}, f32[8,128]{1,0:T(8,128)S(1)}) custom-call(bf16[1792,1024]{1,0:T(8,128)(2,1)S(1)} %shard_map.55.refs_2_.refs_0_, bf16[1792,1024]{1,0:T(8,128)(2,1)S(1)} %collective-permute-done.refs_1_.refs_0_, bf16[32,1920]{1,0:T(8,128)(2,1)S(1)} %collective-permute-done.7.refs_2_), custom_call_target="tpu_custom_call" | custom-call | flops 1 | bytes 1 | tf_op jit(solution)/shard_map/pallas_call | solution.py:24
  17.7 0.0 copy-start
  17.7 0.9 %collective-permute-start.9 = (bf16[48,1024]{1,0:T(8,128)(2,1)S(1)}, bf16[48,1024]{1,0:T(8,128)(2,1)S(1)}, u32[]{:S(2)}, u32[]{:S(2)}) collective-permute-start(bf16[48,1024]{1,0:T(8,128)(2,1)S(1)} %get-tuple-element.33.refs_3_.refs_2_), channel_id=1, source_target_pairs={{0,1},{1,0},{2,3},{3,2},{4,5},{5,4},{6,7},{7,6},{8,9},{9,8},{10,11... | collective-permute-start | bytes 294920 | tf_op jit(solution)/shard_map/ppermute | solution.py:224
  18.6 0.0 collective-permute-done.5.refs_2_
  18.6 0.0 collective-permute-done.4.refs_1_
  18.6 0.9 %shard_map.63 = (bf16[48,1024]{1,0:T(8,128)(2,1)S(1)}, f32[8,128]{1,0:T(8,128)S(1)}) custom-call(bf16[1792,1024]{1,0:T(8,128)(2,1)S(1)} %shard_map.55.refs_2_.refs_0_, bf16[32,1920]{1,0:T(8,128)(2,1)S(1)} %collective-permute-done.4.refs_1_, bf16[32,1920]{1,0:T(8,128)(2,1)S(1)} %collective-permute-done.5.refs_2_, ...), custom_call_target="tpu_custom_call" | custom-call | flops 1 | bytes 1 | tf_op jit(solution)/shard_map/pallas_call | solution.py:24
  19.4 0.3 collective-permute-done.2.refs_1_.refs_3_
  19.8 1.4 %collective-permute-start.8 = (bf16[48,1024]{1,0:T(8,128)(2,1)S(1)}, bf16[48,1024]{1,0:T(8,128)(2,1)S(1)}, u32[]{:S(2)}, u32[]{:S(2)}) collective-permute-start(bf16[48,1024]{1,0:T(8,128)(2,1)S(1)} %shard_map.65.refs_2_), channel_id=1, source_target_pairs={{0,1},{1,0},{2,3},{3,2},{4,5},{5,4},{6,7},{7,6},{8,9},{9,8},{10,11... | collective-permute-start | bytes 294920 | tf_op jit(solution)/shard_map/ppermute | solution.py:224
  21.1 0.9 %shard_map.60 = (bf16[48,1024]{1,0:T(8,128)(2,1)S(1)}, f32[8,128]{1,0:T(8,128)S(1)}) custom-call(bf16[1792,1024]{1,0:T(8,128)(2,1)S(1)} %collective-permute-done.refs_1_.refs_0_, bf16[32,1920]{1,0:T(8,128)(2,1)S(1)} %collective-permute-done.4.refs_1_, bf16[32,1920]{1,0:T(8,128)(2,1)S(1)} %collective-permute-done.5.refs_2_), custom_call_target="tpu_custom_call" | custom-call | flops 1 | bytes 1 | tf_op jit(solution)/shard_map/pallas_call | solution.py:24
  22.0 0.7 %collective-permute-start.6 = (bf16[48,1024]{1,0:T(8,128)(2,1)S(1)}, bf16[48,1024]{1,0:T(8,128)(2,1)S(1)}, u32[]{:S(2)}, u32[]{:S(2)}) collective-permute-start(bf16[48,1024]{1,0:T(8,128)(2,1)S(1)} %get-tuple-element.32.refs_2_), channel_id=1, source_target_pairs={{0,1},{1,0},{2,3},{3,2},{4,5},{5,4},{6,7},{7,6},{8,9},{9,8},{10,11... | collective-permute-start | bytes 294920 | tf_op jit(solution)/shard_map/ppermute | solution.py:224
  22.8 0.2 shard_map.64
  23.0 0.2 shard_map.61
  23.2 0.2 shard_map.66
  23.5 0.0 collective-permute-done.3.refs_5_.refs_4_
  23.5 0.0 collective-permute-done.9.refs_3_
  23.5 0.0 copy-done
  23.5 1.3 %shard_map.67.refs_5_ = bf16[32,1792]{1,0:T(8,128)(2,1)S(1)} custom-call(bf16[64,48]{1,0:T(8,128)(2,1)S(1)} %get-tuple-element.39.refs_0_, f32[64,128]{1,0:T(8,128)S(1)} %get-tuple-element.40.refs_1_, bf16[48,1024]{1,0:T(8,128)(2,1)S(1)} %get-tuple-element.33.refs_3_.refs_2_, bf16[48,1024]{1,0:T(8,128)(2,1)S(1)} %collective-permute-done.9.refs_3_, ...), custom_call_target="tpu_custom_call" | custom-call | flops 1 | bytes 1 | tf_op jit(solution)/shard_map/pallas_call | solution.py:24
  24.8 2.3 %collective-permute-start.12 = (bf16[32,1792]{1,0:T(8,128)(2,1)S(1)}, bf16[32,1792]{1,0:T(8,128)(2,1)S(1)}, u32[]{:S(2)}, u32[]{:S(2)}) collective-permute-start(bf16[32,1792]{1,0:T(8,128)(2,1)S(1)} %shard_map.67.refs_5_), channel_id=1, source_target_pairs={{0,12},{2,14},{4,8},{6,10},{8,4},{10,6},{12,0},{14,2},{16,28},{18,... | collective-permute-start | bytes 344072 | tf_op jit(solution)/shard_map/ppermute | solution.py:188
  27.1 0.0 collective-permute-done.8.refs_3_
  27.1 0.7 %shard_map.68.refs_5_ = f32[64,1792]{1,0:T(8,128)S(1)} custom-call(bf16[64,48]{1,0:T(8,128)(2,1)S(1)} %get-tuple-element.35.refs_0_, f32[64,128]{1,0:T(8,128)S(1)} %get-tuple-element.36.refs_1_, bf16[48,1024]{1,0:T(8,128)(2,1)S(1)} %shard_map.65.refs_2_, bf16[48,1024]{1,0:T(8,128)(2,1)S(1)} %collective-permute-done.8.refs_3_, ...), custom_call_target="tpu_custom_call" | custom-call | flops 1 | bytes 1 | tf_op jit(solution)/shard_map/pallas_call | solution.py:24
  27.9 0.0 collective-permute-done.6.refs_3_
  27.9 0.8 %shard_map.69 = (bf16[32,1792]{1,0:T(8,128)(2,1)S(1)}, bf16[32,1792]{1,0:T(8,128)(2,1)S(1)}) custom-call(bf16[64,48]{1,0:T(8,128)(2,1)S(1)} %get-tuple-element.30.refs_0_, f32[64,128]{1,0:T(8,128)S(1)} %get-tuple-element.31.refs_1_, bf16[48,1024]{1,0:T(8,128)(2,1)S(1)} %get-tuple-element.32.refs_2_, bf16[48,1024]{1,0:T(8,128)(2,1)S(1)} %collective-permute-done.6.refs_3_, ...), custom_call_target="tpu_custom_call" | custom-call | flops 1 | bytes 1 | tf_op jit(solution)/shard_map/pallas_call | solution.py:24
  28.6 1.3 %collective-permute-start.11 = (bf16[32,1792]{1,0:T(8,128)(2,1)S(1)}, bf16[32,1792]{1,0:T(8,128)(2,1)S(1)}, u32[]{:S(2)}, u32[]{:S(2)}) collective-permute-start(bf16[32,1792]{1,0:T(8,128)(2,1)S(1)} %get-tuple-element.42), channel_id=1, source_target_pairs={{0,8},{2,10},{4,12},{6,14},{8,0},{10,2},{12,4},{14,6},{16,24},{18,... | collective-permute-start | bytes 344072 | tf_op jit(solution)/shard_map/ppermute | solution.py:188
  29.9 0.1 collective-permute-start.10
  30.0 0.2 shard_map.59
  30.2 1.3 %shard_map.70.refs_0_ = f32[32,1792]{1,0:T(8,128)S(1)} custom-call(bf16[64,48]{1,0:T(8,128)(2,1)S(1)} %get-tuple-element.26.refs_0_, f32[64,128]{1,0:T(8,128)S(1)} %get-tuple-element.27.refs_1_, bf16[48,1024]{1,0:T(8,128)(2,1)S(1)} %get-tuple-element.28.refs_2_, bf16[48,1024]{1,0:T(8,128)(2,1)S(1)} %collective-permute-done.2.refs_1_.refs_3_, ...), custom_call_target="tpu_custom_call" | custom-call | flops 1 | bytes 1 | tf_op jit(solution)/shard_map/pallas_call | solution.py:24
  31.5 0.0 collective-permute-done.12.refs_3_
  31.5 2.0 %collective-permute-done.11.refs_2_ = bf16[32,1792]{1,0:T(8,128)(2,1)S(1)} collective-permute-done((bf16[32,1792]{1,0:T(8,128)(2,1)S(1)}, bf16[32,1792]{1,0:T(8,128)(2,1)S(1)}, u32[]{:S(2)}, u32[]{:S(2)}) %collective-permute-start.11) | collective-permute-done | bytes 114720 | tf_op jit(solution)/shard_map/ppermute | solution.py:188
  33.5 1.2 %collective-permute-done.10.refs_1_ = bf16[32,1792]{1,0:T(8,128)(2,1)S(1)} collective-permute-done((bf16[32,1792]{1,0:T(8,128)(2,1)S(1)}, bf16[32,1792]{1,0:T(8,128)(2,1)S(1)}, u32[]{:S(2)}, u32[]{:S(2)}) %collective-permute-start.10) | collective-permute-done | bytes 114720 | tf_op jit(solution)/shard_map/ppermute | solution.py:188
  34.7 0.1 shard_map.71
  34.8 2.3 %collective-permute-start.13 = (bf16[16,1792]{1,0:T(8,128)(2,1)S(1)}, bf16[16,1792]{1,0:T(8,128)(2,1)S(1)}, u32[]{:S(2)}, u32[]{:S(2)}) collective-permute-start(bf16[16,1792]{1,0:T(8,128)(2,1)S(1)} %get-tuple-element.44), channel_id=1, source_target_pairs={{0,16},{2,18},{4,20},{6,22},{8,24},{10,26},{12,28},{14,30},{16,0},... | collective-permute-start | bytes 172040 | tf_op jit(solution)/shard_map/ppermute | solution.py:188
  37.1 2.8 %collective-permute-done.13.refs_1_ = bf16[16,1792]{1,0:T(8,128)(2,1)S(1)} collective-permute-done((bf16[16,1792]{1,0:T(8,128)(2,1)S(1)}, bf16[16,1792]{1,0:T(8,128)(2,1)S(1)}, u32[]{:S(2)}, u32[]{:S(2)}) %collective-permute-start.13) | collective-permute-done | bytes 57376 | tf_op jit(solution)/shard_map/ppermute | solution.py:188
  39.9 0.6 %shard_map.72 = bf16[16,1792]{1,0:T(8,128)(2,1)} custom-call(f32[16,1792]{1,0:T(8,128)S(1)} %get-tuple-element.43.refs_0_, bf16[16,1792]{1,0:T(8,128)(2,1)S(1)} %collective-permute-done.13.refs_1_), custom_call_target="tpu_custom_call" | custom-call | flops 1 | bytes 1 | tf_op jit(solution)/shard_map/pallas_call | solution.py:24
  (2 shorter events, 0.0 us)
Async XLA Ops:
  0.0 12.5 %collective-permute-start = (bf16[1792,1024]{1,0:T(8,128)(2,1)}, bf16[1792,1024]{1,0:T(8,128)(2,1)S(1)}, u32[]{:S(2)}, u32[]{:S(2)}) collective-permute-start(bf16[1792,1024]{1,0:T(8,128)(2,1)} %bitcast.8), channel_id=1, source_target_pairs={{0,2},{2,0},{4,6},{6,4},{8,10},{10,8},{12,14},{14,12},{16,18},{18,... | collective-permute-start | bytes 11010056 | tf_op jit(solution)/shard_map/ppermute | solution.py:188
  0.5 23.0 %collective-permute-start.3 = (bf16[1024,1792]{1,0:T(8,128)(2,1)}, bf16[1024,1792]{1,0:T(8,128)(2,1)S(1)}, u32[]{:S(2)}, u32[]{:S(2)}) collective-permute-start(bf16[1024,1792]{1,0:T(8,128)(2,1)} %bitcast.4), channel_id=1, source_target_pairs={{0,2},{2,0},{4,6},{6,4},{8,10},{10,8},{12,14},{14,12},{16,18},{18,... | collective-permute-start | bytes 11010056 | tf_op jit(solution)/shard_map/ppermute | solution.py:188
  1.5 7.0 %collective-permute-start.1 = (bf16[16,1920]{1,0:T(8,128)(2,1)S(1)}, bf16[16,1920]{1,0:T(8,128)(2,1)S(1)}, u32[]{:S(2)}, u32[]{:S(2)}) collective-permute-start(bf16[16,1920]{1,0:T(8,128)(2,1)S(1)} %shard_map.56.refs_0_), channel_id=1, source_target_pairs={{0,16},{2,18},{4,20},{6,22},{8,24},{10,26},{12,28},{14,30},{16,0},... | collective-permute-start | bytes 184328 | tf_op jit(solution)/shard_map/ppermute | solution.py:188
  8.5 7.7 %collective-permute-start.7 = (bf16[32,1920]{1,0:T(8,128)(2,1)S(1)}, bf16[32,1920]{1,0:T(8,128)(2,1)S(1)}, u32[]{:S(2)}, u32[]{:S(2)}) collective-permute-start(bf16[32,1920]{1,0:T(8,128)(2,1)S(1)} %shard_map.57.refs_2_), channel_id=1, source_target_pairs={{0,12},{2,14},{4,8},{6,10},{8,4},{10,6},{12,0},{14,2},{16,28},{18,... | collective-permute-start | bytes 368648 | tf_op jit(solution)/shard_map/ppermute | solution.py:188
  10.8 7.7 %collective-permute-start.5 = (bf16[32,1920]{1,0:T(8,128)(2,1)S(1)}, bf16[32,1920]{1,0:T(8,128)(2,1)S(1)}, u32[]{:S(2)}, u32[]{:S(2)}) collective-permute-start(bf16[32,1920]{1,0:T(8,128)(2,1)S(1)} %shard_map.57.refs_2_), channel_id=1, source_target_pairs={{0,8},{2,10},{4,12},{6,14},{8,0},{10,2},{12,4},{14,6},{16,24},{18,... | collective-permute-start | bytes 368648 | tf_op jit(solution)/shard_map/ppermute | solution.py:188
  12.5 6.1 %collective-permute-start.4 = (bf16[32,1920]{1,0:T(8,128)(2,1)S(1)}, bf16[32,1920]{1,0:T(8,128)(2,1)S(1)}, u32[]{:S(2)}, u32[]{:S(2)}) collective-permute-start(bf16[32,1920]{1,0:T(8,128)(2,1)S(1)} %shard_map.57.refs_2_), channel_id=1, source_target_pairs={{0,4},{2,6},{4,0},{6,2},{8,12},{10,14},{12,8},{14,10},{16,20},{18,... | collective-permute-start | bytes 368648 | tf_op jit(solution)/shard_map/ppermute | solution.py:188
  14.1 5.7 %collective-permute-start.2 = (bf16[48,1024]{1,0:T(8,128)(2,1)S(1)}, bf16[48,1024]{1,0:T(8,128)(2,1)S(1)}, u32[]{:S(2)}, u32[]{:S(2)}) collective-permute-start(bf16[48,1024]{1,0:T(8,128)(2,1)S(1)} %get-tuple-element.28.refs_2_), channel_id=1, source_target_pairs={{0,1},{1,0},{2,3},{3,2},{4,5},{5,4},{6,7},{7,6},{8,9},{9,8},{10,11... | collective-permute-start | bytes 294920 | tf_op jit(solution)/shard_map/ppermute | solution.py:224
  17.7 5.8 %copy-start = (bf16[1,1024,1792]{2,1,0:T(8,128)(2,1)S(1)}, bf16[1,1024,1792]{2,1,0:T(8,128)(2,1)}, u32[]{:S(2)}) copy-start(bf16[1,1024,1792]{2,1,0:T(8,128)(2,1)} %param.9) | copy-start | bytes 11010052
  17.7 5.8 %collective-permute-start.9 = (bf16[48,1024]{1,0:T(8,128)(2,1)S(1)}, bf16[48,1024]{1,0:T(8,128)(2,1)S(1)}, u32[]{:S(2)}, u32[]{:S(2)}) collective-permute-start(bf16[48,1024]{1,0:T(8,128)(2,1)S(1)} %get-tuple-element.33.refs_3_.refs_2_), channel_id=1, source_target_pairs={{0,1},{1,0},{2,3},{3,2},{4,5},{5,4},{6,7},{7,6},{8,9},{9,8},{10,11... | collective-permute-start | bytes 294920 | tf_op jit(solution)/shard_map/ppermute | solution.py:224
  19.8 7.3 %collective-permute-start.8 = (bf16[48,1024]{1,0:T(8,128)(2,1)S(1)}, bf16[48,1024]{1,0:T(8,128)(2,1)S(1)}, u32[]{:S(2)}, u32[]{:S(2)}) collective-permute-start(bf16[48,1024]{1,0:T(8,128)(2,1)S(1)} %shard_map.65.refs_2_), channel_id=1, source_target_pairs={{0,1},{1,0},{2,3},{3,2},{4,5},{5,4},{6,7},{7,6},{8,9},{9,8},{10,11... | collective-permute-start | bytes 294920 | tf_op jit(solution)/shard_map/ppermute | solution.py:224
  22.0 5.8 %collective-permute-start.6 = (bf16[48,1024]{1,0:T(8,128)(2,1)S(1)}, bf16[48,1024]{1,0:T(8,128)(2,1)S(1)}, u32[]{:S(2)}, u32[]{:S(2)}) collective-permute-start(bf16[48,1024]{1,0:T(8,128)(2,1)S(1)} %get-tuple-element.32.refs_2_), channel_id=1, source_target_pairs={{0,1},{1,0},{2,3},{3,2},{4,5},{5,4},{6,7},{7,6},{8,9},{9,8},{10,11... | collective-permute-start | bytes 294920 | tf_op jit(solution)/shard_map/ppermute | solution.py:224
  24.8 6.7 %collective-permute-start.12 = (bf16[32,1792]{1,0:T(8,128)(2,1)S(1)}, bf16[32,1792]{1,0:T(8,128)(2,1)S(1)}, u32[]{:S(2)}, u32[]{:S(2)}) collective-permute-start(bf16[32,1792]{1,0:T(8,128)(2,1)S(1)} %shard_map.67.refs_5_), channel_id=1, source_target_pairs={{0,12},{2,14},{4,8},{6,10},{8,4},{10,6},{12,0},{14,2},{16,28},{18,... | collective-permute-start | bytes 344072 | tf_op jit(solution)/shard_map/ppermute | solution.py:188
  28.6 4.9 %collective-permute-start.11 = (bf16[32,1792]{1,0:T(8,128)(2,1)S(1)}, bf16[32,1792]{1,0:T(8,128)(2,1)S(1)}, u32[]{:S(2)}, u32[]{:S(2)}) collective-permute-start(bf16[32,1792]{1,0:T(8,128)(2,1)S(1)} %get-tuple-element.42), channel_id=1, source_target_pairs={{0,8},{2,10},{4,12},{6,14},{8,0},{10,2},{12,4},{14,6},{16,24},{18,... | collective-permute-start | bytes 344072 | tf_op jit(solution)/shard_map/ppermute | solution.py:188
  29.9 4.8 %collective-permute-start.10 = (bf16[32,1792]{1,0:T(8,128)(2,1)S(1)}, bf16[32,1792]{1,0:T(8,128)(2,1)S(1)}, u32[]{:S(2)}, u32[]{:S(2)}) collective-permute-start(bf16[32,1792]{1,0:T(8,128)(2,1)S(1)} %get-tuple-element.41.refs_6_), channel_id=1, source_target_pairs={{0,4},{2,6},{4,0},{6,2},{8,12},{10,14},{12,8},{14,10},{16,20},{18,... | collective-permute-start | bytes 344072 | tf_op jit(solution)/shard_map/ppermute | solution.py:188
  34.8 5.1 %collective-permute-start.13 = (bf16[16,1792]{1,0:T(8,128)(2,1)S(1)}, bf16[16,1792]{1,0:T(8,128)(2,1)S(1)}, u32[]{:S(2)}, u32[]{:S(2)}) collective-permute-start(bf16[16,1792]{1,0:T(8,128)(2,1)S(1)} %get-tuple-element.44), channel_id=1, source_target_pairs={{0,16},{2,18},{4,20},{6,22},{8,24},{10,26},{12,28},{14,30},{16,0},... | collective-permute-start | bytes 172040 | tf_op jit(solution)/shard_map/ppermute | solution.py:188

commit v5 on v4

--- a/solution.py
+++ b/solution.py
@@ -120,6 +120,8 @@
         size = ref.shape[0]
         x_ref[i * size : (i + 1) * size, :] = ref[:, :width]
         pieces += [ref[j : j + rows, width:].astype(F32) for j in range(0, size, rows)]
+    tokens = len(pieces) * rows
+    x_ref[tokens:, :] = jnp.zeros((LANES - tokens, width), BF16)
     lines = []
     for offset in offsets:
         here = iota((rows, LANES), 0) == lax.axis_index("ep") ^ offset
@@ -129,9 +131,8 @@
     step = 256
     parts = []
     for c in range(0, weights[0].shape[1], step):
-        parts.append([dot(x_ref[...], w_ref[:, c : c + step]).astype(BF16) for w_ref in weights])
-    slots, tokens = len(lines) * cap, len(lines) * rows
-    sel = selection(routing, rows, cap)[:slots, :tokens].astype(BF16)
+        parts.append([dot(x_ref[...], w_ref[:, c : c + step])[:tokens].astype(BF16) for w_ref in weights])
+    sel = selection(routing, rows, cap)[: len(lines) * cap, : len(lines) * rows].astype(BF16)
     for i, part in enumerate(parts):
         pre_ref[:, i * step : (i + 1) * step] = dot(sel, jnp.concatenate(part, axis=0)).astype(BF16)
 
@@ -153,7 +154,7 @@
     rows = outs[0].shape[0]
     step = 256
     for c in range(0, weights[0].shape[1], step):
-        total = [ref[:, c : c + step] for ref in sums]
+        total = [ref[:, c : c + step].astype(F32) for ref in sums]
         for i, w_ref in enumerate(weights):
             at = slice(i * size, (i + 1) * size)
             out = dot(hidden[at], w_ref[:, c : c + step]).astype(BF16).astype(F32)
@@ -206,12 +207,12 @@
     ups, downs = (up, swap(up_weight[0], 1)), (down, swap(down, 1))
 
     def raised(offsets, blocks, before=(), after=()):
-        count, size = len(offsets) * 2 * len(blocks), 2 * len(blocks) * rows
+        count = len(offsets) * 2 * len(blocks)
         pre, routing = call(
             functools.partial(up_kernel, rows, cap, offsets),
             (shape((count * cap, hidden), BF16), shape((LANES // rows, LANES), F32)),
             (*(ups[i] for i in offsets), *blocks),
-            scratch=[pltpu.VMEM((size, width), BF16)],
+            scratch=[pltpu.VMEM((LANES, width), BF16)],
             after=after,
         )
         if before:
@@ -233,13 +234,13 @@
 
     both, single = shape((2 * rows, width), F32), shape((2 * rows, width), BF16)
     here = raised((0, 1), blocks[:1])
-    corner = raised((0, 1), blocks[3:])
-    there = [raised((i,), blocks[1:3], here[-1:] * (1 - i), corner[2:3] * (1 - i)) for i in (0, 1)]
+    corner = raised((0, 1), blocks[3:], (), here[:2])
+    there = [raised((i,), blocks[1:3], here[-1:] * (1 - i), corner[:3] * (1 - i)) for i in (0, 1)]
     diagonal = lowered((0, 1), corner, single)
     first = lowered((0,), there[0], shape((4 * rows, width), F32), after=(diagonal,))
     sends = lowered((1,), there[1], (single,) * 2, first)
-    own = lowered((0, 1), here, both, after=sends[:1])
-    back = [swap(s, 2 * k) for k, s in enumerate((*sends, diagonal), 1)]
+    own = lowered((0, 1), here, both, swap(diagonal, 6), after=sends[:1])
+    back = [swap(s, 2 * k) for k, s in enumerate(sends, 1)]
     mine, theirs = call(
         functools.partial(half_kernel, rows),
         (shape((rows, width), F32), shape((rows, width), BF16)),

time: 40.7 us -> 40 us (0.983)
  Pallas kernels: 13.6 us -> 12.8 us
    pallas_call x18, Pallas kernels: 13.6 us -> 12.8 us  [call(): pl.pallas_call(body, out_shape=outs, in_specs=specs + [pl.BlockSpec(memor...]
  transfers between devices with their start and end apart: 14 -> 14, of which waited for: 5 -> 6; matrix products, arithmetic and copies ran while one was open for 0% -> 0% of each run, Pallas kernels for 32% -> 30%
where the time goes in v5:
time: 40 us; the launch traced here: 39.9 us
  starting transfers between devices  20.1 us (50%)
  Pallas kernels  12.8 us (32%)
  waiting for transfers between devices  6.8 us (17%)
    ppermute x10, starting transfers between devices, swap(): return lax.ppermute(x, 'ep', [(i, i ^ distance) for i in range(n)])  15 us
    pallas_call x18, Pallas kernels, call(): pl.pallas_call(body, out_shape=outs, in_specs=specs + [pl.BlockSpec(memor...  12.8 us
    ppermute x10, waiting for transfers between devices, swap(): return lax.ppermute(x, 'ep', [(i, i ^ distance) for i in range(n)])  6.65 us
    ppermute x4, starting transfers between devices, raised(): return (*plan, pre, lax.ppermute(pre, 'rep', [(0, 1), (1, 0)]))  5.1 us
  transfers between devices with their start and end apart: 14, of which 6 were waited for; matrix products, arithmetic and copies ran while one was open for 0% of the time, Pallas kernels for 30%

profile of v5, /device:TPU:0, one launch (start us, length us, event | category | flops | bytes accessed | tf_op | source)
XLA Modules:
  0.0 39.9 jit_solution(6898968016997471577)
XLA Ops:
  0.0 0.5 %collective-permute-start = (bf16[1792,1024]{1,0:T(8,128)(2,1)}, bf16[1792,1024]{1,0:T(8,128)(2,1)S(1)}, u32[]{:S(2)}, u32[]{:S(2)}) collective-permute-start(bf16[1792,1024]{1,0:T(8,128)(2,1)} %bitcast.8), channel_id=1, source_target_pairs={{0,2},{2,0},{4,6},{6,4},{8,10},{10,8},{12,14},{14,12},{16,18},{18,... | collective-permute-start | bytes 11010056 | tf_op jit(solution)/shard_map/ppermute | solution.py:189
  0.5 0.1 collective-permute-start.3
  0.5 1.0 %shard_map.56.refs_0_ = bf16[16,1920]{1,0:T(8,128)(2,1)S(1)} custom-call(bf16[16,1792]{1,0:T(8,128)(2,1)} %refs_0_.1, s32[8,16]{1,0:T(8,128)} %bitcast.10, f32[8,16]{1,0:T(8,128)} %bitcast.11), custom_call_target="tpu_custom_call" | custom-call | flops 1 | bytes 1 | tf_op jit(solution)/shard_map/pallas_call | solution.py:24
  1.5 4.1 %collective-permute-start.1 = (bf16[16,1920]{1,0:T(8,128)(2,1)S(1)}, bf16[16,1920]{1,0:T(8,128)(2,1)S(1)}, u32[]{:S(2)}, u32[]{:S(2)}) collective-permute-start(bf16[16,1920]{1,0:T(8,128)(2,1)S(1)} %shard_map.56.refs_0_), channel_id=1, source_target_pairs={{0,16},{2,18},{4,20},{6,22},{8,24},{10,26},{12,28},{14,30},{16,0},... | collective-permute-start | bytes 184328 | tf_op jit(solution)/shard_map/ppermute | solution.py:189
  5.6 2.1 %shard_map.55.refs_2_.refs_0_ = bf16[1792,1024]{1,0:T(8,128)(2,1)S(1)} custom-call(bf16[1792,1024]{1,0:T(8,128)(2,1)} %bitcast.9), custom_call_target="tpu_custom_call" | custom-call | flops 1 | bytes 1 | tf_op jit(solution)/shard_map/pallas_call | solution.py:24
  7.7 0.8 %collective-permute-done.1.refs_1_ = bf16[16,1920]{1,0:T(8,128)(2,1)S(1)} collective-permute-done((bf16[16,1920]{1,0:T(8,128)(2,1)S(1)}, bf16[16,1920]{1,0:T(8,128)(2,1)S(1)}, u32[]{:S(2)}, u32[]{:S(2)}) %collective-permute-start.1) | collective-permute-done | bytes 61472 | tf_op jit(solution)/shard_map/ppermute | solution.py:189
  8.5 2.4 %collective-permute-start.4 = (bf16[32,1920]{1,0:T(8,128)(2,1)S(1)}, bf16[32,1920]{1,0:T(8,128)(2,1)S(1)}, u32[]{:S(2)}, u32[]{:S(2)}) collective-permute-start(bf16[32,1920]{1,0:T(8,128)(2,1)S(1)} %shard_map.57.refs_2_), channel_id=1, source_target_pairs={{0,12},{2,14},{4,8},{6,10},{8,4},{10,6},{12,0},{14,2},{16,28},{18,... | collective-permute-start | bytes 368648 | tf_op jit(solution)/shard_map/ppermute | solution.py:189
  10.8 1.7 %collective-permute-start.8 = (bf16[32,1920]{1,0:T(8,128)(2,1)S(1)}, bf16[32,1920]{1,0:T(8,128)(2,1)S(1)}, u32[]{:S(2)}, u32[]{:S(2)}) collective-permute-start(bf16[32,1920]{1,0:T(8,128)(2,1)S(1)} %shard_map.57.refs_2_), channel_id=1, source_target_pairs={{0,8},{2,10},{4,12},{6,14},{8,0},{10,2},{12,4},{14,6},{16,24},{18,... | collective-permute-start | bytes 368648 | tf_op jit(solution)/shard_map/ppermute | solution.py:189
  12.5 0.0 collective-permute-start.7
  12.5 0.0 collective-permute-done.refs_1_.refs_0_
  12.5 1.3 %shard_map.58 = (bf16[48,1024]{1,0:T(8,128)(2,1)S(1)}, f32[8,128]{1,0:T(8,128)S(1)}) custom-call(bf16[1792,1024]{1,0:T(8,128)(2,1)S(1)} %shard_map.55.refs_2_.refs_0_, bf16[1792,1024]{1,0:T(8,128)(2,1)S(1)} %collective-permute-done.refs_1_.refs_0_, bf16[32,1920]{1,0:T(8,128)(2,1)S(1)} %shard_map.57.refs_2_), custom_call_target="tpu_custom_call" | custom-call | flops 1 | bytes 1 | tf_op jit(solution)/shard_map/pallas_call | solution.py:24
  13.8 2.1 %collective-permute-start.2 = (bf16[48,1024]{1,0:T(8,128)(2,1)S(1)}, bf16[48,1024]{1,0:T(8,128)(2,1)S(1)}, u32[]{:S(2)}, u32[]{:S(2)}) collective-permute-start(bf16[48,1024]{1,0:T(8,128)(2,1)S(1)} %get-tuple-element.28.refs_2_), channel_id=1, source_target_pairs={{0,1},{1,0},{2,3},{3,2},{4,5},{5,4},{6,7},{7,6},{8,9},{9,8},{10,11... | collective-permute-start | bytes 294920 | tf_op jit(solution)/shard_map/ppermute | solution.py:225
  15.9 0.2 shard_map.59
  16.1 0.0 collective-permute-done.4.refs_2_
  16.1 1.3 %shard_map.60 = (bf16[48,1024]{1,0:T(8,128)(2,1)S(1)}, f32[8,128]{1,0:T(8,128)S(1)}) custom-call(bf16[1792,1024]{1,0:T(8,128)(2,1)S(1)} %shard_map.55.refs_2_.refs_0_, bf16[1792,1024]{1,0:T(8,128)(2,1)S(1)} %collective-permute-done.refs_1_.refs_0_, bf16[32,1920]{1,0:T(8,128)(2,1)S(1)} %collective-permute-done.4.refs_2_, ...), custom_call_target="tpu_custom_call" | custom-call | flops 1 | bytes 1 | tf_op jit(solution)/shard_map/pallas_call | solution.py:24
  17.4 0.2 shard_map.61
  17.6 0.9 %collective-permute-start.5 = (bf16[48,1024]{1,0:T(8,128)(2,1)S(1)}, bf16[48,1024]{1,0:T(8,128)(2,1)S(1)}, u32[]{:S(2)}, u32[]{:S(2)}) collective-permute-start(bf16[48,1024]{1,0:T(8,128)(2,1)S(1)} %get-tuple-element.32.refs_2_.refs_5_), channel_id=1, source_target_pairs={{0,1},{1,0},{2,3},{3,2},{4,5},{5,4},{6,7},{7,6},{8,9},{9,8},{10,11... | collective-permute-start | bytes 294920 | tf_op jit(solution)/shard_map/ppermute | solution.py:225
  18.5 0.0 collective-permute-done.8.refs_2_
  18.5 0.0 collective-permute-done.7.refs_1_
  18.5 0.0 copy-start
  18.5 0.8 %shard_map.65 = (bf16[48,1024]{1,0:T(8,128)(2,1)S(1)}, f32[8,128]{1,0:T(8,128)S(1)}) custom-call(bf16[1792,1024]{1,0:T(8,128)(2,1)S(1)} %shard_map.55.refs_2_.refs_0_, bf16[32,1920]{1,0:T(8,128)(2,1)S(1)} %collective-permute-done.7.refs_1_, bf16[32,1920]{1,0:T(8,128)(2,1)S(1)} %collective-permute-done.8.refs_2_, ...), custom_call_target="tpu_custom_call" | custom-call | flops 1 | bytes 1 | tf_op jit(solution)/shard_map/pallas_call | solution.py:24
  19.3 0.0 collective-permute-done.2.refs_1_.refs_3_
  19.4 1.4 %collective-permute-start.10 = (bf16[48,1024]{1,0:T(8,128)(2,1)S(1)}, bf16[48,1024]{1,0:T(8,128)(2,1)S(1)}, u32[]{:S(2)}, u32[]{:S(2)}) collective-permute-start(bf16[48,1024]{1,0:T(8,128)(2,1)S(1)} %shard_map.67.refs_2_), channel_id=1, source_target_pairs={{0,1},{1,0},{2,3},{3,2},{4,5},{5,4},{6,7},{7,6},{8,9},{9,8},{10,11... | collective-permute-start | bytes 294920 | tf_op jit(solution)/shard_map/ppermute | solution.py:225
  20.8 0.8 %shard_map.63 = (bf16[48,1024]{1,0:T(8,128)(2,1)S(1)}, f32[8,128]{1,0:T(8,128)S(1)}) custom-call(bf16[1792,1024]{1,0:T(8,128)(2,1)S(1)} %collective-permute-done.refs_1_.refs_0_, bf16[32,1920]{1,0:T(8,128)(2,1)S(1)} %collective-permute-done.7.refs_1_, bf16[32,1920]{1,0:T(8,128)(2,1)S(1)} %collective-permute-done.8.refs_2_), custom_call_target="tpu_custom_call" | custom-call | flops 1 | bytes 1 | tf_op jit(solution)/shard_map/pallas_call | solution.py:24
  21.6 0.7 %collective-permute-start.9 = (bf16[48,1024]{1,0:T(8,128)(2,1)S(1)}, bf16[48,1024]{1,0:T(8,128)(2,1)S(1)}, u32[]{:S(2)}, u32[]{:S(2)}) collective-permute-start(bf16[48,1024]{1,0:T(8,128)(2,1)S(1)} %get-tuple-element.36.refs_2_), channel_id=1, source_target_pairs={{0,1},{1,0},{2,3},{3,2},{4,5},{5,4},{6,7},{7,6},{8,9},{9,8},{10,11... | collective-permute-start | bytes 294920 | tf_op jit(solution)/shard_map/ppermute | solution.py:225
  22.3 0.2 shard_map.64
  22.5 0.2 shard_map.66
  22.7 0.0 collective-permute-done.3.refs_5_.refs_4_
  22.7 0.1 collective-permute-done.5.refs_3_
  22.8 0.0 copy-done
  22.9 1.3 %shard_map.62.refs_5_ = bf16[32,1792]{1,0:T(8,128)(2,1)S(1)} custom-call(bf16[64,48]{1,0:T(8,128)(2,1)S(1)} %get-tuple-element.30.refs_0_.refs_3_, f32[64,128]{1,0:T(8,128)S(1)} %get-tuple-element.31.refs_1_.refs_4_, bf16[48,1024]{1,0:T(8,128)(2,1)S(1)} %get-tuple-element.32.refs_2_.refs_5_, bf16[48,1024]{1,0:T(8,128)(2,1)S(1)} %collective-permute-done.5.refs_3_, ...), custom_call_target="tpu_custom_call" | custom-call | flops 1 | bytes 1 | tf_op jit(solution)/shard_map/pallas_call | solution.py:24
  24.1 2.5 %collective-permute-start.6 = (bf16[32,1792]{1,0:T(8,128)(2,1)S(1)}, bf16[32,1792]{1,0:T(8,128)(2,1)S(1)}, u32[]{:S(2)}, u32[]{:S(2)}) collective-permute-start(bf16[32,1792]{1,0:T(8,128)(2,1)S(1)} %shard_map.62.refs_5_), channel_id=1, source_target_pairs={{0,12},{2,14},{4,8},{6,10},{8,4},{10,6},{12,0},{14,2},{16,28},{18,... | collective-permute-start | bytes 344072 | tf_op jit(solution)/shard_map/ppermute | solution.py:189
  26.6 0.0 collective-permute-done.10.refs_3_
  26.6 0.7 %shard_map.68.refs_5_ = f32[64,1792]{1,0:T(8,128)S(1)} custom-call(bf16[64,48]{1,0:T(8,128)(2,1)S(1)} %get-tuple-element.38.refs_0_, f32[64,128]{1,0:T(8,128)S(1)} %get-tuple-element.39.refs_1_, bf16[48,1024]{1,0:T(8,128)(2,1)S(1)} %shard_map.67.refs_2_, bf16[48,1024]{1,0:T(8,128)(2,1)S(1)} %collective-permute-done.10.refs_3_, ...), custom_call_target="tpu_custom_call" | custom-call | flops 1 | bytes 1 | tf_op jit(solution)/shard_map/pallas_call | solution.py:24
  27.4 0.0 collective-permute-done.9.refs_3_
  27.4 0.8 %shard_map.69 = (bf16[32,1792]{1,0:T(8,128)(2,1)S(1)}, bf16[32,1792]{1,0:T(8,128)(2,1)S(1)}) custom-call(bf16[64,48]{1,0:T(8,128)(2,1)S(1)} %get-tuple-element.34.refs_0_, f32[64,128]{1,0:T(8,128)S(1)} %get-tuple-element.35.refs_1_, bf16[48,1024]{1,0:T(8,128)(2,1)S(1)} %get-tuple-element.36.refs_2_, bf16[48,1024]{1,0:T(8,128)(2,1)S(1)} %collective-permute-done.9.refs_3_, ...), custom_call_target="tpu_custom_call" | custom-call | flops 1 | bytes 1 | tf_op jit(solution)/shard_map/pallas_call | solution.py:24
  28.1 1.1 %collective-permute-start.12 = (bf16[32,1792]{1,0:T(8,128)(2,1)S(1)}, bf16[32,1792]{1,0:T(8,128)(2,1)S(1)}, u32[]{:S(2)}, u32[]{:S(2)}) collective-permute-start(bf16[32,1792]{1,0:T(8,128)(2,1)S(1)} %get-tuple-element.42), channel_id=1, source_target_pairs={{0,8},{2,10},{4,12},{6,14},{8,0},{10,2},{12,4},{14,6},{16,24},{18,... | collective-permute-start | bytes 344072 | tf_op jit(solution)/shard_map/ppermute | solution.py:189
  29.2 0.3 collective-permute-start.11
  29.5 0.5 %collective-permute-done.6.refs_6_ = bf16[32,1792]{1,0:T(8,128)(2,1)S(1)} collective-permute-done((bf16[32,1792]{1,0:T(8,128)(2,1)S(1)}, bf16[32,1792]{1,0:T(8,128)(2,1)S(1)}, u32[]{:S(2)}, u32[]{:S(2)}) %collective-permute-start.6) | collective-permute-done | bytes 114720 | tf_op jit(solution)/shard_map/ppermute | solution.py:189
  30.0 1.3 %shard_map.70.refs_0_ = f32[32,1792]{1,0:T(8,128)S(1)} custom-call(bf16[64,48]{1,0:T(8,128)(2,1)S(1)} %get-tuple-element.26.refs_3_.refs_0_, f32[64,128]{1,0:T(8,128)S(1)} %get-tuple-element.27.refs_4_.refs_1_, bf16[48,1024]{1,0:T(8,128)(2,1)S(1)} %get-tuple-element.28.refs_2_, bf16[48,1024]{1,0:T(8,128)(2,1)S(1)} %collective-permute-done.2.refs_1_.refs_3_, ...), custom_call_target="tpu_custom_call" | custom-call | flops 1 | bytes 1 | tf_op jit(solution)/shard_map/pallas_call | solution.py:24
  31.3 1.7 %collective-permute-done.12.refs_2_ = bf16[32,1792]{1,0:T(8,128)(2,1)S(1)} collective-permute-done((bf16[32,1792]{1,0:T(8,128)(2,1)S(1)}, bf16[32,1792]{1,0:T(8,128)(2,1)S(1)}, u32[]{:S(2)}, u32[]{:S(2)}) %collective-permute-start.12) | collective-permute-done | bytes 114720 | tf_op jit(solution)/shard_map/ppermute | solution.py:189
  33.0 1.0 %collective-permute-done.11.refs_1_ = bf16[32,1792]{1,0:T(8,128)(2,1)S(1)} collective-permute-done((bf16[32,1792]{1,0:T(8,128)(2,1)S(1)}, bf16[32,1792]{1,0:T(8,128)(2,1)S(1)}, u32[]{:S(2)}, u32[]{:S(2)}) %collective-permute-start.11) | collective-permute-done | bytes 114720 | tf_op jit(solution)/shard_map/ppermute | solution.py:189
  34.1 2.5 %collective-permute-start.13 = (bf16[16,1792]{1,0:T(8,128)(2,1)S(1)}, bf16[16,1792]{1,0:T(8,128)(2,1)S(1)}, u32[]{:S(2)}, u32[]{:S(2)}) collective-permute-start(bf16[16,1792]{1,0:T(8,128)(2,1)S(1)} %get-tuple-element.44), channel_id=1, source_target_pairs={{0,16},{2,18},{4,20},{6,22},{8,24},{10,26},{12,28},{14,30},{16,0},... | collective-permute-start | bytes 172040 | tf_op jit(solution)/shard_map/ppermute | solution.py:189
  36.6 2.6 %collective-permute-done.13.refs_1_ = bf16[16,1792]{1,0:T(8,128)(2,1)S(1)} collective-permute-done((bf16[16,1792]{1,0:T(8,128)(2,1)S(1)}, bf16[16,1792]{1,0:T(8,128)(2,1)S(1)}, u32[]{:S(2)}, u32[]{:S(2)}) %collective-permute-start.13) | collective-permute-done | bytes 57376 | tf_op jit(solution)/shard_map/ppermute | solution.py:189
  39.2 0.6 %shard_map.72 = bf16[16,1792]{1,0:T(8,128)(2,1)} custom-call(f32[16,1792]{1,0:T(8,128)S(1)} %get-tuple-element.43.refs_0_, bf16[16,1792]{1,0:T(8,128)(2,1)S(1)} %collective-permute-done.13.refs_1_), custom_call_target="tpu_custom_call" | custom-call | flops 1 | bytes 1 | tf_op jit(solution)/shard_map/pallas_call | solution.py:24
  (3 shorter events, 0.1 us)
Async XLA Ops:
  0.0 12.5 %collective-permute-start = (bf16[1792,1024]{1,0:T(8,128)(2,1)}, bf16[1792,1024]{1,0:T(8,128)(2,1)S(1)}, u32[]{:S(2)}, u32[]{:S(2)}) collective-permute-start(bf16[1792,1024]{1,0:T(8,128)(2,1)} %bitcast.8), channel_id=1, source_target_pairs={{0,2},{2,0},{4,6},{6,4},{8,10},{10,8},{12,14},{14,12},{16,18},{18,... | collective-permute-start | bytes 11010056 | tf_op jit(solution)/shard_map/ppermute | solution.py:189
  0.5 22.3 %collective-permute-start.3 = (bf16[1024,1792]{1,0:T(8,128)(2,1)}, bf16[1024,1792]{1,0:T(8,128)(2,1)S(1)}, u32[]{:S(2)}, u32[]{:S(2)}) collective-permute-start(bf16[1024,1792]{1,0:T(8,128)(2,1)} %bitcast.4), channel_id=1, source_target_pairs={{0,2},{2,0},{4,6},{6,4},{8,10},{10,8},{12,14},{14,12},{16,18},{18,... | collective-permute-start | bytes 11010056 | tf_op jit(solution)/shard_map/ppermute | solution.py:189
  1.5 7.0 %collective-permute-start.1 = (bf16[16,1920]{1,0:T(8,128)(2,1)S(1)}, bf16[16,1920]{1,0:T(8,128)(2,1)S(1)}, u32[]{:S(2)}, u32[]{:S(2)}) collective-permute-start(bf16[16,1920]{1,0:T(8,128)(2,1)S(1)} %shard_map.56.refs_0_), channel_id=1, source_target_pairs={{0,16},{2,18},{4,20},{6,22},{8,24},{10,26},{12,28},{14,30},{16,0},... | collective-permute-start | bytes 184328 | tf_op jit(solution)/shard_map/ppermute | solution.py:189
  8.5 7.6 %collective-permute-start.4 = (bf16[32,1920]{1,0:T(8,128)(2,1)S(1)}, bf16[32,1920]{1,0:T(8,128)(2,1)S(1)}, u32[]{:S(2)}, u32[]{:S(2)}) collective-permute-start(bf16[32,1920]{1,0:T(8,128)(2,1)S(1)} %shard_map.57.refs_2_), channel_id=1, source_target_pairs={{0,12},{2,14},{4,8},{6,10},{8,4},{10,6},{12,0},{14,2},{16,28},{18,... | collective-permute-start | bytes 368648 | tf_op jit(solution)/shard_map/ppermute | solution.py:189
  10.8 7.7 %collective-permute-start.8 = (bf16[32,1920]{1,0:T(8,128)(2,1)S(1)}, bf16[32,1920]{1,0:T(8,128)(2,1)S(1)}, u32[]{:S(2)}, u32[]{:S(2)}) collective-permute-start(bf16[32,1920]{1,0:T(8,128)(2,1)S(1)} %shard_map.57.refs_2_), channel_id=1, source_target_pairs={{0,8},{2,10},{4,12},{6,14},{8,0},{10,2},{12,4},{14,6},{16,24},{18,... | collective-permute-start | bytes 368648 | tf_op jit(solution)/shard_map/ppermute | solution.py:189
  12.5 6.0 %collective-permute-start.7 = (bf16[32,1920]{1,0:T(8,128)(2,1)S(1)}, bf16[32,1920]{1,0:T(8,128)(2,1)S(1)}, u32[]{:S(2)}, u32[]{:S(2)}) collective-permute-start(bf16[32,1920]{1,0:T(8,128)(2,1)S(1)} %shard_map.57.refs_2_), channel_id=1, source_target_pairs={{0,4},{2,6},{4,0},{6,2},{8,12},{10,14},{12,8},{14,10},{16,20},{18,... | collective-permute-start | bytes 368648 | tf_op jit(solution)/shard_map/ppermute | solution.py:189
  13.8 5.6 %collective-permute-start.2 = (bf16[48,1024]{1,0:T(8,128)(2,1)S(1)}, bf16[48,1024]{1,0:T(8,128)(2,1)S(1)}, u32[]{:S(2)}, u32[]{:S(2)}) collective-permute-start(bf16[48,1024]{1,0:T(8,128)(2,1)S(1)} %get-tuple-element.28.refs_2_), channel_id=1, source_target_pairs={{0,1},{1,0},{2,3},{3,2},{4,5},{5,4},{6,7},{7,6},{8,9},{9,8},{10,11... | collective-permute-start | bytes 294920 | tf_op jit(solution)/shard_map/ppermute | solution.py:225
  17.6 5.2 %collective-permute-start.5 = (bf16[48,1024]{1,0:T(8,128)(2,1)S(1)}, bf16[48,1024]{1,0:T(8,128)(2,1)S(1)}, u32[]{:S(2)}, u32[]{:S(2)}) collective-permute-start(bf16[48,1024]{1,0:T(8,128)(2,1)S(1)} %get-tuple-element.32.refs_2_.refs_5_), channel_id=1, source_target_pairs={{0,1},{1,0},{2,3},{3,2},{4,5},{5,4},{6,7},{7,6},{8,9},{9,8},{10,11... | collective-permute-start | bytes 294920 | tf_op jit(solution)/shard_map/ppermute | solution.py:225
  18.5 4.3 %copy-start = (bf16[1,1024,1792]{2,1,0:T(8,128)(2,1)S(1)}, bf16[1,1024,1792]{2,1,0:T(8,128)(2,1)}, u32[]{:S(2)}) copy-start(bf16[1,1024,1792]{2,1,0:T(8,128)(2,1)} %param.9) | copy-start | bytes 11010052
  19.4 7.3 %collective-permute-start.10 = (bf16[48,1024]{1,0:T(8,128)(2,1)S(1)}, bf16[48,1024]{1,0:T(8,128)(2,1)S(1)}, u32[]{:S(2)}, u32[]{:S(2)}) collective-permute-start(bf16[48,1024]{1,0:T(8,128)(2,1)S(1)} %shard_map.67.refs_2_), channel_id=1, source_target_pairs={{0,1},{1,0},{2,3},{3,2},{4,5},{5,4},{6,7},{7,6},{8,9},{9,8},{10,11... | collective-permute-start | bytes 294920 | tf_op jit(solution)/shard_map/ppermute | solution.py:225
  21.6 5.8 %collective-permute-start.9 = (bf16[48,1024]{1,0:T(8,128)(2,1)S(1)}, bf16[48,1024]{1,0:T(8,128)(2,1)S(1)}, u32[]{:S(2)}, u32[]{:S(2)}) collective-permute-start(bf16[48,1024]{1,0:T(8,128)(2,1)S(1)} %get-tuple-element.36.refs_2_), channel_id=1, source_target_pairs={{0,1},{1,0},{2,3},{3,2},{4,5},{5,4},{6,7},{7,6},{8,9},{9,8},{10,11... | collective-permute-start | bytes 294920 | tf_op jit(solution)/shard_map/ppermute | solution.py:225
  24.1 5.9 %collective-permute-start.6 = (bf16[32,1792]{1,0:T(8,128)(2,1)S(1)}, bf16[32,1792]{1,0:T(8,128)(2,1)S(1)}, u32[]{:S(2)}, u32[]{:S(2)}) collective-permute-start(bf16[32,1792]{1,0:T(8,128)(2,1)S(1)} %shard_map.62.refs_5_), channel_id=1, source_target_pairs={{0,12},{2,14},{4,8},{6,10},{8,4},{10,6},{12,0},{14,2},{16,28},{18,... | collective-permute-start | bytes 344072 | tf_op jit(solution)/shard_map/ppermute | solution.py:189
  28.1 4.9 %collective-permute-start.12 = (bf16[32,1792]{1,0:T(8,128)(2,1)S(1)}, bf16[32,1792]{1,0:T(8,128)(2,1)S(1)}, u32[]{:S(2)}, u32[]{:S(2)}) collective-permute-start(bf16[32,1792]{1,0:T(8,128)(2,1)S(1)} %get-tuple-element.42), channel_id=1, source_target_pairs={{0,8},{2,10},{4,12},{6,14},{8,0},{10,2},{12,4},{14,6},{16,24},{18,... | collective-permute-start | bytes 344072 | tf_op jit(solution)/shard_map/ppermute | solution.py:189
  29.2 4.8 %collective-permute-start.11 = (bf16[32,1792]{1,0:T(8,128)(2,1)S(1)}, bf16[32,1792]{1,0:T(8,128)(2,1)S(1)}, u32[]{:S(2)}, u32[]{:S(2)}) collective-permute-start(bf16[32,1792]{1,0:T(8,128)(2,1)S(1)} %get-tuple-element.41.refs_7_), channel_id=1, source_target_pairs={{0,4},{2,6},{4,0},{6,2},{8,12},{10,14},{12,8},{14,10},{16,20},{18,... | collective-permute-start | bytes 344072 | tf_op jit(solution)/shard_map/ppermute | solution.py:189
  34.1 5.1 %collective-permute-start.13 = (bf16[16,1792]{1,0:T(8,128)(2,1)S(1)}, bf16[16,1792]{1,0:T(8,128)(2,1)S(1)}, u32[]{:S(2)}, u32[]{:S(2)}) collective-permute-start(bf16[16,1792]{1,0:T(8,128)(2,1)S(1)} %get-tuple-element.44), channel_id=1, source_target_pairs={{0,16},{2,18},{4,20},{6,22},{8,24},{10,26},{12,28},{14,30},{16,0},... | collective-permute-start | bytes 172040 | tf_op jit(solution)/shard_map/ppermute | solution.py:189

commit v6 on v5

--- a/solution.py
+++ b/solution.py
@@ -105,10 +105,13 @@
     return jnp.sum(jnp.where(mine, lined, 0.0), axis=0, keepdims=True)
 
 
+def slot_of(routing, rows, cap):
+    rank = routed(routing, rows, 3).astype(jnp.int32)
+    return jnp.where(rank > 0, iota((1, LANES), 1) // rows * cap + rank - 1, -1)
+
+
 def selection(routing, rows, cap):
-    rank = routed(routing, rows, 3).astype(jnp.int32)
-    at = iota((1, LANES), 1) // rows * cap + rank - 1
-    hit = iota((LANES // rows * cap, LANES), 0) == jnp.where(rank > 0, at, -1)
+    hit = iota((LANES // rows * cap, LANES), 0) == slot_of(routing, rows, cap)
     return jnp.where(hit, 1.0, 0.0)
 
 
@@ -137,12 +140,14 @@
         pre_ref[:, i * step : (i + 1) * step] = dot(sel, jnp.concatenate(part, axis=0)).astype(BF16)
 
 
-def plan_kernel(rows, cap, routing_ref, turned_ref, gate_ref):
-    routing = routing_ref[...]
-    tokens, slots = turned_ref.shape
-    turned_ref[...] = jnp.transpose(selection(routing, rows, cap))[:tokens, :slots].astype(BF16)
-    gate = routed(routing, rows, 0) + routed(routing, rows, 1) + routed(routing, rows, 2)
-    gate_ref[...] = jnp.transpose(jnp.broadcast_to(gate, (LANES, LANES)))[:tokens]
+def plan_kernel(rows, cap, *refs):
+    count = len(refs) // 3
+    for routing_ref, turned_ref, gate_ref in zip(refs[:count], refs[count::2], refs[count + 1 :: 2]):
+        routing = routing_ref[...]
+        tokens, slots = turned_ref.shape
+        turned_ref[...] = jnp.transpose(selection(routing, rows, cap))[:tokens, :slots].astype(BF16)
+        gate = routed(routing, rows, 0) + routed(routing, rows, 1) + routed(routing, rows, 2)
+        gate_ref[...] = jnp.transpose(jnp.broadcast_to(gate, (LANES, LANES)))[:tokens]
 
 
 def down_kernel(experts, terms, turned_ref, gate_ref, a_ref, b_ref, *refs):
@@ -217,12 +222,14 @@
         )
         if before:
             pre = tie(pre, *before)
-        plan = call(
-            functools.partial(plan_kernel, rows, cap),
-            (shape((count * rows, count * cap), BF16), shape((count * rows, LANES), F32)),
-            (routing,),
-        )
-        return (*plan, pre, lax.ppermute(pre, "rep", [(0, 1), (1, 0)]))
+        return count, routing, pre, lax.ppermute(pre, "rep", [(0, 1), (1, 0)])
+
+    def planned(*steps):
+        outs = []
+        for count, *_ in steps:
+            outs += [shape((count * rows, count * cap), BF16), shape((count * rows, LANES), F32)]
+        made = call(functools.partial(plan_kernel, rows, cap), tuple(outs), tuple(step[1] for step in steps))
+        return [(*made[2 * i : 2 * i + 2], *step[2:]) for i, step in enumerate(steps)]
 
     def lowered(offsets, step, outs, *terms, after=()):
         return call(
@@ -233,9 +240,9 @@
         )
 
     both, single = shape((2 * rows, width), F32), shape((2 * rows, width), BF16)
-    here = raised((0, 1), blocks[:1])
-    corner = raised((0, 1), blocks[3:], (), here[:2])
-    there = [raised((i,), blocks[1:3], here[-1:] * (1 - i), corner[:3] * (1 - i)) for i in (0, 1)]
+    (here,) = planned(raised((0, 1), blocks[:1]))
+    (corner,) = planned(raised((0, 1), blocks[3:], (), here[2:3]))
+    there = planned(*(raised((i,), blocks[1:3], here[-1:] * i, corner[:3] * (1 - i)) for i in (0, 1)))
     diagonal = lowered((0, 1), corner, single)
     first = lowered((0,), there[0], shape((4 * rows, width), F32), after=(diagonal,))
     sends = lowered((1,), there[1], (single,) * 2, first)

time: 40 us -> 39.3 us (0.982)
  waiting for transfers between devices: 6.8 us -> 5.51 us
  starting transfers between devices: 20.1 us -> 20.9 us
    ppermute x10, waiting for transfers between devices: 6.65 us -> 5.41 us  [swap(): return lax.ppermute(x, 'ep', [(i, i ^ distance) for i in range(n)])]
    ppermute x10, starting transfers between devices: 15 us -> 15.5 us  [swap(): return lax.ppermute(x, 'ep', [(i, i ^ distance) for i in range(n)])]
    pallas_call x18 -> x17, Pallas kernels: 12.8 us -> 12.6 us  [call(): pl.pallas_call(body, out_shape=outs, in_specs=specs + [pl.BlockSpec(memor...]
where the time goes in v6:
time: 39.3 us; the launch traced here: 39.2 us
  starting transfers between devices  20.9 us (53%)
  Pallas kernels  12.6 us (32%)
  waiting for transfers between devices  5.51 us (14%)
    ppermute x10, starting transfers between devices, swap(): return lax.ppermute(x, 'ep', [(i, i ^ distance) for i in range(n)])  15.5 us
    pallas_call x17, Pallas kernels, call(): pl.pallas_call(body, out_shape=outs, in_specs=specs + [pl.BlockSpec(memor...  12.6 us
    ppermute x10, waiting for transfers between devices, swap(): return lax.ppermute(x, 'ep', [(i, i ^ distance) for i in range(n)])  5.41 us
    ppermute x4, starting transfers between devices, raised(): return (count, routing, pre, lax.ppermute(pre, 'rep', [(0, 1), (1, 0)]))  5.37 us
  transfers between devices with their start and end apart: 14, of which 6 were waited for; matrix products, arithmetic and copies ran while one was open for 0% of the time, Pallas kernels for 30%

profile of v6, /device:TPU:0, one launch (start us, length us, event | category | flops | bytes accessed | tf_op | source)
XLA Modules:
  0.0 39.2 jit_solution(3566782246936437531)
XLA Ops:
  0.0 0.5 %collective-permute-start = (bf16[1792,1024]{1,0:T(8,128)(2,1)}, bf16[1792,1024]{1,0:T(8,128)(2,1)S(1)}, u32[]{:S(2)}, u32[]{:S(2)}) collective-permute-start(bf16[1792,1024]{1,0:T(8,128)(2,1)} %bitcast.8), channel_id=1, source_target_pairs={{0,2},{2,0},{4,6},{6,4},{8,10},{10,8},{12,14},{14,12},{16,18},{18,... | collective-permute-start | bytes 11010056 | tf_op jit(solution)/shard_map/ppermute | solution.py:194
  0.5 0.1 collective-permute-start.3
  0.5 1.0 %shard_map.56.refs_0_ = bf16[16,1920]{1,0:T(8,128)(2,1)S(1)} custom-call(bf16[16,1792]{1,0:T(8,128)(2,1)} %refs_0_.1, s32[8,16]{1,0:T(8,128)} %bitcast.10, f32[8,16]{1,0:T(8,128)} %bitcast.11), custom_call_target="tpu_custom_call" | custom-call | flops 1 | bytes 1 | tf_op jit(solution)/shard_map/pallas_call | solution.py:24
  1.5 4.1 %collective-permute-start.1 = (bf16[16,1920]{1,0:T(8,128)(2,1)S(1)}, bf16[16,1920]{1,0:T(8,128)(2,1)S(1)}, u32[]{:S(2)}, u32[]{:S(2)}) collective-permute-start(bf16[16,1920]{1,0:T(8,128)(2,1)S(1)} %shard_map.56.refs_0_), channel_id=1, source_target_pairs={{0,16},{2,18},{4,20},{6,22},{8,24},{10,26},{12,28},{14,30},{16,0},... | collective-permute-start | bytes 184328 | tf_op jit(solution)/shard_map/ppermute | solution.py:194
  5.6 2.1 %shard_map.55.refs_2_.refs_0_ = bf16[1792,1024]{1,0:T(8,128)(2,1)S(1)} custom-call(bf16[1792,1024]{1,0:T(8,128)(2,1)} %bitcast.9), custom_call_target="tpu_custom_call" | custom-call | flops 1 | bytes 1 | tf_op jit(solution)/shard_map/pallas_call | solution.py:24
  7.7 0.8 %collective-permute-done.1.refs_1_ = bf16[16,1920]{1,0:T(8,128)(2,1)S(1)} collective-permute-done((bf16[16,1920]{1,0:T(8,128)(2,1)S(1)}, bf16[16,1920]{1,0:T(8,128)(2,1)S(1)}, u32[]{:S(2)}, u32[]{:S(2)}) %collective-permute-start.1) | collective-permute-done | bytes 61472 | tf_op jit(solution)/shard_map/ppermute | solution.py:194
  8.5 2.4 %collective-permute-start.4 = (bf16[32,1920]{1,0:T(8,128)(2,1)S(1)}, bf16[32,1920]{1,0:T(8,128)(2,1)S(1)}, u32[]{:S(2)}, u32[]{:S(2)}) collective-permute-start(bf16[32,1920]{1,0:T(8,128)(2,1)S(1)} %shard_map.57.refs_2_), channel_id=1, source_target_pairs={{0,12},{2,14},{4,8},{6,10},{8,4},{10,6},{12,0},{14,2},{16,28},{18,... | collective-permute-start | bytes 368648 | tf_op jit(solution)/shard_map/ppermute | solution.py:194
  10.8 1.7 %collective-permute-start.8 = (bf16[32,1920]{1,0:T(8,128)(2,1)S(1)}, bf16[32,1920]{1,0:T(8,128)(2,1)S(1)}, u32[]{:S(2)}, u32[]{:S(2)}) collective-permute-start(bf16[32,1920]{1,0:T(8,128)(2,1)S(1)} %shard_map.57.refs_2_), channel_id=1, source_target_pairs={{0,8},{2,10},{4,12},{6,14},{8,0},{10,2},{12,4},{14,6},{16,24},{18,... | collective-permute-start | bytes 368648 | tf_op jit(solution)/shard_map/ppermute | solution.py:194
  12.5 0.0 collective-permute-start.7
  12.5 0.0 collective-permute-done.refs_1_.refs_0_
  12.5 1.3 %shard_map.58 = (bf16[48,1024]{1,0:T(8,128)(2,1)S(1)}, f32[8,128]{1,0:T(8,128)S(1)}) custom-call(bf16[1792,1024]{1,0:T(8,128)(2,1)S(1)} %shard_map.55.refs_2_.refs_0_, bf16[1792,1024]{1,0:T(8,128)(2,1)S(1)} %collective-permute-done.refs_1_.refs_0_, bf16[32,1920]{1,0:T(8,128)(2,1)S(1)} %shard_map.57.refs_2_), custom_call_target="tpu_custom_call" | custom-call | flops 1 | bytes 1 | tf_op jit(solution)/shard_map/pallas_call | solution.py:24
  13.8 2.1 %collective-permute-start.2 = (bf16[48,1024]{1,0:T(8,128)(2,1)S(1)}, bf16[48,1024]{1,0:T(8,128)(2,1)S(1)}, u32[]{:S(2)}, u32[]{:S(2)}) collective-permute-start(bf16[48,1024]{1,0:T(8,128)(2,1)S(1)} %get-tuple-element.28.refs_3_.refs_2_), channel_id=1, source_target_pairs={{0,1},{1,0},{2,3},{3,2},{4,5},{5,4},{6,7},{7,6},{8,9},{9,8},{10,11... | collective-permute-start | bytes 294920 | tf_op jit(solution)/shard_map/ppermute | solution.py:225
  15.9 0.0 collective-permute-done.4.refs_2_
  15.9 1.3 %shard_map.60 = (bf16[48,1024]{1,0:T(8,128)(2,1)S(1)}, f32[8,128]{1,0:T(8,128)S(1)}) custom-call(bf16[1792,1024]{1,0:T(8,128)(2,1)S(1)} %shard_map.55.refs_2_.refs_0_, bf16[1792,1024]{1,0:T(8,128)(2,1)S(1)} %collective-permute-done.refs_1_.refs_0_, bf16[32,1920]{1,0:T(8,128)(2,1)S(1)} %collective-permute-done.4.refs_2_, ...), custom_call_target="tpu_custom_call" | custom-call | flops 1 | bytes 1 | tf_op jit(solution)/shard_map/pallas_call | solution.py:24
  17.1 0.2 shard_map.61
  17.4 1.1 %collective-permute-start.5 = (bf16[48,1024]{1,0:T(8,128)(2,1)S(1)}, bf16[48,1024]{1,0:T(8,128)(2,1)S(1)}, u32[]{:S(2)}, u32[]{:S(2)}) collective-permute-start(bf16[48,1024]{1,0:T(8,128)(2,1)S(1)} %get-tuple-element.32.refs_2_.refs_5_), channel_id=1, source_target_pairs={{0,1},{1,0},{2,3},{3,2},{4,5},{5,4},{6,7},{7,6},{8,9},{9,8},{10,11... | collective-permute-start | bytes 294920 | tf_op jit(solution)/shard_map/ppermute | solution.py:225
  18.5 0.0 collective-permute-done.8.refs_2_
  18.5 0.0 collective-permute-done.7.refs_1_
  18.5 0.0 copy-start
  18.5 0.8 %shard_map.63 = (bf16[48,1024]{1,0:T(8,128)(2,1)S(1)}, f32[8,128]{1,0:T(8,128)S(1)}) custom-call(bf16[1792,1024]{1,0:T(8,128)(2,1)S(1)} %shard_map.55.refs_2_.refs_0_, bf16[32,1920]{1,0:T(8,128)(2,1)S(1)} %collective-permute-done.7.refs_1_, bf16[32,1920]{1,0:T(8,128)(2,1)S(1)} %collective-permute-done.8.refs_2_, ...), custom_call_target="tpu_custom_call" | custom-call | flops 1 | bytes 1 | tf_op jit(solution)/shard_map/pallas_call | solution.py:24
  19.3 1.0 %collective-permute-start.10 = (bf16[48,1024]{1,0:T(8,128)(2,1)S(1)}, bf16[48,1024]{1,0:T(8,128)(2,1)S(1)}, u32[]{:S(2)}, u32[]{:S(2)}) collective-permute-start(bf16[48,1024]{1,0:T(8,128)(2,1)S(1)} %get-tuple-element.40.refs_2_), channel_id=1, source_target_pairs={{0,1},{1,0},{2,3},{3,2},{4,5},{5,4},{6,7},{7,6},{8,9},{9,8},{10,11... | collective-permute-start | bytes 294920 | tf_op jit(solution)/shard_map/ppermute | solution.py:225
  20.3 0.8 %shard_map.64 = (bf16[48,1024]{1,0:T(8,128)(2,1)S(1)}, f32[8,128]{1,0:T(8,128)S(1)}) custom-call(bf16[1792,1024]{1,0:T(8,128)(2,1)S(1)} %collective-permute-done.refs_1_.refs_0_, bf16[32,1920]{1,0:T(8,128)(2,1)S(1)} %collective-permute-done.7.refs_1_, bf16[32,1920]{1,0:T(8,128)(2,1)S(1)} %collective-permute-done.8.refs_2_), custom_call_target="tpu_custom_call" | custom-call | flops 1 | bytes 1 | tf_op jit(solution)/shard_map/pallas_call | solution.py:24
  21.1 0.0 collective-permute-done.2.refs_1_.refs_3_
  21.1 1.1 %collective-permute-start.9 = (bf16[48,1024]{1,0:T(8,128)(2,1)S(1)}, bf16[48,1024]{1,0:T(8,128)(2,1)S(1)}, u32[]{:S(2)}, u32[]{:S(2)}) collective-permute-start(bf16[48,1024]{1,0:T(8,128)(2,1)S(1)} %shard_map.66.refs_2_), channel_id=1, source_target_pairs={{0,1},{1,0},{2,3},{3,2},{4,5},{5,4},{6,7},{7,6},{8,9},{9,8},{10,11... | collective-permute-start | bytes 294920 | tf_op jit(solution)/shard_map/ppermute | solution.py:225
  22.3 0.3 shard_map.65
  22.5 0.0 collective-permute-done.3.refs_5_.refs_4_
  22.5 0.1 collective-permute-done.5.refs_3_
  22.6 0.0 copy-done
  22.6 1.3 %shard_map.62.refs_5_ = bf16[32,1792]{1,0:T(8,128)(2,1)S(1)} custom-call(bf16[64,48]{1,0:T(8,128)(2,1)S(1)} %get-tuple-element.30.refs_0_.refs_3_, f32[64,128]{1,0:T(8,128)S(1)} %get-tuple-element.31.refs_1_.refs_4_, bf16[48,1024]{1,0:T(8,128)(2,1)S(1)} %get-tuple-element.32.refs_2_.refs_5_, bf16[48,1024]{1,0:T(8,128)(2,1)S(1)} %collective-permute-done.5.refs_3_, ...), custom_call_target="tpu_custom_call" | custom-call | flops 1 | bytes 1 | tf_op jit(solution)/shard_map/pallas_call | solution.py:24
  23.9 2.5 %collective-permute-start.6 = (bf16[32,1792]{1,0:T(8,128)(2,1)S(1)}, bf16[32,1792]{1,0:T(8,128)(2,1)S(1)}, u32[]{:S(2)}, u32[]{:S(2)}) collective-permute-start(bf16[32,1792]{1,0:T(8,128)(2,1)S(1)} %shard_map.62.refs_5_), channel_id=1, source_target_pairs={{0,12},{2,14},{4,8},{6,10},{8,4},{10,6},{12,0},{14,2},{16,28},{18,... | collective-permute-start | bytes 344072 | tf_op jit(solution)/shard_map/ppermute | solution.py:194
  26.4 0.0 collective-permute-done.10.refs_3_
  26.4 0.7 %shard_map.67.refs_5_ = f32[64,1792]{1,0:T(8,128)S(1)} custom-call(bf16[64,48]{1,0:T(8,128)(2,1)S(1)} %get-tuple-element.38.refs_0_, f32[64,128]{1,0:T(8,128)S(1)} %get-tuple-element.39.refs_1_, bf16[48,1024]{1,0:T(8,128)(2,1)S(1)} %get-tuple-element.40.refs_2_, bf16[48,1024]{1,0:T(8,128)(2,1)S(1)} %collective-permute-done.10.refs_3_, ...), custom_call_target="tpu_custom_call" | custom-call | flops 1 | bytes 1 | tf_op jit(solution)/shard_map/pallas_call | solution.py:24
  27.2 0.0 collective-permute-done.9.refs_3_
  27.2 0.8 %shard_map.68 = (bf16[32,1792]{1,0:T(8,128)(2,1)S(1)}, bf16[32,1792]{1,0:T(8,128)(2,1)S(1)}) custom-call(bf16[64,48]{1,0:T(8,128)(2,1)S(1)} %get-tuple-element.35.refs_0_, f32[64,128]{1,0:T(8,128)S(1)} %get-tuple-element.36.refs_1_, bf16[48,1024]{1,0:T(8,128)(2,1)S(1)} %shard_map.66.refs_2_, bf16[48,1024]{1,0:T(8,128)(2,1)S(1)} %collective-permute-done.9.refs_3_, ...), custom_call_target="tpu_custom_call" | custom-call | flops 1 | bytes 1 | tf_op jit(solution)/shard_map/pallas_call | solution.py:24
  27.9 0.5 %collective-permute-start.12 = (bf16[32,1792]{1,0:T(8,128)(2,1)S(1)}, bf16[32,1792]{1,0:T(8,128)(2,1)S(1)}, u32[]{:S(2)}, u32[]{:S(2)}) collective-permute-start(bf16[32,1792]{1,0:T(8,128)(2,1)S(1)} %get-tuple-element.42), channel_id=1, source_target_pairs={{0,8},{2,10},{4,12},{6,14},{8,0},{10,2},{12,4},{14,6},{16,24},{18,... | collective-permute-start | bytes 344072 | tf_op jit(solution)/shard_map/ppermute | solution.py:194
  28.5 0.8 %collective-permute-start.11 = (bf16[32,1792]{1,0:T(8,128)(2,1)S(1)}, bf16[32,1792]{1,0:T(8,128)(2,1)S(1)}, u32[]{:S(2)}, u32[]{:S(2)}) collective-permute-start(bf16[32,1792]{1,0:T(8,128)(2,1)S(1)} %get-tuple-element.41.refs_7_), channel_id=1, source_target_pairs={{0,4},{2,6},{4,0},{6,2},{8,12},{10,14},{12,8},{14,10},{16,20},{18,... | collective-permute-start | bytes 344072 | tf_op jit(solution)/shard_map/ppermute | solution.py:194
  29.3 0.2 shard_map.59
  29.5 0.3 collective-permute-done.6.refs_6_
  29.8 1.3 %shard_map.69.refs_0_ = f32[32,1792]{1,0:T(8,128)S(1)} custom-call(bf16[64,48]{1,0:T(8,128)(2,1)S(1)} %get-tuple-element.26.refs_0_, f32[64,128]{1,0:T(8,128)S(1)} %get-tuple-element.27.refs_1_, bf16[48,1024]{1,0:T(8,128)(2,1)S(1)} %get-tuple-element.28.refs_3_.refs_2_, bf16[48,1024]{1,0:T(8,128)(2,1)S(1)} %collective-permute-done.2.refs_1_.refs_3_, ...), custom_call_target="tpu_custom_call" | custom-call | flops 1 | bytes 1 | tf_op jit(solution)/shard_map/pallas_call | solution.py:24
  31.1 1.7 %collective-permute-done.12.refs_2_ = bf16[32,1792]{1,0:T(8,128)(2,1)S(1)} collective-permute-done((bf16[32,1792]{1,0:T(8,128)(2,1)S(1)}, bf16[32,1792]{1,0:T(8,128)(2,1)S(1)}, u32[]{:S(2)}, u32[]{:S(2)}) %collective-permute-start.12) | collective-permute-done | bytes 114720 | tf_op jit(solution)/shard_map/ppermute | solution.py:194
  32.8 0.5 %collective-permute-done.11.refs_1_ = bf16[32,1792]{1,0:T(8,128)(2,1)S(1)} collective-permute-done((bf16[32,1792]{1,0:T(8,128)(2,1)S(1)}, bf16[32,1792]{1,0:T(8,128)(2,1)S(1)}, u32[]{:S(2)}, u32[]{:S(2)}) %collective-permute-start.11) | collective-permute-done | bytes 114720 | tf_op jit(solution)/shard_map/ppermute | solution.py:194
  33.3 3.1 %collective-permute-start.13 = (bf16[16,1792]{1,0:T(8,128)(2,1)S(1)}, bf16[16,1792]{1,0:T(8,128)(2,1)S(1)}, u32[]{:S(2)}, u32[]{:S(2)}) collective-permute-start(bf16[16,1792]{1,0:T(8,128)(2,1)S(1)} %get-tuple-element.44), channel_id=1, source_target_pairs={{0,16},{2,18},{4,20},{6,22},{8,24},{10,26},{12,28},{14,30},{16,0},... | collective-permute-start | bytes 172040 | tf_op jit(solution)/shard_map/ppermute | solution.py:194
  36.4 2.2 %collective-permute-done.13.refs_1_ = bf16[16,1792]{1,0:T(8,128)(2,1)S(1)} collective-permute-done((bf16[16,1792]{1,0:T(8,128)(2,1)S(1)}, bf16[16,1792]{1,0:T(8,128)(2,1)S(1)}, u32[]{:S(2)}, u32[]{:S(2)}) %collective-permute-start.13) | collective-permute-done | bytes 57376 | tf_op jit(solution)/shard_map/ppermute | solution.py:194
  38.5 0.6 %shard_map.71 = bf16[16,1792]{1,0:T(8,128)(2,1)} custom-call(f32[16,1792]{1,0:T(8,128)S(1)} %get-tuple-element.43.refs_0_, bf16[16,1792]{1,0:T(8,128)(2,1)S(1)} %collective-permute-done.13.refs_1_), custom_call_target="tpu_custom_call" | custom-call | flops 1 | bytes 1 | tf_op jit(solution)/shard_map/pallas_call | solution.py:24
  (3 shorter events, 0.1 us)
Async XLA Ops:
  0.0 12.5 %collective-permute-start = (bf16[1792,1024]{1,0:T(8,128)(2,1)}, bf16[1792,1024]{1,0:T(8,128)(2,1)S(1)}, u32[]{:S(2)}, u32[]{:S(2)}) collective-permute-start(bf16[1792,1024]{1,0:T(8,128)(2,1)} %bitcast.8), channel_id=1, source_target_pairs={{0,2},{2,0},{4,6},{6,4},{8,10},{10,8},{12,14},{14,12},{16,18},{18,... | collective-permute-start | bytes 11010056 | tf_op jit(solution)/shard_map/ppermute | solution.py:194
  0.5 22.1 %collective-permute-start.3 = (bf16[1024,1792]{1,0:T(8,128)(2,1)}, bf16[1024,1792]{1,0:T(8,128)(2,1)S(1)}, u32[]{:S(2)}, u32[]{:S(2)}) collective-permute-start(bf16[1024,1792]{1,0:T(8,128)(2,1)} %bitcast.4), channel_id=1, source_target_pairs={{0,2},{2,0},{4,6},{6,4},{8,10},{10,8},{12,14},{14,12},{16,18},{18,... | collective-permute-start | bytes 11010056 | tf_op jit(solution)/shard_map/ppermute | solution.py:194
  1.5 7.0 %collective-permute-start.1 = (bf16[16,1920]{1,0:T(8,128)(2,1)S(1)}, bf16[16,1920]{1,0:T(8,128)(2,1)S(1)}, u32[]{:S(2)}, u32[]{:S(2)}) collective-permute-start(bf16[16,1920]{1,0:T(8,128)(2,1)S(1)} %shard_map.56.refs_0_), channel_id=1, source_target_pairs={{0,16},{2,18},{4,20},{6,22},{8,24},{10,26},{12,28},{14,30},{16,0},... | collective-permute-start | bytes 184328 | tf_op jit(solution)/shard_map/ppermute | solution.py:194
  8.5 7.4 %collective-permute-start.4 = (bf16[32,1920]{1,0:T(8,128)(2,1)S(1)}, bf16[32,1920]{1,0:T(8,128)(2,1)S(1)}, u32[]{:S(2)}, u32[]{:S(2)}) collective-permute-start(bf16[32,1920]{1,0:T(8,128)(2,1)S(1)} %shard_map.57.refs_2_), channel_id=1, source_target_pairs={{0,12},{2,14},{4,8},{6,10},{8,4},{10,6},{12,0},{14,2},{16,28},{18,... | collective-permute-start | bytes 368648 | tf_op jit(solution)/shard_map/ppermute | solution.py:194
  10.8 7.7 %collective-permute-start.8 = (bf16[32,1920]{1,0:T(8,128)(2,1)S(1)}, bf16[32,1920]{1,0:T(8,128)(2,1)S(1)}, u32[]{:S(2)}, u32[]{:S(2)}) collective-permute-start(bf16[32,1920]{1,0:T(8,128)(2,1)S(1)} %shard_map.57.refs_2_), channel_id=1, source_target_pairs={{0,8},{2,10},{4,12},{6,14},{8,0},{10,2},{12,4},{14,6},{16,24},{18,... | collective-permute-start | bytes 368648 | tf_op jit(solution)/shard_map/ppermute | solution.py:194
  12.5 6.0 %collective-permute-start.7 = (bf16[32,1920]{1,0:T(8,128)(2,1)S(1)}, bf16[32,1920]{1,0:T(8,128)(2,1)S(1)}, u32[]{:S(2)}, u32[]{:S(2)}) collective-permute-start(bf16[32,1920]{1,0:T(8,128)(2,1)S(1)} %shard_map.57.refs_2_), channel_id=1, source_target_pairs={{0,4},{2,6},{4,0},{6,2},{8,12},{10,14},{12,8},{14,10},{16,20},{18,... | collective-permute-start | bytes 368648 | tf_op jit(solution)/shard_map/ppermute | solution.py:194
  13.8 7.3 %collective-permute-start.2 = (bf16[48,1024]{1,0:T(8,128)(2,1)S(1)}, bf16[48,1024]{1,0:T(8,128)(2,1)S(1)}, u32[]{:S(2)}, u32[]{:S(2)}) collective-permute-start(bf16[48,1024]{1,0:T(8,128)(2,1)S(1)} %get-tuple-element.28.refs_3_.refs_2_), channel_id=1, source_target_pairs={{0,1},{1,0},{2,3},{3,2},{4,5},{5,4},{6,7},{7,6},{8,9},{9,8},{10,11... | collective-permute-start | bytes 294920 | tf_op jit(solution)/shard_map/ppermute | solution.py:225
  17.4 5.2 %collective-permute-start.5 = (bf16[48,1024]{1,0:T(8,128)(2,1)S(1)}, bf16[48,1024]{1,0:T(8,128)(2,1)S(1)}, u32[]{:S(2)}, u32[]{:S(2)}) collective-permute-start(bf16[48,1024]{1,0:T(8,128)(2,1)S(1)} %get-tuple-element.32.refs_2_.refs_5_), channel_id=1, source_target_pairs={{0,1},{1,0},{2,3},{3,2},{4,5},{5,4},{6,7},{7,6},{8,9},{9,8},{10,11... | collective-permute-start | bytes 294920 | tf_op jit(solution)/shard_map/ppermute | solution.py:225
  18.5 4.1 %copy-start = (bf16[1,1024,1792]{2,1,0:T(8,128)(2,1)S(1)}, bf16[1,1024,1792]{2,1,0:T(8,128)(2,1)}, u32[]{:S(2)}) copy-start(bf16[1,1024,1792]{2,1,0:T(8,128)(2,1)} %param.9) | copy-start | bytes 11010052
  19.3 7.1 %collective-permute-start.10 = (bf16[48,1024]{1,0:T(8,128)(2,1)S(1)}, bf16[48,1024]{1,0:T(8,128)(2,1)S(1)}, u32[]{:S(2)}, u32[]{:S(2)}) collective-permute-start(bf16[48,1024]{1,0:T(8,128)(2,1)S(1)} %get-tuple-element.40.refs_2_), channel_id=1, source_target_pairs={{0,1},{1,0},{2,3},{3,2},{4,5},{5,4},{6,7},{7,6},{8,9},{9,8},{10,11... | collective-permute-start | bytes 294920 | tf_op jit(solution)/shard_map/ppermute | solution.py:225
  21.1 6.1 %collective-permute-start.9 = (bf16[48,1024]{1,0:T(8,128)(2,1)S(1)}, bf16[48,1024]{1,0:T(8,128)(2,1)S(1)}, u32[]{:S(2)}, u32[]{:S(2)}) collective-permute-start(bf16[48,1024]{1,0:T(8,128)(2,1)S(1)} %shard_map.66.refs_2_), channel_id=1, source_target_pairs={{0,1},{1,0},{2,3},{3,2},{4,5},{5,4},{6,7},{7,6},{8,9},{9,8},{10,11... | collective-permute-start | bytes 294920 | tf_op jit(solution)/shard_map/ppermute | solution.py:225
  23.9 5.9 %collective-permute-start.6 = (bf16[32,1792]{1,0:T(8,128)(2,1)S(1)}, bf16[32,1792]{1,0:T(8,128)(2,1)S(1)}, u32[]{:S(2)}, u32[]{:S(2)}) collective-permute-start(bf16[32,1792]{1,0:T(8,128)(2,1)S(1)} %shard_map.62.refs_5_), channel_id=1, source_target_pairs={{0,12},{2,14},{4,8},{6,10},{8,4},{10,6},{12,0},{14,2},{16,28},{18,... | collective-permute-start | bytes 344072 | tf_op jit(solution)/shard_map/ppermute | solution.py:194
  27.9 4.9 %collective-permute-start.12 = (bf16[32,1792]{1,0:T(8,128)(2,1)S(1)}, bf16[32,1792]{1,0:T(8,128)(2,1)S(1)}, u32[]{:S(2)}, u32[]{:S(2)}) collective-permute-start(bf16[32,1792]{1,0:T(8,128)(2,1)S(1)} %get-tuple-element.42), channel_id=1, source_target_pairs={{0,8},{2,10},{4,12},{6,14},{8,0},{10,2},{12,4},{14,6},{16,24},{18,... | collective-permute-start | bytes 344072 | tf_op jit(solution)/shard_map/ppermute | solution.py:194
  28.5 4.8 %collective-permute-start.11 = (bf16[32,1792]{1,0:T(8,128)(2,1)S(1)}, bf16[32,1792]{1,0:T(8,128)(2,1)S(1)}, u32[]{:S(2)}, u32[]{:S(2)}) collective-permute-start(bf16[32,1792]{1,0:T(8,128)(2,1)S(1)} %get-tuple-element.41.refs_7_), channel_id=1, source_target_pairs={{0,4},{2,6},{4,0},{6,2},{8,12},{10,14},{12,8},{14,10},{16,20},{18,... | collective-permute-start | bytes 344072 | tf_op jit(solution)/shard_map/ppermute | solution.py:194
  33.3 5.2 %collective-permute-start.13 = (bf16[16,1792]{1,0:T(8,128)(2,1)S(1)}, bf16[16,1792]{1,0:T(8,128)(2,1)S(1)}, u32[]{:S(2)}, u32[]{:S(2)}) collective-permute-start(bf16[16,1792]{1,0:T(8,128)(2,1)S(1)} %get-tuple-element.44), channel_id=1, source_target_pairs={{0,16},{2,18},{4,20},{6,22},{8,24},{10,26},{12,28},{14,30},{16,0},... | collective-permute-start | bytes 172040 | tf_op jit(solution)/shard_map/ppermute | solution.py:194

commit v7 on v6

--- a/solution.py
+++ b/solution.py
@@ -57,23 +57,26 @@
         copy.start()
     copies[0].wait()
     copies[1].wait()
-    expert = iota((rows, rows), 0)
-    gate = jnp.zeros((rows, rows), F32)
-    mask = jnp.zeros((rows, rows), F32)
+    gates = gates_ref[...]
+    hi = gates.astype(BF16).astype(F32)
+    mid = (gates - hi).astype(BF16).astype(F32)
+    low = gates - hi - mid
+    terms = jnp.concatenate([ids_ref[...].astype(F32), hi, mid, low], axis=0).astype(BF16)
+    tiles = dot(terms, (iota((rows, LANES), 0) == iota((rows, LANES), 1) % rows).astype(BF16))
+    ids, hi, mid, low = (tiles[i * top : (i + 1) * top] for i in range(4))
+    group = iota((1, LANES), 1) // rows
+    value = jnp.where(group == 0, hi, jnp.where(group == 1, mid, low))
+    expert = iota((rows, LANES), 0).astype(F32)
+    gate = jnp.zeros((rows, LANES), F32)
+    mask = jnp.zeros((rows, LANES), F32)
     for k in range(top):
-        hit = ids_ref[k : k + 1, :] == expert
-        gate = gate + jnp.where(hit, gates_ref[k : k + 1, :], 0.0)
+        hit = ids[k : k + 1, :] == expert
+        gate = gate + jnp.where(hit, value[k : k + 1, :], 0.0)
         mask = mask + jnp.where(hit, 1.0, 0.0)
-    hi = gate.astype(BF16)
-    rest = gate - hi.astype(F32)
-    mid = rest.astype(BF16)
-    low = (rest - mid.astype(F32)).astype(BF16)
-    earlier = (iota((rows, rows), 0) < iota((rows, rows), 1)).astype(BF16)
-    rank = (mask * (dot(mask.astype(BF16), earlier) + 1.0)).astype(BF16)
-    routing = jnp.zeros((rows, LANES), F32)
-    for q, part in enumerate((hi, mid, low, rank)):
-        place = (iota((rows, LANES), 0) + q * rows == iota((rows, LANES), 1)).astype(BF16)
-        routing = routing + dot(part, place)
+    before, after = iota((LANES, LANES), 0), iota((LANES, LANES), 1)
+    earlier = ((before // rows == after // rows) & (before < after)).astype(BF16)
+    rank = mask * (dot(mask.astype(BF16), earlier) + 1.0)
+    routing = jnp.where(group < 3, gate, jnp.where(group == 3, rank, 0.0))
     out_ref[:, width:] = routing.astype(BF16)
     copies[2].wait()
 

time: 39.3 us -> 39.3 us (level)
  transfers between devices with their start and end apart: 14 -> 14, of which waited for: 6 -> 6; matrix products, arithmetic and copies ran while one was open for 0% -> 0% of each run, Pallas kernels for 30% -> 31%
where the time goes in v7:
time: 39.3 us; the launch traced here: 39.2 us
  starting transfers between devices  20.9 us (53%)
  Pallas kernels  12.6 us (32%)
  waiting for transfers between devices  5.52 us (14%)
    ppermute x10, starting transfers between devices, swap(): return lax.ppermute(x, 'ep', [(i, i ^ distance) for i in range(n)])  15.5 us
    pallas_call x17, Pallas kernels, call(): pl.pallas_call(body, out_shape=outs, in_specs=specs + [pl.BlockSpec(memor...  12.6 us
    ppermute x10, waiting for transfers between devices, swap(): return lax.ppermute(x, 'ep', [(i, i ^ distance) for i in range(n)])  5.43 us
    ppermute x4, starting transfers between devices, raised(): return (count, routing, pre, lax.ppermute(pre, 'rep', [(0, 1), (1, 0)]))  5.36 us
  transfers between devices with their start and end apart: 14, of which 6 were waited for; matrix products, arithmetic and copies ran while one was open for 0% of the time, Pallas kernels for 31%

profile of v7, /device:TPU:0, one launch (start us, length us, event | category | flops | bytes accessed | tf_op | source)
XLA Modules:
  0.0 39.2 jit_solution(16474549309146571850)
XLA Ops:
  0.0 0.5 %collective-permute-start = (bf16[1792,1024]{1,0:T(8,128)(2,1)}, bf16[1792,1024]{1,0:T(8,128)(2,1)S(1)}, u32[]{:S(2)}, u32[]{:S(2)}) collective-permute-start(bf16[1792,1024]{1,0:T(8,128)(2,1)} %bitcast.8), channel_id=1, source_target_pairs={{0,2},{2,0},{4,6},{6,4},{8,10},{10,8},{12,14},{14,12},{16,18},{18,... | collective-permute-start | bytes 11010056 | tf_op jit(solution)/shard_map/ppermute | solution.py:197
  0.5 0.1 collective-permute-start.3
  0.5 1.0 %shard_map.56.refs_0_ = bf16[16,1920]{1,0:T(8,128)(2,1)S(1)} custom-call(bf16[16,1792]{1,0:T(8,128)(2,1)} %refs_0_.1, s32[8,16]{1,0:T(8,128)} %bitcast.10, f32[8,16]{1,0:T(8,128)} %bitcast.11), custom_call_target="tpu_custom_call" | custom-call | flops 1 | bytes 1 | tf_op jit(solution)/shard_map/pallas_call | solution.py:24
  1.5 4.1 %collective-permute-start.1 = (bf16[16,1920]{1,0:T(8,128)(2,1)S(1)}, bf16[16,1920]{1,0:T(8,128)(2,1)S(1)}, u32[]{:S(2)}, u32[]{:S(2)}) collective-permute-start(bf16[16,1920]{1,0:T(8,128)(2,1)S(1)} %shard_map.56.refs_0_), channel_id=1, source_target_pairs={{0,16},{2,18},{4,20},{6,22},{8,24},{10,26},{12,28},{14,30},{16,0},... | collective-permute-start | bytes 184328 | tf_op jit(solution)/shard_map/ppermute | solution.py:197
  5.6 2.1 %shard_map.55.refs_2_.refs_0_ = bf16[1792,1024]{1,0:T(8,128)(2,1)S(1)} custom-call(bf16[1792,1024]{1,0:T(8,128)(2,1)} %bitcast.9), custom_call_target="tpu_custom_call" | custom-call | flops 1 | bytes 1 | tf_op jit(solution)/shard_map/pallas_call | solution.py:24
  7.7 0.8 %collective-permute-done.1.refs_1_ = bf16[16,1920]{1,0:T(8,128)(2,1)S(1)} collective-permute-done((bf16[16,1920]{1,0:T(8,128)(2,1)S(1)}, bf16[16,1920]{1,0:T(8,128)(2,1)S(1)}, u32[]{:S(2)}, u32[]{:S(2)}) %collective-permute-start.1) | collective-permute-done | bytes 61472 | tf_op jit(solution)/shard_map/ppermute | solution.py:197
  8.5 2.4 %collective-permute-start.4 = (bf16[32,1920]{1,0:T(8,128)(2,1)S(1)}, bf16[32,1920]{1,0:T(8,128)(2,1)S(1)}, u32[]{:S(2)}, u32[]{:S(2)}) collective-permute-start(bf16[32,1920]{1,0:T(8,128)(2,1)S(1)} %shard_map.57.refs_2_), channel_id=1, source_target_pairs={{0,12},{2,14},{4,8},{6,10},{8,4},{10,6},{12,0},{14,2},{16,28},{18,... | collective-permute-start | bytes 368648 | tf_op jit(solution)/shard_map/ppermute | solution.py:197
  10.9 1.7 %collective-permute-start.8 = (bf16[32,1920]{1,0:T(8,128)(2,1)S(1)}, bf16[32,1920]{1,0:T(8,128)(2,1)S(1)}, u32[]{:S(2)}, u32[]{:S(2)}) collective-permute-start(bf16[32,1920]{1,0:T(8,128)(2,1)S(1)} %shard_map.57.refs_2_), channel_id=1, source_target_pairs={{0,8},{2,10},{4,12},{6,14},{8,0},{10,2},{12,4},{14,6},{16,24},{18,... | collective-permute-start | bytes 368648 | tf_op jit(solution)/shard_map/ppermute | solution.py:197
  12.5 0.0 collective-permute-start.7
  12.5 0.0 collective-permute-done.refs_1_.refs_0_
  12.5 1.3 %shard_map.58 = (bf16[48,1024]{1,0:T(8,128)(2,1)S(1)}, f32[8,128]{1,0:T(8,128)S(1)}) custom-call(bf16[1792,1024]{1,0:T(8,128)(2,1)S(1)} %shard_map.55.refs_2_.refs_0_, bf16[1792,1024]{1,0:T(8,128)(2,1)S(1)} %collective-permute-done.refs_1_.refs_0_, bf16[32,1920]{1,0:T(8,128)(2,1)S(1)} %shard_map.57.refs_2_), custom_call_target="tpu_custom_call" | custom-call | flops 1 | bytes 1 | tf_op jit(solution)/shard_map/pallas_call | solution.py:24
  13.8 2.1 %collective-permute-start.2 = (bf16[48,1024]{1,0:T(8,128)(2,1)S(1)}, bf16[48,1024]{1,0:T(8,128)(2,1)S(1)}, u32[]{:S(2)}, u32[]{:S(2)}) collective-permute-start(bf16[48,1024]{1,0:T(8,128)(2,1)S(1)} %get-tuple-element.28.refs_3_.refs_2_), channel_id=1, source_target_pairs={{0,1},{1,0},{2,3},{3,2},{4,5},{5,4},{6,7},{7,6},{8,9},{9,8},{10,11... | collective-permute-start | bytes 294920 | tf_op jit(solution)/shard_map/ppermute | solution.py:228
  15.9 0.0 collective-permute-done.4.refs_2_
  15.9 1.3 %shard_map.60 = (bf16[48,1024]{1,0:T(8,128)(2,1)S(1)}, f32[8,128]{1,0:T(8,128)S(1)}) custom-call(bf16[1792,1024]{1,0:T(8,128)(2,1)S(1)} %shard_map.55.refs_2_.refs_0_, bf16[1792,1024]{1,0:T(8,128)(2,1)S(1)} %collective-permute-done.refs_1_.refs_0_, bf16[32,1920]{1,0:T(8,128)(2,1)S(1)} %collective-permute-done.4.refs_2_, ...), custom_call_target="tpu_custom_call" | custom-call | flops 1 | bytes 1 | tf_op jit(solution)/shard_map/pallas_call | solution.py:24
  17.2 0.2 shard_map.61
  17.4 1.1 %collective-permute-start.5 = (bf16[48,1024]{1,0:T(8,128)(2,1)S(1)}, bf16[48,1024]{1,0:T(8,128)(2,1)S(1)}, u32[]{:S(2)}, u32[]{:S(2)}) collective-permute-start(bf16[48,1024]{1,0:T(8,128)(2,1)S(1)} %get-tuple-element.32.refs_2_.refs_5_), channel_id=1, source_target_pairs={{0,1},{1,0},{2,3},{3,2},{4,5},{5,4},{6,7},{7,6},{8,9},{9,8},{10,11... | collective-permute-start | bytes 294920 | tf_op jit(solution)/shard_map/ppermute | solution.py:228
  18.5 0.0 collective-permute-done.8.refs_2_
  18.5 0.0 collective-permute-done.7.refs_1_
  18.5 0.0 copy-start
  18.5 0.8 %shard_map.63 = (bf16[48,1024]{1,0:T(8,128)(2,1)S(1)}, f32[8,128]{1,0:T(8,128)S(1)}) custom-call(bf16[1792,1024]{1,0:T(8,128)(2,1)S(1)} %shard_map.55.refs_2_.refs_0_, bf16[32,1920]{1,0:T(8,128)(2,1)S(1)} %collective-permute-done.7.refs_1_, bf16[32,1920]{1,0:T(8,128)(2,1)S(1)} %collective-permute-done.8.refs_2_, ...), custom_call_target="tpu_custom_call" | custom-call | flops 1 | bytes 1 | tf_op jit(solution)/shard_map/pallas_call | solution.py:24
  19.3 1.0 %collective-permute-start.10 = (bf16[48,1024]{1,0:T(8,128)(2,1)S(1)}, bf16[48,1024]{1,0:T(8,128)(2,1)S(1)}, u32[]{:S(2)}, u32[]{:S(2)}) collective-permute-start(bf16[48,1024]{1,0:T(8,128)(2,1)S(1)} %get-tuple-element.40.refs_2_), channel_id=1, source_target_pairs={{0,1},{1,0},{2,3},{3,2},{4,5},{5,4},{6,7},{7,6},{8,9},{9,8},{10,11... | collective-permute-start | bytes 294920 | tf_op jit(solution)/shard_map/ppermute | solution.py:228
  20.3 0.8 %shard_map.64 = (bf16[48,1024]{1,0:T(8,128)(2,1)S(1)}, f32[8,128]{1,0:T(8,128)S(1)}) custom-call(bf16[1792,1024]{1,0:T(8,128)(2,1)S(1)} %collective-permute-done.refs_1_.refs_0_, bf16[32,1920]{1,0:T(8,128)(2,1)S(1)} %collective-permute-done.7.refs_1_, bf16[32,1920]{1,0:T(8,128)(2,1)S(1)} %collective-permute-done.8.refs_2_), custom_call_target="tpu_custom_call" | custom-call | flops 1 | bytes 1 | tf_op jit(solution)/shard_map/pallas_call | solution.py:24
  21.1 0.0 collective-permute-done.2.refs_1_.refs_3_
  21.1 1.1 %collective-permute-start.9 = (bf16[48,1024]{1,0:T(8,128)(2,1)S(1)}, bf16[48,1024]{1,0:T(8,128)(2,1)S(1)}, u32[]{:S(2)}, u32[]{:S(2)}) collective-permute-start(bf16[48,1024]{1,0:T(8,128)(2,1)S(1)} %shard_map.66.refs_2_), channel_id=1, source_target_pairs={{0,1},{1,0},{2,3},{3,2},{4,5},{5,4},{6,7},{7,6},{8,9},{9,8},{10,11... | collective-permute-start | bytes 294920 | tf_op jit(solution)/shard_map/ppermute | solution.py:228
  22.3 0.3 shard_map.65
  22.5 0.0 collective-permute-done.3.refs_5_.refs_4_
  22.5 0.1 collective-permute-done.5.refs_3_
  22.6 0.0 copy-done
  22.6 1.3 %shard_map.62.refs_5_ = bf16[32,1792]{1,0:T(8,128)(2,1)S(1)} custom-call(bf16[64,48]{1,0:T(8,128)(2,1)S(1)} %get-tuple-element.30.refs_0_.refs_3_, f32[64,128]{1,0:T(8,128)S(1)} %get-tuple-element.31.refs_1_.refs_4_, bf16[48,1024]{1,0:T(8,128)(2,1)S(1)} %get-tuple-element.32.refs_2_.refs_5_, bf16[48,1024]{1,0:T(8,128)(2,1)S(1)} %collective-permute-done.5.refs_3_, ...), custom_call_target="tpu_custom_call" | custom-call | flops 1 | bytes 1 | tf_op jit(solution)/shard_map/pallas_call | solution.py:24
  23.9 2.5 %collective-permute-start.6 = (bf16[32,1792]{1,0:T(8,128)(2,1)S(1)}, bf16[32,1792]{1,0:T(8,128)(2,1)S(1)}, u32[]{:S(2)}, u32[]{:S(2)}) collective-permute-start(bf16[32,1792]{1,0:T(8,128)(2,1)S(1)} %shard_map.62.refs_5_), channel_id=1, source_target_pairs={{0,12},{2,14},{4,8},{6,10},{8,4},{10,6},{12,0},{14,2},{16,28},{18,... | collective-permute-start | bytes 344072 | tf_op jit(solution)/shard_map/ppermute | solution.py:197
  26.4 0.0 collective-permute-done.10.refs_3_
  26.4 0.7 %shard_map.67.refs_5_ = f32[64,1792]{1,0:T(8,128)S(1)} custom-call(bf16[64,48]{1,0:T(8,128)(2,1)S(1)} %get-tuple-element.38.refs_0_, f32[64,128]{1,0:T(8,128)S(1)} %get-tuple-element.39.refs_1_, bf16[48,1024]{1,0:T(8,128)(2,1)S(1)} %get-tuple-element.40.refs_2_, bf16[48,1024]{1,0:T(8,128)(2,1)S(1)} %collective-permute-done.10.refs_3_, ...), custom_call_target="tpu_custom_call" | custom-call | flops 1 | bytes 1 | tf_op jit(solution)/shard_map/pallas_call | solution.py:24
  27.2 0.0 collective-permute-done.9.refs_3_
  27.2 0.8 %shard_map.68 = (bf16[32,1792]{1,0:T(8,128)(2,1)S(1)}, bf16[32,1792]{1,0:T(8,128)(2,1)S(1)}) custom-call(bf16[64,48]{1,0:T(8,128)(2,1)S(1)} %get-tuple-element.35.refs_0_, f32[64,128]{1,0:T(8,128)S(1)} %get-tuple-element.36.refs_1_, bf16[48,1024]{1,0:T(8,128)(2,1)S(1)} %shard_map.66.refs_2_, bf16[48,1024]{1,0:T(8,128)(2,1)S(1)} %collective-permute-done.9.refs_3_, ...), custom_call_target="tpu_custom_call" | custom-call | flops 1 | bytes 1 | tf_op jit(solution)/shard_map/pallas_call | solution.py:24
  27.9 0.5 %collective-permute-start.12 = (bf16[32,1792]{1,0:T(8,128)(2,1)S(1)}, bf16[32,1792]{1,0:T(8,128)(2,1)S(1)}, u32[]{:S(2)}, u32[]{:S(2)}) collective-permute-start(bf16[32,1792]{1,0:T(8,128)(2,1)S(1)} %get-tuple-element.42), channel_id=1, source_target_pairs={{0,8},{2,10},{4,12},{6,14},{8,0},{10,2},{12,4},{14,6},{16,24},{18,... | collective-permute-start | bytes 344072 | tf_op jit(solution)/shard_map/ppermute | solution.py:197
  28.5 0.8 %collective-permute-start.11 = (bf16[32,1792]{1,0:T(8,128)(2,1)S(1)}, bf16[32,1792]{1,0:T(8,128)(2,1)S(1)}, u32[]{:S(2)}, u32[]{:S(2)}) collective-permute-start(bf16[32,1792]{1,0:T(8,128)(2,1)S(1)} %get-tuple-element.41.refs_7_), channel_id=1, source_target_pairs={{0,4},{2,6},{4,0},{6,2},{8,12},{10,14},{12,8},{14,10},{16,20},{18,... | collective-permute-start | bytes 344072 | tf_op jit(solution)/shard_map/ppermute | solution.py:197
  29.3 0.2 shard_map.59
  29.5 0.3 collective-permute-done.6.refs_6_
  29.8 1.3 %shard_map.69.refs_0_ = f32[32,1792]{1,0:T(8,128)S(1)} custom-call(bf16[64,48]{1,0:T(8,128)(2,1)S(1)} %get-tuple-element.26.refs_0_, f32[64,128]{1,0:T(8,128)S(1)} %get-tuple-element.27.refs_1_, bf16[48,1024]{1,0:T(8,128)(2,1)S(1)} %get-tuple-element.28.refs_3_.refs_2_, bf16[48,1024]{1,0:T(8,128)(2,1)S(1)} %collective-permute-done.2.refs_1_.refs_3_, ...), custom_call_target="tpu_custom_call" | custom-call | flops 1 | bytes 1 | tf_op jit(solution)/shard_map/pallas_call | solution.py:24
  31.1 1.7 %collective-permute-done.12.refs_2_ = bf16[32,1792]{1,0:T(8,128)(2,1)S(1)} collective-permute-done((bf16[32,1792]{1,0:T(8,128)(2,1)S(1)}, bf16[32,1792]{1,0:T(8,128)(2,1)S(1)}, u32[]{:S(2)}, u32[]{:S(2)}) %collective-permute-start.12) | collective-permute-done | bytes 114720 | tf_op jit(solution)/shard_map/ppermute | solution.py:197
  32.8 0.5 %collective-permute-done.11.refs_1_ = bf16[32,1792]{1,0:T(8,128)(2,1)S(1)} collective-permute-done((bf16[32,1792]{1,0:T(8,128)(2,1)S(1)}, bf16[32,1792]{1,0:T(8,128)(2,1)S(1)}, u32[]{:S(2)}, u32[]{:S(2)}) %collective-permute-start.11) | collective-permute-done | bytes 114720 | tf_op jit(solution)/shard_map/ppermute | solution.py:197
  33.3 3.1 %collective-permute-start.13 = (bf16[16,1792]{1,0:T(8,128)(2,1)S(1)}, bf16[16,1792]{1,0:T(8,128)(2,1)S(1)}, u32[]{:S(2)}, u32[]{:S(2)}) collective-permute-start(bf16[16,1792]{1,0:T(8,128)(2,1)S(1)} %get-tuple-element.44), channel_id=1, source_target_pairs={{0,16},{2,18},{4,20},{6,22},{8,24},{10,26},{12,28},{14,30},{16,0},... | collective-permute-start | bytes 172040 | tf_op jit(solution)/shard_map/ppermute | solution.py:197
  36.4 2.2 %collective-permute-done.13.refs_1_ = bf16[16,1792]{1,0:T(8,128)(2,1)S(1)} collective-permute-done((bf16[16,1792]{1,0:T(8,128)(2,1)S(1)}, bf16[16,1792]{1,0:T(8,128)(2,1)S(1)}, u32[]{:S(2)}, u32[]{:S(2)}) %collective-permute-start.13) | collective-permute-done | bytes 57376 | tf_op jit(solution)/shard_map/ppermute | solution.py:197
  38.5 0.6 %shard_map.71 = bf16[16,1792]{1,0:T(8,128)(2,1)} custom-call(f32[16,1792]{1,0:T(8,128)S(1)} %get-tuple-element.43.refs_0_, bf16[16,1792]{1,0:T(8,128)(2,1)S(1)} %collective-permute-done.13.refs_1_), custom_call_target="tpu_custom_call" | custom-call | flops 1 | bytes 1 | tf_op jit(solution)/shard_map/pallas_call | solution.py:24
  (3 shorter events, 0.1 us)
Async XLA Ops:
  0.0 12.5 %collective-permute-start = (bf16[1792,1024]{1,0:T(8,128)(2,1)}, bf16[1792,1024]{1,0:T(8,128)(2,1)S(1)}, u32[]{:S(2)}, u32[]{:S(2)}) collective-permute-start(bf16[1792,1024]{1,0:T(8,128)(2,1)} %bitcast.8), channel_id=1, source_target_pairs={{0,2},{2,0},{4,6},{6,4},{8,10},{10,8},{12,14},{14,12},{16,18},{18,... | collective-permute-start | bytes 11010056 | tf_op jit(solution)/shard_map/ppermute | solution.py:197
  0.5 22.1 %collective-permute-start.3 = (bf16[1024,1792]{1,0:T(8,128)(2,1)}, bf16[1024,1792]{1,0:T(8,128)(2,1)S(1)}, u32[]{:S(2)}, u32[]{:S(2)}) collective-permute-start(bf16[1024,1792]{1,0:T(8,128)(2,1)} %bitcast.4), channel_id=1, source_target_pairs={{0,2},{2,0},{4,6},{6,4},{8,10},{10,8},{12,14},{14,12},{16,18},{18,... | collective-permute-start | bytes 11010056 | tf_op jit(solution)/shard_map/ppermute | solution.py:197
  1.5 7.0 %collective-permute-start.1 = (bf16[16,1920]{1,0:T(8,128)(2,1)S(1)}, bf16[16,1920]{1,0:T(8,128)(2,1)S(1)}, u32[]{:S(2)}, u32[]{:S(2)}) collective-permute-start(bf16[16,1920]{1,0:T(8,128)(2,1)S(1)} %shard_map.56.refs_0_), channel_id=1, source_target_pairs={{0,16},{2,18},{4,20},{6,22},{8,24},{10,26},{12,28},{14,30},{16,0},... | collective-permute-start | bytes 184328 | tf_op jit(solution)/shard_map/ppermute | solution.py:197
  8.5 7.4 %collective-permute-start.4 = (bf16[32,1920]{1,0:T(8,128)(2,1)S(1)}, bf16[32,1920]{1,0:T(8,128)(2,1)S(1)}, u32[]{:S(2)}, u32[]{:S(2)}) collective-permute-start(bf16[32,1920]{1,0:T(8,128)(2,1)S(1)} %shard_map.57.refs_2_), channel_id=1, source_target_pairs={{0,12},{2,14},{4,8},{6,10},{8,4},{10,6},{12,0},{14,2},{16,28},{18,... | collective-permute-start | bytes 368648 | tf_op jit(solution)/shard_map/ppermute | solution.py:197
  10.9 7.7 %collective-permute-start.8 = (bf16[32,1920]{1,0:T(8,128)(2,1)S(1)}, bf16[32,1920]{1,0:T(8,128)(2,1)S(1)}, u32[]{:S(2)}, u32[]{:S(2)}) collective-permute-start(bf16[32,1920]{1,0:T(8,128)(2,1)S(1)} %shard_map.57.refs_2_), channel_id=1, source_target_pairs={{0,8},{2,10},{4,12},{6,14},{8,0},{10,2},{12,4},{14,6},{16,24},{18,... | collective-permute-start | bytes 368648 | tf_op jit(solution)/shard_map/ppermute | solution.py:197
  12.5 6.0 %collective-permute-start.7 = (bf16[32,1920]{1,0:T(8,128)(2,1)S(1)}, bf16[32,1920]{1,0:T(8,128)(2,1)S(1)}, u32[]{:S(2)}, u32[]{:S(2)}) collective-permute-start(bf16[32,1920]{1,0:T(8,128)(2,1)S(1)} %shard_map.57.refs_2_), channel_id=1, source_target_pairs={{0,4},{2,6},{4,0},{6,2},{8,12},{10,14},{12,8},{14,10},{16,20},{18,... | collective-permute-start | bytes 368648 | tf_op jit(solution)/shard_map/ppermute | solution.py:197
  13.8 7.3 %collective-permute-start.2 = (bf16[48,1024]{1,0:T(8,128)(2,1)S(1)}, bf16[48,1024]{1,0:T(8,128)(2,1)S(1)}, u32[]{:S(2)}, u32[]{:S(2)}) collective-permute-start(bf16[48,1024]{1,0:T(8,128)(2,1)S(1)} %get-tuple-element.28.refs_3_.refs_2_), channel_id=1, source_target_pairs={{0,1},{1,0},{2,3},{3,2},{4,5},{5,4},{6,7},{7,6},{8,9},{9,8},{10,11... | collective-permute-start | bytes 294920 | tf_op jit(solution)/shard_map/ppermute | solution.py:228
  17.4 5.2 %collective-permute-start.5 = (bf16[48,1024]{1,0:T(8,128)(2,1)S(1)}, bf16[48,1024]{1,0:T(8,128)(2,1)S(1)}, u32[]{:S(2)}, u32[]{:S(2)}) collective-permute-start(bf16[48,1024]{1,0:T(8,128)(2,1)S(1)} %get-tuple-element.32.refs_2_.refs_5_), channel_id=1, source_target_pairs={{0,1},{1,0},{2,3},{3,2},{4,5},{5,4},{6,7},{7,6},{8,9},{9,8},{10,11... | collective-permute-start | bytes 294920 | tf_op jit(solution)/shard_map/ppermute | solution.py:228
  18.5 4.1 %copy-start = (bf16[1,1024,1792]{2,1,0:T(8,128)(2,1)S(1)}, bf16[1,1024,1792]{2,1,0:T(8,128)(2,1)}, u32[]{:S(2)}) copy-start(bf16[1,1024,1792]{2,1,0:T(8,128)(2,1)} %param.9) | copy-start | bytes 11010052
  19.3 7.1 %collective-permute-start.10 = (bf16[48,1024]{1,0:T(8,128)(2,1)S(1)}, bf16[48,1024]{1,0:T(8,128)(2,1)S(1)}, u32[]{:S(2)}, u32[]{:S(2)}) collective-permute-start(bf16[48,1024]{1,0:T(8,128)(2,1)S(1)} %get-tuple-element.40.refs_2_), channel_id=1, source_target_pairs={{0,1},{1,0},{2,3},{3,2},{4,5},{5,4},{6,7},{7,6},{8,9},{9,8},{10,11... | collective-permute-start | bytes 294920 | tf_op jit(solution)/shard_map/ppermute | solution.py:228
  21.1 6.1 %collective-permute-start.9 = (bf16[48,1024]{1,0:T(8,128)(2,1)S(1)}, bf16[48,1024]{1,0:T(8,128)(2,1)S(1)}, u32[]{:S(2)}, u32[]{:S(2)}) collective-permute-start(bf16[48,1024]{1,0:T(8,128)(2,1)S(1)} %shard_map.66.refs_2_), channel_id=1, source_target_pairs={{0,1},{1,0},{2,3},{3,2},{4,5},{5,4},{6,7},{7,6},{8,9},{9,8},{10,11... | collective-permute-start | bytes 294920 | tf_op jit(solution)/shard_map/ppermute | solution.py:228
  23.9 5.9 %collective-permute-start.6 = (bf16[32,1792]{1,0:T(8,128)(2,1)S(1)}, bf16[32,1792]{1,0:T(8,128)(2,1)S(1)}, u32[]{:S(2)}, u32[]{:S(2)}) collective-permute-start(bf16[32,1792]{1,0:T(8,128)(2,1)S(1)} %shard_map.62.refs_5_), channel_id=1, source_target_pairs={{0,12},{2,14},{4,8},{6,10},{8,4},{10,6},{12,0},{14,2},{16,28},{18,... | collective-permute-start | bytes 344072 | tf_op jit(solution)/shard_map/ppermute | solution.py:197
  27.9 4.9 %collective-permute-start.12 = (bf16[32,1792]{1,0:T(8,128)(2,1)S(1)}, bf16[32,1792]{1,0:T(8,128)(2,1)S(1)}, u32[]{:S(2)}, u32[]{:S(2)}) collective-permute-start(bf16[32,1792]{1,0:T(8,128)(2,1)S(1)} %get-tuple-element.42), channel_id=1, source_target_pairs={{0,8},{2,10},{4,12},{6,14},{8,0},{10,2},{12,4},{14,6},{16,24},{18,... | collective-permute-start | bytes 344072 | tf_op jit(solution)/shard_map/ppermute | solution.py:197
  28.5 4.8 %collective-permute-start.11 = (bf16[32,1792]{1,0:T(8,128)(2,1)S(1)}, bf16[32,1792]{1,0:T(8,128)(2,1)S(1)}, u32[]{:S(2)}, u32[]{:S(2)}) collective-permute-start(bf16[32,1792]{1,0:T(8,128)(2,1)S(1)} %get-tuple-element.41.refs_7_), channel_id=1, source_target_pairs={{0,4},{2,6},{4,0},{6,2},{8,12},{10,14},{12,8},{14,10},{16,20},{18,... | collective-permute-start | bytes 344072 | tf_op jit(solution)/shard_map/ppermute | solution.py:197
  33.3 5.2 %collective-permute-start.13 = (bf16[16,1792]{1,0:T(8,128)(2,1)S(1)}, bf16[16,1792]{1,0:T(8,128)(2,1)S(1)}, u32[]{:S(2)}, u32[]{:S(2)}) collective-permute-start(bf16[16,1792]{1,0:T(8,128)(2,1)S(1)} %get-tuple-element.44), channel_id=1, source_target_pairs={{0,16},{2,18},{4,20},{6,22},{8,24},{10,26},{12,28},{14,30},{16,0},... | collective-permute-start | bytes 172040 | tf_op jit(solution)/shard_map/ppermute | solution.py:197
